TPU v7x, 256 devices: a whole 4x4x8 slice. The times are simulated.
256 devices in a mesh: dp: 16 (over y, x), emb: 8 (over z), section: 2 (over core).
Axes of the slice: x: 4, y: 4, z: 8, core: 2. Of those that a mesh axis runs over, the one named last changes fastest.
Arguments:
- events: bfloat16 [8192, 64, 4, 256], P(('emb', 'section'), 'dp'), may hold values from -6 to 6
- counts: int32 [8192, 64], P(('emb', 'section'), 'dp'), may hold values from 1 to 4
- live: int32 [8192, 64], P(('emb', 'section'), 'dp'), may hold values 0 or 1
- enc_weight: bfloat16 [256, 256], replicated, may hold values from -0.375 to 0.375
- fm_proj: bfloat16 [64, 32], replicated, may hold values from -0.75 to 0.75
- ln_gain: float32 [2048], replicated, may hold values from 0.1 to 1.9
- w_hidden: bfloat16 [2048, 4096], P(None, ('emb', 'section')), may hold values from -0.125 to 0.125
- w_out: bfloat16 [4096, 32, 256], P(None, None, ('emb', 'section')), may hold values from -0.09375 to 0.09375
- lcb_weight: bfloat16 [32, 64], replicated, may hold values from -0.75 to 0.75
- out_gain: float32 [256], P(('emb', 'section')), may hold values from 0.1 to 1.9
Outputs:
- layer_out: bfloat16 [8192, 64, 256], P('dp', None, ('emb', 'section'))
All inputs are finite; a program needn't handle non-finite values. No bound on the sum of `live` on one device may be relied on, other than what follows from the above.
Results may differ from a plain program's by a relative error of at most 0.013.
Values may be sent and summed in bfloat16 or wider, within the bound.
No kernel may reach another device: no remote copies, remote signals or barrier semaphores. Data moves between devices by JAX's collectives and lax.ppermute only.
A program may use at most 128 MiB of HBM per device.

v0:
```python
import jax
import jax.numpy as jnp
from jax import lax
from jax.sharding import PartitionSpec as P

D = 256
NF = 32


def layer_norm_rows(values, gain):
    center = jnp.mean(values, axis=-1, keepdims=True)
    meansq = jnp.mean(values * values, axis=-1, keepdims=True)
    return (values - center) * lax.rsqrt(meansq - center * center + 1e-05) * gain


def shards(
    events, counts, live, enc_weight, fm_proj, ln_gain, w_hidden, w_out, lcb_weight, out_gain
):
    users_enc, sess_dev, slot_count, full_width = events.shape
    inside = (lax.broadcasted_iota(jnp.int32, (1, 1, slot_count), 2) < counts[:, :, None]).astype(
        jnp.bfloat16
    )
    session_sums = jnp.einsum("usj,usjd->usd", inside, events, preferred_element_type=jnp.float32)
    pooled = (session_sums / counts[:, :, None].astype(jnp.float32)).astype(jnp.bfloat16)
    encoded = jnp.dot(
        pooled.reshape(-1, full_width), enc_weight, preferred_element_type=jnp.float32
    )
    encoded = encoded.reshape(users_enc, sess_dev, full_width)
    session = (encoded * live[:, :, None].astype(jnp.float32)).astype(jnp.bfloat16)
    interact = lax.all_to_all(
        lax.all_to_all(session, ("emb", "section"), split_axis=2, concat_axis=0, tiled=True),
        "dp",
        split_axis=0,
        concat_axis=1,
        tiled=True,
    )
    user_rows, sessions, narrow = interact.shape
    reduced = jnp.einsum(
        "und,nk->udk", interact, fm_proj, preferred_element_type=jnp.float32
    ).astype(jnp.bfloat16)
    partial_fm = jnp.einsum("und,udk->unk", interact, reduced, preferred_element_type=jnp.float32)
    partial_fm = partial_fm.reshape(user_rows, -1)
    whole_sum = lax.psum(partial_fm, ("emb", "section"))
    normed = layer_norm_rows(whole_sum, ln_gain).astype(jnp.bfloat16)
    hidden = jnp.maximum(jnp.dot(normed, w_hidden, preferred_element_type=jnp.float32), 0.0).astype(
        jnp.bfloat16
    )
    out_flat = w_out.reshape(w_out.shape[0], -1)
    fm_out = jnp.dot(
        lax.all_gather(hidden, ("emb", "section"), axis=1, tiled=True),
        out_flat,
        preferred_element_type=jnp.float32,
    )
    compressed = jnp.einsum("mn,und->umd", lcb_weight, interact, preferred_element_type=jnp.float32)
    summed = jnp.concatenate(
        [fm_out.reshape(user_rows, NF, narrow), compressed], axis=1
    ) + interact.astype(jnp.float32)
    totals = (
        lax.psum(jnp.sum(summed, axis=2).astype(jnp.bfloat16), ("emb", "section")).astype(
            jnp.float32
        ),
        lax.psum(jnp.sum(summed * summed, axis=2).astype(jnp.bfloat16), ("emb", "section")).astype(
            jnp.float32
        ),
    )
    center = totals[0][:, :, None] / D
    meansq = totals[1][:, :, None] / D
    scaled = (summed - center) * lax.rsqrt(meansq - center * center + 1e-05) * out_gain
    return scaled.astype(jnp.bfloat16)


def solution(mesh):
    in_specs = (
        P(("emb", "section"), "dp", None, None),
        P(("emb", "section"), "dp"),
        P(("emb", "section"), "dp"),
        P(),
        P(),
        P(),
        P(None, ("emb", "section")),
        P(None, None, ("emb", "section")),
        P(),
        P(("emb", "section")),
    )
    out_specs = P("dp", None, ("emb", "section"))
    return jax.shard_map(shards, mesh=mesh, in_specs=in_specs, out_specs=out_specs, check_vma=False)
```

profile of v0, /device:TPU:1, one launch (start us, length us, event | category | flops | bytes accessed | tf_op | source)
XLA Modules:
  0.0 438.0 jit_solution(18015834065280793075)
XLA Ops:
  6.5 0.8 convert_element_type.52
  7.3 0.8 copy.28
  8.2 0.7 convert_element_type.54
  8.9 1.3 fusion.14
  10.2 0.0 copy-start.7
  10.2 4.7 %fusion.3 = f32[512,4,1,256]{3,2,1,0:T(1,128)S(1)} fusion(bf16[512,4,4,256]{3,2,1,0:T(4,128)(2,1)} %param.10, pred[512,4,4,1]{2,1,0,3:T(4,128)(4,1)S(1)} %fusion.14), kind=kOutput, calls=%fused_computation.5 | convolution fusion | flops 4194304 | bytes 6299648 | tf_op jit(solution)/shard_map/usj,usjd->usd/dot_general | solution.py:23
  15.0 0.8 multiply_convert_fusion.3
  15.8 1.0 copy.29
  16.8 38.3 %all_to_all.36 = bf16[512,4,256]{0,1,2:T(4,128)(2,1)S(1)} all-to-all(bf16[512,4,256]{0,1,2:T(4,128)(2,1)S(1)} %copy.29), channel_id=1, replica_groups=mesh['dp'=16,'emb'=8,'section'=2] {'emb','section'}, dimensions={2} | all-to-all | bytes 2097152 | tf_op jit(solution)/shard_map/all_to_all | solution.py:31
  55.2 0.2 copy.30
  55.4 9.0 %copy.49 = bf16[16,512,4,16]{3,2,1,0:T(4,128)(2,1)} copy(bf16[16,512,4,16]{1,3,0,2:T(8,128)(2,1)S(1)} %bitcast.56) | data formatting | bytes 2097152 | tf_op jit(solution)/shard_map/all_to_all | solution.py:31
  64.3 10.4 %reshape.59 = bf16[16,2,16384]{2,1,0:T(2,128)(2,1)S(1)} reshape(bf16[8192,4,16]{2,1,0:T(4,128)(2,1)} %bitcast.49) | data formatting | bytes 2097152
  74.7 23.6 %all_to_all.37 = bf16[16,2,16384]{2,1,0:T(2,128)(2,1)S(1)} all-to-all(bf16[16,2,16384]{2,1,0:T(2,128)(2,1)S(1)} %reshape.59), channel_id=1, replica_groups=mesh['dp'=16,'emb'=8,'section'=2] {'dp'}, dimensions={0} | all-to-all | bytes 2097152 | tf_op jit(solution)/shard_map/all_to_all | solution.py:30
  98.3 7.5 %reshape.60 = bf16[8192,4,16]{2,1,0:T(4,128)(2,1)} reshape(bf16[16,2,16384]{2,1,0:T(2,128)(2,1)S(1)} %all_to_all.37) | data formatting | bytes 2097152
  105.8 10.8 %copy.51 = bf16[16,512,4,16]{1,3,2,0:T(8,128)(2,1)S(1)} copy(bf16[16,512,4,16]{3,2,1,0:T(4,128)(2,1)} %bitcast.47) | data formatting | bytes 2097152 | tf_op jit(solution)/shard_map/all_to_all | solution.py:30
  116.6 0.0 copy-start.4
  116.6 3.6 copy.36
  120.2 1.3 convolution_convert_fusion
  121.5 2.8 copy.37
  124.4 6.9 %fusion.21 = f32[512,64,32]{1,2,0:T(8,128)} fusion(bf16[512,64,16]{1,2,0:T(8,128)(2,1)} %copy.36, bf16[512,16,32]{2,1,0:T(8,128)(2,1)} %copy.37), kind=kOutput, calls=%fused_computation.35 | convolution fusion | flops 33554432 | bytes 5767168 | tf_op jit(solution)/shard_map/und,udk->unk/dot_general | solution.py:41
  131.3 7.7 %copy.38 = f32[512,64,32]{0,2,1:T(8,128)} copy(f32[512,64,32]{1,2,0:T(8,128)} %fusion.21) | data formatting | bytes 8388608 | tf_op jit(solution)/shard_map/und,udk->unk/dot_general | solution.py:41
  138.9 0.0 all-reduce.4.cloned.1.call-update
  139.0 0.0 all-gather.2.cloned.1.call-start
  139.0 114.6 %all-reduce.4.cloned.1.call-done = f32[512,2048]{0,1:T(8,128)} async-done(((f32[512,2048]{0,1:T(8,128)}), f32[512,2048]{0,1:T(8,128)}) %all-reduce.4.cloned.1.call-update) | async-done | bytes 4194320 | tf_op jit(solution)/shard_map/psum | solution.py:43
  253.6 2.8 fusion.20
  256.5 0.6 copy-done.2
  257.1 2.0 fusion.12
  259.0 0.0 all-gather.2.cloned.1.call-update
  259.1 0.3 all-reduce.6.cloned.1.call-start
  259.3 9.2 %copy.50 = bf16[16,512,4,16]{1,0,3,2:T(8,128)(2,1)} copy(bf16[16,512,4,16]{3,2,1,0:T(4,128)(2,1)} %bitcast.48) | data formatting | bytes 2097152 | tf_op jit(solution)/shard_map/all_to_all | solution.py:30
  268.5 1.3 convolution_bitcast_fusion
  269.9 39.5 %all-gather.2.cloned.1.call-done = bf16[512,4096]{1,0:T(8,128)(2,1)} async-done(((bf16[512,256]{1,0:T(8,128)(2,1)}), bf16[512,4096]{1,0:T(8,128)(2,1)}) %all-gather.2.cloned.1.call-update) | async-done | bytes 4194320 | tf_op jit(solution)/shard_map/all_gather | solution.py:50
  309.3 6.3 %fusion = f32[512,32,16]{0,1,2:T(8,128)S(1)} fusion(bf16[512,4096]{1,0:T(8,128)(2,1)} %all-gather.2.cloned.1.call-done, bf16[32,16,4096]{2,1,0:T(8,128)(2,1)} %bitcast.57), kind=kOutput, calls=%fused_computation | convolution fusion | flops 2147483648 | bytes 9437184 | tf_op jit(solution)/shard_map/dot_general | solution.py:49
  315.7 0.2 pad_maximum_fusion
  315.9 0.8 copy-done.3
  316.6 1.2 copy.42
  317.9 0.0 copy-done.1
  317.9 0.0 copy-start.6
  317.9 1.4 fusion.10
  319.3 0.1 copy.44
  319.4 0.6 convert_element_type.62
  320.0 0.1 copy.45
  320.0 0.7 convert_element_type.65
  320.7 0.0 all-reduce.6.cloned.1.call-update
  320.7 106.2 %all-reduce.6.cloned.1.call-done = (bf16[512,64]{0,1:T(8,128)(2,1)}, bf16[512,64]{0,1:T(8,128)(2,1)}) async-done(((bf16[512,64]{0,1:T(8,128)(2,1)}, bf16[512,64]{0,1:T(8,128)(2,1)}), (bf16[512,64]{0,1:T(8,128)(2,1)}, bf16[512,64]{0,1:T(8,128)(2,1)})) %all-reduce.6.cloned.1.call-update) | async-done | bytes 131088 | tf_op jit(solution)/shard_map/psum | solution.py:62
  427.0 0.9 convert_multiply_fusion
  427.9 2.0 multiply_convert_fusion.2
  429.9 1.5 copy.46
  (14 shorter events, 0.0 us)
Async XLA Ops:
  6.5 249.9 %copy-start = (bf16[2048,256]{1,0:T(8,128)(2,1)S(1)}, bf16[2048,256]{1,0:T(8,128)(2,1)}, u32[]{:S(2)}) copy-start(bf16[2048,256]{1,0:T(8,128)(2,1)} %param.16) | copy-start | bytes 3145732
  6.5 247.1 %all-reduce.4.cloned.1.call-start = ((), (), s32[]{:S(2)}) async-start(), calls=%async_computation.2 | async-start | bytes 8388608 | tf_op jit(solution)/shard_map/psum | solution.py:43
  10.2 4.7 %copy-start.7 = (bf16[256,256]{1,0:T(8,128)(2,1)S(1)}, bf16[256,256]{1,0:T(8,128)(2,1)}, u32[]{:S(2)}) copy-start(bf16[256,256]{1,0:T(8,128)(2,1)} %param.13) | copy-start | bytes 393220
  116.6 3.6 copy-start.4
  139.0 117.5 %copy-start.8 = (f32[2048]{0:T(1024)S(1)}, f32[2048]{0:T(1024)}, u32[]{:S(2)}) copy-start(f32[2048]{0:T(1024)} %param.15) | copy-start | bytes 24580
  139.0 170.4 %all-gather.2.cloned.1.call-start = ((), (), s32[]{:S(2)}) async-start(), calls=%async_computation.3 | async-start | bytes 4456448 | tf_op jit(solution)/shard_map/all_gather | solution.py:50
  253.6 3.4 copy-start.2
  259.0 9.5 %copy-start.5 = (bf16[32,64]{1,0:T(8,128)(2,1)S(1)}, bf16[32,64]{1,0:T(8,128)(2,1)}, u32[]{:S(2)}) copy-start(bf16[32,64]{1,0:T(8,128)(2,1)} %param.18) | copy-start | bytes 12292
  259.1 167.9 %all-reduce.6.cloned.1.call-start = ((), (), s32[]{:S(2)}) async-start(), calls=%async_computation.4 | async-start | bytes 262144 | tf_op jit(solution)/shard_map/psum | solution.py:62
  315.7 1.0 copy-start.3
  316.6 1.2 copy-start.1
  317.9 110.0 %copy-start.6 = (f32[16]{0:T(128)S(1)}, f32[16]{0:T(128)}, u32[]{:S(2)}) copy-start(f32[16]{0:T(128)} %param.19) | copy-start | bytes 196
Sparse Core Ops, SparseCore 0:
  139.1 114.4 all-reduce.3
  259.2 50.1 all-gather.1
  320.8 106.0 all-reduce.5
where the time goes:
time: 439 us; the launch traced here: 438 us
  waiting for transfers between devices  260 us (59%)
  local copies, waits for them, and re-layouts  68.5 us (16%)
  blocking collectives  61.9 us (14%)
  matrix products  23.4 us (5%)
  between operations  13.3 us (3%)
  other arithmetic  10.2 us (2%)
    psum x1, waiting for transfers between devices, shards(): whole_sum = lax.psum(partial_fm, ('emb', 'section'))  115 us
    psum x1, waiting for transfers between devices, shards(): lax.psum(jnp.sum(summed * summed, axis=2).astype(jnp.bfloat16), ('emb', '...  106 us
    all_gather x1, waiting for transfers between devices, shards(): lax.all_gather(hidden, ('emb', 'section'), axis=1, tiled=True)  39.5 us
    all_to_all x1, blocking collectives, shards(): lax.all_to_all(session, ('emb', 'section'), split_axis=2, concat_axis=0,...  38.3 us
    all_to_all x1, blocking collectives, shards(): lax.all_to_all(lax.all_to_all(session, ('emb', 'section'), split_axis=2,...  23.6 us
    all_to_all x3, local copies, waits for them, and re-layouts, shards(): lax.all_to_all(lax.all_to_all(session, ('emb', 'section'), split_axis=2,...  23.5 us
    unnamed x21, local copies, waits for them, and re-layouts  20.2 us
    all_to_all x2, local copies, waits for them, and re-layouts, shards(): lax.all_to_all(session, ('emb', 'section'), split_axis=2, concat_axis=0,...  9.16 us
  transfers between devices with their start and end apart: 3, of which 3 were waited for; matrix products, arithmetic and copies ran while one was open for 2% of the time, Pallas kernels for 0%

commit v1 on v0

v1 whole, which is shorter than its diff:
```python
import functools

import jax
import jax.numpy as jnp
from jax import lax
from jax.experimental import pallas as pl
from jax.experimental.pallas import tpu as pltpu
from jax.sharding import PartitionSpec as P

D = 256
N = 64
K = 32
U = 32
Z = 8
F32 = jnp.float32
BF = jnp.bfloat16
VMEM = pl.BlockSpec(memory_space=pltpu.VMEM)
SMEM = pl.BlockSpec(memory_space=pltpu.SMEM)
PARAMS = pltpu.CompilerParams(vmem_limit_bytes=48 * 1024 * 1024)
UP = [(i, (i + 1) % Z) for i in range(Z)]
DOWN = [(i, (i - 1) % Z) for i in range(Z)]
SWAP = [(0, 1), (1, 0)]
LANES = ((1,), (1,)), ((), ())


def dot_t(a, b):
    return lax.dot_general(a, b, LANES, preferred_element_type=F32)


def fm_kernel(x_ref, mix_ref, gain_ref, normed_ref, comp_a, comp_b, xa, xb, ts):
    xa[...] = x_ref[:, :128].astype(F32)
    xb[...] = x_ref[:, 128:].astype(F32)
    for u in range(U):
        sides = [
            jnp.concatenate(
                [xs[pl.ds(first * U + u, 16, stride=4 * U), :] for first in range(4)], axis=0
            )
            for xs in (xa, xb)
        ]
        xu = jnp.concatenate(sides, axis=1).astype(BF)
        both = jnp.dot(mix_ref[...], xu, preferred_element_type=F32)
        comp_a[pl.ds(u, 32, stride=U), :] = both[K:, :128]
        comp_b[pl.ds(u, 32, stride=U), :] = both[K:, 128:]
        fm = dot_t(xu, both[:K].astype(BF))
        ts[pl.ds(u, 16, stride=U), :] = jnp.concatenate(
            [fm[16 * i : 16 * i + 16] for i in range(4)], axis=1
        )
    t = ts[...].reshape(16, U, 128)
    m = jnp.sum(jnp.sum(t, axis=0), axis=-1, keepdims=True) / (N * K)
    q = jnp.sum(jnp.sum(t * t, axis=0), axis=-1, keepdims=True) / (N * K)
    scale = lax.rsqrt(q - m * m + 1e-05)
    for g in range(16):
        normed_ref[:, g * 128 : g * 128 + 128] = (
            (t[g] - m) * scale * gain_ref[g : g + 1, :]
        ).astype(BF)


def slice_kernel(x_ref, comp_a, comp_b, perm_ref, out_ref, cut):
    y = jnp.concatenate([comp_a[...], comp_b[...]], axis=1) + x_ref[32 * U :, :].astype(F32)
    m = jnp.mean(y, axis=-1, keepdims=True)
    q = jnp.mean(y * y, axis=-1, keepdims=True)
    y = ((y - m) * lax.rsqrt(q - m * m + 1e-05)).astype(BF)
    for big in range(8):
        for t in range(2):
            for i in range(8):
                row = (8 * big + i) * U
                if big < 4:
                    piece = x_ref[row : row + U, t * 128 : t * 128 + 128]
                else:
                    row -= 32 * U
                    piece = y[row : row + U, t * 128 : t * 128 + 128]
                at = (2 * big + t) * U
                cut[at : at + U, i * 128 : i * 128 + 128] = piece
    o = jnp.dot(cut[...], perm_ref[...], preferred_element_type=F32).astype(BF)
    for big in range(8):
        for t in range(2):
            at = (2 * big + t) * U
            for e in range(8):
                out_ref[t * 8 + e, :, big * 128 : big * 128 + 128] = o[
                    at : at + U, e * 128 : e * 128 + 128
                ]


def hidden_kernel(at_ref, *refs):
    chunks, (own, other, out_ref, held) = refs[:9], refs[9:]
    z, c = at_ref[0], at_ref[1]
    for k, ref in zip((0, 7, 6, 5, 1, 2, 3), chunks[:7]):
        held[pl.ds(pl.multiple_of(lax.rem(z + k, Z) * U, U), U), :] = ref[...]
    half = pl.multiple_of(lax.rem(z + 4, Z) * U, U)
    held[pl.ds(half, U // 2), :] = chunks[7][...]
    held[pl.ds(half + U // 2, U // 2), :] = chunks[8][...]
    for where, w in ((c, own), (1 - c, other)):
        h = jnp.dot(held[...], w[...], preferred_element_type=F32)
        out_ref[:, pl.ds(pl.multiple_of(where * 256, 256), 256)] = jnp.maximum(h, 0.0).astype(BF)


def out_kernel(at_ref, *refs):
    chunks = refs[:9]
    own, other, s_own, s_other, o_own, o_other, t1_ref, t2_ref = refs[9:]
    z = at_ref[0]
    users, wide = o_own.shape
    mask = (
        lax.broadcasted_iota(jnp.int32, (8, wide), 1) // 16
        == lax.broadcasted_iota(jnp.int32, (8, wide), 0)
    ).astype(BF)
    t1 = jnp.zeros((8, users), F32)
    t2 = jnp.zeros((8, users), F32)
    for w, s, o in ((own, s_own, o_own), (other, s_other, o_other)):
        acc = s[:, 0].reshape(users, wide).astype(F32)
        for k, ref in zip((0, 7, 6, 5, 1, 2, 3), chunks[:7]):
            at = pl.multiple_of(lax.rem(z + k, Z) * 512, 512)
            acc += dot_t(ref[...], w[:, pl.ds(at, 512)])
        at = pl.multiple_of(lax.rem(z + 4, Z) * 512, 512)
        acc += jnp.concatenate(
            [dot_t(chunks[7][...], w[:, pl.ds(at, 512)]), dot_t(chunks[8][...], w[:, pl.ds(at, 512)])],
            axis=0,
        )
        o[...] = acc
        for v, which in ((acc, 0), (acc * acc, 1)):
            high = v.astype(BF)
            low = (v - high.astype(F32)).astype(BF)
            part = dot_t(mask, high) + dot_t(mask, low)
            if which:
                t2 += part
            else:
                t1 += part
    t1_ref[...] = t1
    t2_ref[...] = t2


def scale_kernel(c_ref, s_own, s_other, tot_ref, slices_ref, o_own, o_other):
    c = c_ref[1]
    users = s_own.shape[0]
    m = tot_ref[:32, :] / D
    q = tot_ref[32:, :] / D
    r = lax.rsqrt(q - m * m + 1e-05)
    spread = (
        lax.broadcasted_iota(jnp.int32, (32, 512), 1) // 16
        == lax.broadcasted_iota(jnp.int32, (32, 512), 0)
    ).astype(BF)

    def widen(v):
        high = v.astype(BF)
        low = (v - high.astype(F32)).astype(BF)
        dims = ((0,), (0,)), ((), ())
        return lax.dot_general(high, spread, dims, preferred_element_type=F32) + lax.dot_general(
            low, spread, dims, preferred_element_type=F32
        )

    m, r = widen(m), widen(r)
    for which, s, o in ((c, s_own, o_own), (1 - c, s_other, o_other)):
        o[:, :512] = ((s[...] - m) * r).astype(BF)
        o[:, 512:] = slices_ref[:, pl.ds(which, 1), :, 512:].reshape(users, 512)


def finish_kernel(v_ref, gain_ref, o_ref):
    v = v_ref[...].astype(F32).T * gain_ref[...]
    o_ref[...] = v.astype(BF)


def ring(v):
    half = v.shape[0] // 2
    ups, downs = [v], [v]
    for _ in range(3):
        ups.append(lax.ppermute(ups[-1], "emb", UP))
        downs.append(lax.ppermute(downs[-1], "emb", DOWN))
    last = [
        lax.ppermute(ups[-1][:half], "emb", UP),
        lax.ppermute(downs[-1][half:], "emb", DOWN),
    ]
    return [*ups, *downs[1:], *last]


def shards(
    events, counts, live, enc_weight, fm_proj, ln_gain, w_hidden, w_out, lcb_weight, out_gain
):
    users_enc, sess_dev, slot_count, full_width = events.shape
    z, c = lax.axis_index("emb"), lax.axis_index("section")
    place = jnp.stack([z, c]).astype(jnp.int32)
    w_hidden_other = lax.ppermute(w_hidden, "section", SWAP)
    w_own = jnp.transpose(w_out, (1, 2, 0)).reshape(512, -1)
    w_other = lax.ppermute(w_own, "section", SWAP)

    inside = (lax.broadcasted_iota(jnp.int32, (1, 1, slot_count), 2) < counts[:, :, None]).astype(BF)
    session_sums = jnp.einsum("usj,usjd->usd", inside, events, preferred_element_type=F32)
    pooled = (session_sums / counts[:, :, None].astype(F32)).astype(BF)
    encoded = jnp.dot(pooled.reshape(-1, full_width), enc_weight, preferred_element_type=F32)
    encoded = encoded.reshape(users_enc, sess_dev, full_width)
    session = (encoded * live[:, :, None].astype(F32)).astype(BF)
    chunks = jnp.transpose(session.reshape(16, U, sess_dev, D), (0, 2, 1, 3))
    x = lax.all_to_all(chunks, "dp", 0, 0, tiled=True).reshape(N * U, D)

    mix = jnp.concatenate([fm_proj.T, lcb_weight], axis=0)
    mix = jnp.transpose(mix.reshape(64, 16, 4), (0, 2, 1)).reshape(64, 64)
    normed, comp_a, comp_b = pl.pallas_call(
        fm_kernel,
        out_shape=[jax.ShapeDtypeStruct((U, N * K), BF)]
        + [jax.ShapeDtypeStruct((32 * U, 128), F32)] * 2,
        in_specs=[VMEM] * 3,
        out_specs=[VMEM] * 3,
        scratch_shapes=[pltpu.VMEM((N * U, 128), F32)] * 2 + [pltpu.VMEM((16 * U, 128), F32)],
        compiler_params=PARAMS,
        name="fm_rows",
    )(x, mix, ln_gain.reshape(16, 128))

    place_in = lax.broadcasted_iota(jnp.int32, (1024, 1), 0)
    i, e, f = place_in // 128, (place_in // 16) % 8, place_in % 16
    perm = (e * 128 + i * 16 + f == lax.broadcasted_iota(jnp.int32, (1, 1024), 1)).astype(BF)
    slices = pl.pallas_call(
        slice_kernel,
        out_shape=jax.ShapeDtypeStruct((16, U, 1024), BF),
        in_specs=[VMEM] * 4,
        out_specs=VMEM,
        scratch_shapes=[pltpu.VMEM((512, 1024), BF)],
        compiler_params=PARAMS,
        name="slices",
    )(x, comp_a, comp_b, perm)
    slices = lax.all_to_all(slices.reshape(Z, 2 * U, 1024), "emb", 0, 0, tiled=True)
    slices = slices.reshape(Z, 2, U, 1024)

    gathered = ring(normed)
    hidden = pl.pallas_call(
        hidden_kernel,
        out_shape=jax.ShapeDtypeStruct((Z * U, 512), BF),
        in_specs=[SMEM] + [VMEM] * 11,
        out_specs=VMEM,
        scratch_shapes=[pltpu.VMEM((Z * U, N * K), BF)],
        compiler_params=PARAMS,
        name="hidden",
    )(place, *gathered, w_hidden, w_hidden_other)

    gathered = ring(hidden)
    users = Z * U
    whole = [pl.BlockSpec(v.shape, lambda i, s: (0, 0)) for v in gathered]
    s_own, s_other, t1, t2 = pl.pallas_call(
        out_kernel,
        grid_spec=pltpu.PrefetchScalarGridSpec(
            num_scalar_prefetch=1,
            grid=(4,),
            in_specs=whole
            + [pl.BlockSpec((128, 4096), lambda i, s: (i, 0))] * 2
            + [
                pl.BlockSpec((Z, 1, U, 128), lambda i, s: (0, s[1], 0, i)),
                pl.BlockSpec((Z, 1, U, 128), lambda i, s: (0, 1 - s[1], 0, i)),
            ],
            out_specs=[pl.BlockSpec((users, 128), lambda i, s: (0, i))] * 2
            + [pl.BlockSpec((8, users), lambda i, s: (i, 0))] * 2,
        ),
        out_shape=[jax.ShapeDtypeStruct((users, 512), F32)] * 2
        + [jax.ShapeDtypeStruct((32, users), F32)] * 2,
        compiler_params=PARAMS,
        name="fm_out",
    )(place, *gathered, w_own, w_other, slices, slices)

    totals = jnp.concatenate([t1, t2], axis=0)
    for bit in (1, 2, 4):
        totals = totals + lax.ppermute(totals, "emb", [(i, i ^ bit) for i in range(Z)])

    o_own, o_other = pl.pallas_call(
        scale_kernel,
        out_shape=[jax.ShapeDtypeStruct((users, 1024), BF)] * 2,
        in_specs=[SMEM] + [VMEM] * 4,
        out_specs=[VMEM] * 2,
        compiler_params=PARAMS,
        name="scale",
    )(place, s_own, s_other, totals, slices)
    came = lax.ppermute(o_other, "section", SWAP)
    o_own, came = o_own.reshape(Z, 1, U, 1024), came.reshape(Z, 1, U, 1024)
    send = jnp.where(
        c == 0, jnp.concatenate([o_own, came], axis=1), jnp.concatenate([came, o_own], axis=1)
    )
    out = lax.all_to_all(send.reshape(16, U, 1024), "dp", 0, 0, tiled=True)
    gain = jnp.tile(out_gain, 64).reshape(1024, 1)
    out = pl.pallas_call(
        finish_kernel,
        out_shape=jax.ShapeDtypeStruct((1024, 512), BF),
        in_specs=[VMEM] * 2,
        out_specs=VMEM,
        compiler_params=PARAMS,
        name="finish",
    )(out.reshape(512, 1024), gain)
    return jnp.transpose(out.reshape(64, 16, 512), (2, 0, 1))


def solution(mesh):
    in_specs = (
        P(("emb", "section"), "dp", None, None),
        P(("emb", "section"), "dp"),
        P(("emb", "section"), "dp"),
        P(),
        P(),
        P(),
        P(None, ("emb", "section")),
        P(None, None, ("emb", "section")),
        P(),
        P(("emb", "section")),
    )
    out_specs = P("dp", None, ("emb", "section"))
    return jax.shard_map(shards, mesh=mesh, in_specs=in_specs, out_specs=out_specs, check_vma=False)
```

time: 439 us -> 192 us (0.44)
  waiting for transfers between devices: 260 us -> 91.7 us
  local copies, waits for them, and re-layouts: 68.5 us -> 4.58 us
  starting transfers between devices: 0.31 us -> 63.6 us
  blocking collectives: 61.9 us -> 0 us
  Pallas kernels: 0 us -> 22.8 us
  matrix products: 23.4 us -> 5.51 us
  between operations: 13.3 us -> 0.29 us
  other arithmetic: 10.2 us -> 3.5 us
    psum x2 -> x0, waiting for transfers between devices: 221 us -> none  [the longest x1 115 us: shards(): whole_sum = lax.psum(partial_fm, ('emb', 'section'))]
    all_to_all x2 -> x0, blocking collectives: 61.9 us -> none  [the longest x1 38.3 us: shards(): lax.all_to_all(session, ('emb', 'section'), split_axis=2, concat_axis=0,...]
    ppermute x0 -> x22, waiting for transfers between devices: none -> 58.8 us  [the longest x6 44.4 us: ring(): ups.append(lax.ppermute(ups[-1], 'emb', UP))]
    ppermute x0 -> x22, starting transfers between devices: none -> 46.6 us  [the longest x6 15.1 us: ring(): downs.append(lax.ppermute(downs[-1], 'emb', DOWN))]
    all_gather x1 -> x0, waiting for transfers between devices: 39.5 us -> none  [shards(): lax.all_gather(hidden, ('emb', 'section'), axis=1, tiled=True)]
    all_to_all x0 -> x3, waiting for transfers between devices: none -> 32.8 us  [the longest x1 16.7 us: shards(): out = lax.all_to_all(send.reshape(16, U, 1024), 'dp', 0, 0, tiled=True)]
    all_to_all x5 -> x0, local copies, waits for them, and re-layouts: 32.7 us -> none  [the longest x3 23.5 us: shards(): lax.all_to_all(lax.all_to_all(session, ('emb', 'section'), split_axis=2,...]
    pallas_call x0 -> x6, Pallas kernels: none -> 22.8 us  [the longest x1 13 us: shards(): pl.pallas_call(out_kernel, grid_spec=pltpu.PrefetchScalarGridSpec(num_sca...]
  transfers between devices with their start and end apart: 3 -> 25, of which waited for: 3 -> 14; matrix products, arithmetic and copies ran while one was open for 2% -> 6% of each run, Pallas kernels for 0% -> 4%
where the time goes in v1:
time: 192 us
  waiting for transfers between devices  91.7 us (48%)
  starting transfers between devices  63.6 us (33%)
  Pallas kernels  22.8 us (12%)
  matrix products  5.51 us (3%)
  local copies, waits for them, and re-layouts  4.58 us (2%)
  other arithmetic  3.5 us (2%)
    ppermute x6, waiting for transfers between devices, ring(): ups.append(lax.ppermute(ups[-1], 'emb', UP))  44.4 us
    all_to_all x1, waiting for transfers between devices, shards(): out = lax.all_to_all(send.reshape(16, U, 1024), 'dp', 0, 0, tiled=True)  16.7 us
    all_to_all x1, waiting for transfers between devices, shards(): x = lax.all_to_all(chunks, 'dp', 0, 0, tiled=True).reshape(N * U, D)  16.1 us
    ppermute x6, starting transfers between devices, ring(): downs.append(lax.ppermute(downs[-1], 'emb', DOWN))  15.1 us
    pallas_call x1, Pallas kernels, shards(): pl.pallas_call(out_kernel, grid_spec=pltpu.PrefetchScalarGridSpec(num_sca...  13 us
    ppermute x1, starting transfers between devices, shards(): came = lax.ppermute(o_other, 'section', SWAP)  13 us
    ppermute x3, waiting for transfers between devices, shards(): lax.ppermute(totals, 'emb', [(i, i ^ bit) for i in range(Z)])  8.37 us
    all_to_all x1, starting transfers between devices, shards(): lax.all_to_all(slices.reshape(Z, 2 * U, 1024), 'emb', 0, 0, tiled=True)  8.19 us
  transfers between devices with their start and end apart: 25, of which 14 were waited for; matrix products, arithmetic and copies ran while one was open for 6% of the time, Pallas kernels for 4%

profile of v1, /device:TPU:1, one launch (start us, length us, event | category | flops | bytes accessed | tf_op | source)
XLA Modules:
  0.0 192.0 jit_solution(13322879403715646811)
XLA Ops:
  0.0 3.2 %collective-permute-start.17 = (bf16[512,4096]{1,0:T(8,128)(2,1)}, bf16[512,4096]{1,0:T(8,128)(2,1)}, u32[]{:S(2)}, u32[]{:S(2)}) collective-permute-start(bf16[512,4096]{1,0:T(8,128)(2,1)} %bitcast.45), channel_id=1, source_target_pairs={{0,1},{1,0},{2,3},{3,2},{4,5},{5,4},{6,7},{7,6},{8,9},{9,8},{10,11... | collective-permute-start | bytes 12582920 | tf_op jit(solution)/shard_map/ppermute | solution.py:182
  3.2 0.8 copy.15
  4.1 0.7 convert_element_type.18
  4.8 0.7 convert_element_type.20
  5.5 1.3 fusion.5
  6.8 4.7 %fusion.1 = f32[512,4,1,256]{3,2,1,0:T(1,128)S(1)} fusion(bf16[512,4,4,256]{3,2,1,0:T(4,128)(2,1)} %param.10, pred[512,4,4,1]{2,1,0,3:T(4,128)(4,1)S(1)} %fusion.5), kind=kOutput, calls=%fused_computation.2 | convolution fusion | flops 4194304 | bytes 6299648 | tf_op jit(solution)/shard_map/usj,usjd->usd/dot_general | solution.py:185
  11.5 0.8 multiply_convert_fusion
  12.4 1.1 copy.30
  13.4 5.1 %all-to-all-start = ((bf16[16,4,32,256]{3,2,1,0:T(8,128)(2,1)}), bf16[16,4,32,256]{3,2,1,0:T(8,128)(2,1)S(1)}, u32[]{:S(2)}, u32[]{:S(2)}) async-start(bf16[16,4,32,256]{3,2,1,0:T(8,128)(2,1)} %bitcast.35), calls=%async_computation | async-start | bytes 2097152 | tf_op jit(solution)/shard_map/all_to_all | solution.py:191
  18.6 0.4 collective-permute-start.8
  19.0 0.4 fusion.perm_ref
  19.8 16.1 %all-to-all-done = bf16[16,4,32,256]{3,2,1,0:T(8,128)(2,1)S(1)} async-done(((bf16[16,4,32,256]{3,2,1,0:T(8,128)(2,1)}), bf16[16,4,32,256]{3,2,1,0:T(8,128)(2,1)S(1)}, u32[]{:S(2)}, u32[]{:S(2)}) %all-to-all-start) | async-done | bytes 1048608 | tf_op jit(solution)/shard_map/all_to_all | solution.py:191
  35.9 3.5 %fm_rows.1 = (bf16[32,2048]{1,0:T(8,128)(2,1)S(1)}, f32[1024,128]{1,0:T(8,128)S(1)}, f32[1024,128]{1,0:T(8,128)S(1)}) custom-call(bf16[2048,256]{1,0:T(8,128)(2,1)S(1)} %bitcast.39, bf16[64,64]{1,0:T(8,128)(2,1)S(1)} %copy.20.mix_ref, f32[16,128]{1,0:T(8,128)S(1)} %bitcast.44), custom_call_target="tpu_custom_call" | custom-call | tf_op jit(solution)/shard_map/fm_rows/pallas_call | solution.py:195
  39.5 1.4 slices.1
  40.9 1.0 copy-done.1
  41.9 8.2 %all-to-all-start.1 = ((bf16[8,64,1024]{2,1,0:T(8,128)(2,1)}), bf16[8,64,1024]{2,1,0:T(8,128)(2,1)S(1)}, u32[]{:S(2)}, u32[]{:S(2)}) async-start(bf16[8,64,1024]{2,1,0:T(8,128)(2,1)} %bitcast.41), calls=%async_computation.1 | async-start | bytes 2097152 | tf_op jit(solution)/shard_map/all_to_all | solution.py:218
  50.0 1.5 collective-permute-start
  51.5 1.2 collective-permute-start.3
  52.8 23.8 %collective-permute-done.refs_1_ = bf16[32,2048]{1,0:T(8,128)(2,1)S(1)} collective-permute-done((bf16[32,2048]{1,0:T(8,128)(2,1)S(1)}, bf16[32,2048]{1,0:T(8,128)(2,1)S(1)}, u32[]{:S(2)}, u32[]{:S(2)}) %collective-permute-start) | collective-permute-done | bytes 131104 | tf_op jit(solution)/shard_map/ppermute | solution.py:165
  76.5 2.8 %collective-permute-start.4 = (bf16[32,2048]{1,0:T(8,128)(2,1)S(1)}, bf16[32,2048]{1,0:T(8,128)(2,1)S(1)}, u32[]{:S(2)}, u32[]{:S(2)}) collective-permute-start(bf16[32,2048]{1,0:T(8,128)(2,1)S(1)} %collective-permute-done.3.refs_4_), channel_id=1, source_target_pairs={{0,14},{2,0},{4,2},{6,4},{8,6},{10,8},{12,10},{14,12},{1,15},{3,1}... | collective-permute-start | bytes 393224 | tf_op jit(solution)/shard_map/ppermute | solution.py:166
  79.3 2.3 %collective-permute-done.1.refs_2_ = bf16[32,2048]{1,0:T(8,128)(2,1)S(1)} collective-permute-done((bf16[32,2048]{1,0:T(8,128)(2,1)S(1)}, bf16[32,2048]{1,0:T(8,128)(2,1)S(1)}, u32[]{:S(2)}, u32[]{:S(2)}) %collective-permute-start.1) | collective-permute-done | bytes 131104 | tf_op jit(solution)/shard_map/ppermute | solution.py:165
  81.7 2.7 %collective-permute-start.5 = (bf16[32,2048]{1,0:T(8,128)(2,1)S(1)}, bf16[32,2048]{1,0:T(8,128)(2,1)S(1)}, u32[]{:S(2)}, u32[]{:S(2)}) collective-permute-start(bf16[32,2048]{1,0:T(8,128)(2,1)S(1)} %collective-permute-done.4.refs_5_), channel_id=1, source_target_pairs={{0,14},{2,0},{4,2},{6,4},{8,6},{10,8},{12,10},{14,12},{1,15},{3,1}... | collective-permute-start | bytes 393224 | tf_op jit(solution)/shard_map/ppermute | solution.py:166
  84.4 2.4 %collective-permute-done.2.refs_3_ = bf16[32,2048]{1,0:T(8,128)(2,1)S(1)} collective-permute-done((bf16[32,2048]{1,0:T(8,128)(2,1)S(1)}, bf16[32,2048]{1,0:T(8,128)(2,1)S(1)}, u32[]{:S(2)}, u32[]{:S(2)}) %collective-permute-start.2) | collective-permute-done | bytes 131104 | tf_op jit(solution)/shard_map/ppermute | solution.py:165
  86.8 2.9 %collective-permute-start.7 = (bf16[16,2048]{1,0:T(8,128)(2,1)S(1)}, bf16[16,2048]{1,0:T(8,128)(2,1)S(1)}, u32[]{:S(2)}, u32[]{:S(2)}) collective-permute-start(bf16[16,2048]{1,0:T(8,128)(2,1)S(1)} %slice.17), channel_id=1, source_target_pairs={{0,14},{2,0},{4,2},{6,4},{8,6},{10,8},{12,10},{14,12},{1,15},{3,1}... | collective-permute-start | bytes 196616 | tf_op jit(solution)/shard_map/ppermute | solution.py:169
  89.8 2.3 %collective-permute-done.6.refs_7_ = bf16[16,2048]{1,0:T(8,128)(2,1)S(1)} collective-permute-done((bf16[16,2048]{1,0:T(8,128)(2,1)S(1)}, bf16[16,2048]{1,0:T(8,128)(2,1)S(1)}, u32[]{:S(2)}, u32[]{:S(2)}) %collective-permute-start.6) | collective-permute-done | bytes 65568 | tf_op jit(solution)/shard_map/ppermute | solution.py:168
  92.1 2.3 %hidden.1.refs_0_ = bf16[256,512]{1,0:T(8,128)(2,1)S(1)} custom-call(s32[2]{0:T(128)S(1)} %pad_add_fusion.at_ref.c_ref, bf16[32,2048]{1,0:T(8,128)(2,1)S(1)} %get-tuple-element.14.refs_0_, bf16[32,2048]{1,0:T(8,128)(2,1)S(1)} %collective-permute-done.refs_1_, bf16[32,2048]{1,0:T(8,128)(2,1)S(1)} %collective-permute-done.1.refs_2_, ...), custom_call_target="tpu_custom_call" | custom-call | tf_op jit(solution)/shard_map/hidden/pallas_call | solution.py:222
  94.5 3.0 %collective-permute-start.12 = (bf16[256,512]{1,0:T(8,128)(2,1)S(1)}, bf16[256,512]{1,0:T(8,128)(2,1)S(1)}, u32[]{:S(2)}, u32[]{:S(2)}) collective-permute-start(bf16[256,512]{1,0:T(8,128)(2,1)S(1)} %hidden.1.refs_0_), channel_id=1, source_target_pairs={{0,14},{2,0},{4,2},{6,4},{8,6},{10,8},{12,10},{14,12},{1,15},{3,1}... | collective-permute-start | bytes 786440 | tf_op jit(solution)/shard_map/ppermute | solution.py:166
  97.5 3.7 %collective-permute-done.9.refs_1_ = bf16[256,512]{1,0:T(8,128)(2,1)S(1)} collective-permute-done((bf16[256,512]{1,0:T(8,128)(2,1)S(1)}, bf16[256,512]{1,0:T(8,128)(2,1)S(1)}, u32[]{:S(2)}, u32[]{:S(2)}) %collective-permute-start.9) | collective-permute-done | bytes 262176 | tf_op jit(solution)/shard_map/ppermute | solution.py:165
  101.2 2.8 %collective-permute-start.13 = (bf16[256,512]{1,0:T(8,128)(2,1)S(1)}, bf16[256,512]{1,0:T(8,128)(2,1)S(1)}, u32[]{:S(2)}, u32[]{:S(2)}) collective-permute-start(bf16[256,512]{1,0:T(8,128)(2,1)S(1)} %collective-permute-done.12.refs_4_), channel_id=1, source_target_pairs={{0,14},{2,0},{4,2},{6,4},{8,6},{10,8},{12,10},{14,12},{1,15},{3,1}... | collective-permute-start | bytes 786440 | tf_op jit(solution)/shard_map/ppermute | solution.py:166
  103.9 6.5 %collective-permute-done.10.refs_2_ = bf16[256,512]{1,0:T(8,128)(2,1)S(1)} collective-permute-done((bf16[256,512]{1,0:T(8,128)(2,1)S(1)}, bf16[256,512]{1,0:T(8,128)(2,1)S(1)}, u32[]{:S(2)}, u32[]{:S(2)}) %collective-permute-start.10) | collective-permute-done | bytes 262176 | tf_op jit(solution)/shard_map/ppermute | solution.py:165
  110.4 2.7 %collective-permute-start.14 = (bf16[256,512]{1,0:T(8,128)(2,1)S(1)}, bf16[256,512]{1,0:T(8,128)(2,1)S(1)}, u32[]{:S(2)}, u32[]{:S(2)}) collective-permute-start(bf16[256,512]{1,0:T(8,128)(2,1)S(1)} %collective-permute-done.13.refs_5_), channel_id=1, source_target_pairs={{0,14},{2,0},{4,2},{6,4},{8,6},{10,8},{12,10},{14,12},{1,15},{3,1}... | collective-permute-start | bytes 786440 | tf_op jit(solution)/shard_map/ppermute | solution.py:166
  113.1 5.7 %collective-permute-done.11.refs_3_ = bf16[256,512]{1,0:T(8,128)(2,1)S(1)} collective-permute-done((bf16[256,512]{1,0:T(8,128)(2,1)S(1)}, bf16[256,512]{1,0:T(8,128)(2,1)S(1)}, u32[]{:S(2)}, u32[]{:S(2)}) %collective-permute-start.11) | collective-permute-done | bytes 262176 | tf_op jit(solution)/shard_map/ppermute | solution.py:165
  118.9 2.7 %collective-permute-start.16 = (bf16[128,512]{1,0:T(8,128)(2,1)S(1)}, bf16[128,512]{1,0:T(8,128)(2,1)S(1)}, u32[]{:S(2)}, u32[]{:S(2)}) collective-permute-start(bf16[128,512]{1,0:T(8,128)(2,1)S(1)} %slice.19), channel_id=1, source_target_pairs={{0,14},{2,0},{4,2},{6,4},{8,6},{10,8},{12,10},{14,12},{1,15},{3,1}... | collective-permute-start | bytes 393224 | tf_op jit(solution)/shard_map/ppermute | solution.py:169
  121.6 2.3 %collective-permute-done.15.refs_7_ = bf16[128,512]{1,0:T(8,128)(2,1)S(1)} collective-permute-done((bf16[128,512]{1,0:T(8,128)(2,1)S(1)}, bf16[128,512]{1,0:T(8,128)(2,1)S(1)}, u32[]{:S(2)}, u32[]{:S(2)}) %collective-permute-start.15) | collective-permute-done | bytes 131104 | tf_op jit(solution)/shard_map/ppermute | solution.py:168
  123.9 13.0 %fm_out.1 = (f32[256,512]{1,0:T(8,128)S(1)}, f32[256,512]{1,0:T(8,128)S(1)}, f32[32,256]{1,0:T(8,128)S(1)}, f32[32,256]{1,0:T(8,128)S(1)}) custom-call(s32[2]{0:T(128)S(1)} %pad_add_fusion.at_ref.c_ref, bf16[256,512]{1,0:T(8,128)(2,1)S(1)} %hidden.1.refs_0_, bf16[256,512]{1,0:T(8,128)(2,1)S(1)} %collective-permute-done.9.refs_1_, ...), custom_call_target="tpu_custom_call" | custom-call | tf_op jit(solution)/shard_map/fm_out/pallas_call | solution.py:235
  137.1 3.1 %collective-permute-done.18 = f32[64,256]{1,0:T(8,128)S(1)} collective-permute-done((f32[64,256]{1,0:T(8,128)S(1)}, f32[64,256]{1,0:T(8,128)S(1)}, u32[]{:S(2)}, u32[]{:S(2)}) %collective-permute-start.18) | collective-permute-done | bytes 65568 | tf_op jit(solution)/shard_map/ppermute | solution.py:257
  140.2 3.5 %collective-permute-start.19 = (f32[64,256]{1,0:T(8,128)S(1)}, f32[64,256]{1,0:T(8,128)S(1)}, u32[]{:S(2)}, u32[]{:S(2)}) collective-permute-start(f32[64,256]{1,0:T(8,128)S(1)} %add.61), channel_id=1, source_target_pairs={{0,4},{2,6},{4,0},{6,2},{8,12},{10,14},{12,8},{14,10},{1,5},{3,7},... | collective-permute-start | bytes 196616 | tf_op jit(solution)/shard_map/ppermute | solution.py:257
  143.7 1.7 collective-permute-done.19
  145.4 3.9 %collective-permute-start.20 = (f32[64,256]{1,0:T(8,128)S(1)}, f32[64,256]{1,0:T(8,128)S(1)}, u32[]{:S(2)}, u32[]{:S(2)}) collective-permute-start(f32[64,256]{1,0:T(8,128)S(1)} %add.62), channel_id=1, source_target_pairs={{0,8},{2,10},{4,12},{6,14},{8,0},{10,2},{12,4},{14,6},{1,9},{3,11}... | collective-permute-start | bytes 196616 | tf_op jit(solution)/shard_map/ppermute | solution.py:257
  149.3 3.6 %collective-permute-done.20 = f32[64,256]{1,0:T(8,128)S(1)} collective-permute-done((f32[64,256]{1,0:T(8,128)S(1)}, f32[64,256]{1,0:T(8,128)S(1)}, u32[]{:S(2)}, u32[]{:S(2)}) %collective-permute-start.20) | collective-permute-done | bytes 65568 | tf_op jit(solution)/shard_map/ppermute | solution.py:257
  152.9 1.1 scale.1
  154.0 13.0 %collective-permute-start.21 = (bf16[256,1024]{1,0:T(8,128)(2,1)S(1)}, bf16[256,1024]{1,0:T(8,128)(2,1)S(1)}, u32[]{:S(2)}, u32[]{:S(2)}) collective-permute-start(bf16[256,1024]{1,0:T(8,128)(2,1)S(1)} %get-tuple-element.22), channel_id=1, source_target_pairs={{0,1},{1,0},{2,3},{3,2},{4,5},{5,4},{6,7},{7,6},{8,9},{9,8},{10,11... | collective-permute-start | bytes 1572872 | tf_op jit(solution)/shard_map/ppermute | solution.py:267
  167.0 1.5 collective-permute-done.21
  168.7 1.1 copy.21
  169.8 3.7 %all-to-all-start.2 = ((bf16[16,32,1024]{2,1,0:T(8,128)(2,1)}), bf16[16,32,1024]{2,1,0:T(8,128)(2,1)S(1)}, u32[]{:S(2)}, u32[]{:S(2)}) async-start(bf16[16,32,1024]{2,1,0:T(8,128)(2,1)} %bitcast.20), calls=%async_computation.2 | async-start | bytes 2097152 | tf_op jit(solution)/shard_map/all_to_all | solution.py:272
  173.4 0.3 reshape_tile.4.gain_ref
  173.7 16.7 %all-to-all-done.2 = bf16[16,32,1024]{2,1,0:T(8,128)(2,1)S(1)} async-done(((bf16[16,32,1024]{2,1,0:T(8,128)(2,1)}), bf16[16,32,1024]{2,1,0:T(8,128)(2,1)S(1)}, u32[]{:S(2)}, u32[]{:S(2)}) %all-to-all-start.2) | async-done | bytes 1048608 | tf_op jit(solution)/shard_map/all_to_all | solution.py:272
  190.5 1.5 finish.1
  (48 shorter events, 1.0 us)
Async XLA Ops:
  0.0 11.5 %copy-start = (bf16[256,256]{1,0:T(8,128)(2,1)S(1)}, bf16[256,256]{1,0:T(8,128)(2,1)}, u32[]{:S(2)}) copy-start(bf16[256,256]{1,0:T(8,128)(2,1)} %param.13) | copy-start | bytes 393220
  0.0 123.9 %collective-permute-start.17 = (bf16[512,4096]{1,0:T(8,128)(2,1)}, bf16[512,4096]{1,0:T(8,128)(2,1)}, u32[]{:S(2)}, u32[]{:S(2)}) collective-permute-start(bf16[512,4096]{1,0:T(8,128)(2,1)} %bitcast.45), channel_id=1, source_target_pairs={{0,1},{1,0},{2,3},{3,2},{4,5},{5,4},{6,7},{7,6},{8,9},{9,8},{10,11... | collective-permute-start | bytes 12582920 | tf_op jit(solution)/shard_map/ppermute | solution.py:182
  13.4 6.0 %copy-start.3 = (bf16[64,32]{0,1:T(8,128)(2,1)S(1)}, bf16[64,32]{0,1:T(8,128)(2,1)}, u32[]{:S(2)}) copy-start(bf16[64,32]{0,1:T(8,128)(2,1)} %param.14) | copy-start | bytes 12292
  13.4 6.1 %copy-start.4 = (bf16[32,64]{1,0:T(8,128)(2,1)S(1)}, bf16[32,64]{1,0:T(8,128)(2,1)}, u32[]{:S(2)}) copy-start(bf16[32,64]{1,0:T(8,128)(2,1)} %param.18) | copy-start | bytes 12292
  13.4 22.5 %copy-start.2 = (f32[2048]{0:T(1024)S(1)}, f32[2048]{0:T(1024)}, u32[]{:S(2)}) copy-start(f32[2048]{0:T(1024)} %param.15) | copy-start | bytes 24580
  13.4 22.5 %all-to-all-start = ((bf16[16,4,32,256]{3,2,1,0:T(8,128)(2,1)}), bf16[16,4,32,256]{3,2,1,0:T(8,128)(2,1)S(1)}, u32[]{:S(2)}, u32[]{:S(2)}) async-start(bf16[16,4,32,256]{3,2,1,0:T(8,128)(2,1)} %bitcast.35), calls=%async_computation | async-start | bytes 2097152 | tf_op jit(solution)/shard_map/all_to_all | solution.py:191
  18.6 71.2 %collective-permute-start.8 = (bf16[2048,256]{1,0:T(8,128)(2,1)}, bf16[2048,256]{1,0:T(8,128)(2,1)}, u32[]{:S(2)}, u32[]{:S(2)}) collective-permute-start(bf16[2048,256]{1,0:T(8,128)(2,1)} %refs_9_.1), channel_id=1, source_target_pairs={{0,1},{1,0},{2,3},{3,2},{4,5},{5,4},{6,7},{7,6},{8,9},{9,8},{10,11... | collective-permute-start | bytes 3145736 | tf_op jit(solution)/shard_map/ppermute | solution.py:180
  40.9 1.0 copy-start.1
  41.9 82.1 %all-to-all-start.1 = ((bf16[8,64,1024]{2,1,0:T(8,128)(2,1)}), bf16[8,64,1024]{2,1,0:T(8,128)(2,1)S(1)}, u32[]{:S(2)}, u32[]{:S(2)}) async-start(bf16[8,64,1024]{2,1,0:T(8,128)(2,1)} %bitcast.41), calls=%async_computation.1 | async-start | bytes 2097152 | tf_op jit(solution)/shard_map/all_to_all | solution.py:218
  50.0 26.5 %collective-permute-start = (bf16[32,2048]{1,0:T(8,128)(2,1)S(1)}, bf16[32,2048]{1,0:T(8,128)(2,1)S(1)}, u32[]{:S(2)}, u32[]{:S(2)}) collective-permute-start(bf16[32,2048]{1,0:T(8,128)(2,1)S(1)} %get-tuple-element.14.refs_0_), channel_id=1, source_target_pairs={{0,2},{2,4},{4,6},{6,8},{8,10},{10,12},{12,14},{14,0},{1,3},{3,5},... | collective-permute-start | bytes 393224 | tf_op jit(solution)/shard_map/ppermute | solution.py:165
  51.5 25.0 %collective-permute-start.3 = (bf16[32,2048]{1,0:T(8,128)(2,1)S(1)}, bf16[32,2048]{1,0:T(8,128)(2,1)S(1)}, u32[]{:S(2)}, u32[]{:S(2)}) collective-permute-start(bf16[32,2048]{1,0:T(8,128)(2,1)S(1)} %get-tuple-element.14.refs_0_), channel_id=1, source_target_pairs={{0,14},{2,0},{4,2},{6,4},{8,6},{10,8},{12,10},{14,12},{1,15},{3,1}... | collective-permute-start | bytes 393224 | tf_op jit(solution)/shard_map/ppermute | solution.py:166
  76.5 5.2 %collective-permute-start.1 = (bf16[32,2048]{1,0:T(8,128)(2,1)S(1)}, bf16[32,2048]{1,0:T(8,128)(2,1)S(1)}, u32[]{:S(2)}, u32[]{:S(2)}) collective-permute-start(bf16[32,2048]{1,0:T(8,128)(2,1)S(1)} %collective-permute-done.refs_1_), channel_id=1, source_target_pairs={{0,2},{2,4},{4,6},{6,8},{8,10},{10,12},{12,14},{14,0},{1,3},{3,5},... | collective-permute-start | bytes 393224 | tf_op jit(solution)/shard_map/ppermute | solution.py:165
  76.5 5.2 %collective-permute-start.4 = (bf16[32,2048]{1,0:T(8,128)(2,1)S(1)}, bf16[32,2048]{1,0:T(8,128)(2,1)S(1)}, u32[]{:S(2)}, u32[]{:S(2)}) collective-permute-start(bf16[32,2048]{1,0:T(8,128)(2,1)S(1)} %collective-permute-done.3.refs_4_), channel_id=1, source_target_pairs={{0,14},{2,0},{4,2},{6,4},{8,6},{10,8},{12,10},{14,12},{1,15},{3,1}... | collective-permute-start | bytes 393224 | tf_op jit(solution)/shard_map/ppermute | solution.py:166
  81.7 5.1 %collective-permute-start.2 = (bf16[32,2048]{1,0:T(8,128)(2,1)S(1)}, bf16[32,2048]{1,0:T(8,128)(2,1)S(1)}, u32[]{:S(2)}, u32[]{:S(2)}) collective-permute-start(bf16[32,2048]{1,0:T(8,128)(2,1)S(1)} %collective-permute-done.1.refs_2_), channel_id=1, source_target_pairs={{0,2},{2,4},{4,6},{6,8},{8,10},{10,12},{12,14},{14,0},{1,3},{3,5},... | collective-permute-start | bytes 393224 | tf_op jit(solution)/shard_map/ppermute | solution.py:165
  81.7 5.1 %collective-permute-start.5 = (bf16[32,2048]{1,0:T(8,128)(2,1)S(1)}, bf16[32,2048]{1,0:T(8,128)(2,1)S(1)}, u32[]{:S(2)}, u32[]{:S(2)}) collective-permute-start(bf16[32,2048]{1,0:T(8,128)(2,1)S(1)} %collective-permute-done.4.refs_5_), channel_id=1, source_target_pairs={{0,14},{2,0},{4,2},{6,4},{8,6},{10,8},{12,10},{14,12},{1,15},{3,1}... | collective-permute-start | bytes 393224 | tf_op jit(solution)/shard_map/ppermute | solution.py:166
  86.7 5.3 %collective-permute-start.6 = (bf16[16,2048]{1,0:T(8,128)(2,1)S(1)}, bf16[16,2048]{1,0:T(8,128)(2,1)S(1)}, u32[]{:S(2)}, u32[]{:S(2)}) collective-permute-start(bf16[16,2048]{1,0:T(8,128)(2,1)S(1)} %slice.16), channel_id=1, source_target_pairs={{0,2},{2,4},{4,6},{6,8},{8,10},{10,12},{12,14},{14,0},{1,3},{3,5},... | collective-permute-start | bytes 196616 | tf_op jit(solution)/shard_map/ppermute | solution.py:168
  86.8 5.3 %collective-permute-start.7 = (bf16[16,2048]{1,0:T(8,128)(2,1)S(1)}, bf16[16,2048]{1,0:T(8,128)(2,1)S(1)}, u32[]{:S(2)}, u32[]{:S(2)}) collective-permute-start(bf16[16,2048]{1,0:T(8,128)(2,1)S(1)} %slice.17), channel_id=1, source_target_pairs={{0,14},{2,0},{4,2},{6,4},{8,6},{10,8},{12,10},{14,12},{1,15},{3,1}... | collective-permute-start | bytes 196616 | tf_op jit(solution)/shard_map/ppermute | solution.py:169
  94.4 6.8 %collective-permute-start.9 = (bf16[256,512]{1,0:T(8,128)(2,1)S(1)}, bf16[256,512]{1,0:T(8,128)(2,1)S(1)}, u32[]{:S(2)}, u32[]{:S(2)}) collective-permute-start(bf16[256,512]{1,0:T(8,128)(2,1)S(1)} %hidden.1.refs_0_), channel_id=1, source_target_pairs={{0,2},{2,4},{4,6},{6,8},{8,10},{10,12},{12,14},{14,0},{1,3},{3,5},... | collective-permute-start | bytes 786440 | tf_op jit(solution)/shard_map/ppermute | solution.py:165
  94.5 6.7 %collective-permute-start.12 = (bf16[256,512]{1,0:T(8,128)(2,1)S(1)}, bf16[256,512]{1,0:T(8,128)(2,1)S(1)}, u32[]{:S(2)}, u32[]{:S(2)}) collective-permute-start(bf16[256,512]{1,0:T(8,128)(2,1)S(1)} %hidden.1.refs_0_), channel_id=1, source_target_pairs={{0,14},{2,0},{4,2},{6,4},{8,6},{10,8},{12,10},{14,12},{1,15},{3,1}... | collective-permute-start | bytes 786440 | tf_op jit(solution)/shard_map/ppermute | solution.py:166
  101.2 9.3 %collective-permute-start.10 = (bf16[256,512]{1,0:T(8,128)(2,1)S(1)}, bf16[256,512]{1,0:T(8,128)(2,1)S(1)}, u32[]{:S(2)}, u32[]{:S(2)}) collective-permute-start(bf16[256,512]{1,0:T(8,128)(2,1)S(1)} %collective-permute-done.9.refs_1_), channel_id=1, source_target_pairs={{0,2},{2,4},{4,6},{6,8},{8,10},{10,12},{12,14},{14,0},{1,3},{3,5},... | collective-permute-start | bytes 786440 | tf_op jit(solution)/shard_map/ppermute | solution.py:165
  101.2 9.3 %collective-permute-start.13 = (bf16[256,512]{1,0:T(8,128)(2,1)S(1)}, bf16[256,512]{1,0:T(8,128)(2,1)S(1)}, u32[]{:S(2)}, u32[]{:S(2)}) collective-permute-start(bf16[256,512]{1,0:T(8,128)(2,1)S(1)} %collective-permute-done.12.refs_4_), channel_id=1, source_target_pairs={{0,14},{2,0},{4,2},{6,4},{8,6},{10,8},{12,10},{14,12},{1,15},{3,1}... | collective-permute-start | bytes 786440 | tf_op jit(solution)/shard_map/ppermute | solution.py:166
  110.4 8.4 %collective-permute-start.11 = (bf16[256,512]{1,0:T(8,128)(2,1)S(1)}, bf16[256,512]{1,0:T(8,128)(2,1)S(1)}, u32[]{:S(2)}, u32[]{:S(2)}) collective-permute-start(bf16[256,512]{1,0:T(8,128)(2,1)S(1)} %collective-permute-done.10.refs_2_), channel_id=1, source_target_pairs={{0,2},{2,4},{4,6},{6,8},{8,10},{10,12},{12,14},{14,0},{1,3},{3,5},... | collective-permute-start | bytes 786440 | tf_op jit(solution)/shard_map/ppermute | solution.py:165
  110.4 8.5 %collective-permute-start.14 = (bf16[256,512]{1,0:T(8,128)(2,1)S(1)}, bf16[256,512]{1,0:T(8,128)(2,1)S(1)}, u32[]{:S(2)}, u32[]{:S(2)}) collective-permute-start(bf16[256,512]{1,0:T(8,128)(2,1)S(1)} %collective-permute-done.13.refs_5_), channel_id=1, source_target_pairs={{0,14},{2,0},{4,2},{6,4},{8,6},{10,8},{12,10},{14,12},{1,15},{3,1}... | collective-permute-start | bytes 786440 | tf_op jit(solution)/shard_map/ppermute | solution.py:166
  118.8 5.1 %collective-permute-start.15 = (bf16[128,512]{1,0:T(8,128)(2,1)S(1)}, bf16[128,512]{1,0:T(8,128)(2,1)S(1)}, u32[]{:S(2)}, u32[]{:S(2)}) collective-permute-start(bf16[128,512]{1,0:T(8,128)(2,1)S(1)} %slice.18), channel_id=1, source_target_pairs={{0,2},{2,4},{4,6},{6,8},{8,10},{10,12},{12,14},{14,0},{1,3},{3,5},... | collective-permute-start | bytes 393224 | tf_op jit(solution)/shard_map/ppermute | solution.py:168
  118.9 5.0 %collective-permute-start.16 = (bf16[128,512]{1,0:T(8,128)(2,1)S(1)}, bf16[128,512]{1,0:T(8,128)(2,1)S(1)}, u32[]{:S(2)}, u32[]{:S(2)}) collective-permute-start(bf16[128,512]{1,0:T(8,128)(2,1)S(1)} %slice.19), channel_id=1, source_target_pairs={{0,14},{2,0},{4,2},{6,4},{8,6},{10,8},{12,10},{14,12},{1,15},{3,1}... | collective-permute-start | bytes 393224 | tf_op jit(solution)/shard_map/ppermute | solution.py:169
  137.0 3.2 %collective-permute-start.18 = (f32[64,256]{1,0:T(8,128)S(1)}, f32[64,256]{1,0:T(8,128)S(1)}, u32[]{:S(2)}, u32[]{:S(2)}) collective-permute-start(f32[64,256]{1,0:T(8,128)S(1)} %constant_dynamic-update-slice_fusion), channel_id=1, source_target_pairs={{0,2},{2,0},{4,6},{6,4},{8,10},{10,8},{12,14},{14,12},{1,3},{3,1},... | collective-permute-start | bytes 196616 | tf_op jit(solution)/shard_map/ppermute | solution.py:257
  140.2 5.2 %collective-permute-start.19 = (f32[64,256]{1,0:T(8,128)S(1)}, f32[64,256]{1,0:T(8,128)S(1)}, u32[]{:S(2)}, u32[]{:S(2)}) collective-permute-start(f32[64,256]{1,0:T(8,128)S(1)} %add.61), channel_id=1, source_target_pairs={{0,4},{2,6},{4,0},{6,2},{8,12},{10,14},{12,8},{14,10},{1,5},{3,7},... | collective-permute-start | bytes 196616 | tf_op jit(solution)/shard_map/ppermute | solution.py:257
  145.4 7.6 %collective-permute-start.20 = (f32[64,256]{1,0:T(8,128)S(1)}, f32[64,256]{1,0:T(8,128)S(1)}, u32[]{:S(2)}, u32[]{:S(2)}) collective-permute-start(f32[64,256]{1,0:T(8,128)S(1)} %add.62), channel_id=1, source_target_pairs={{0,8},{2,10},{4,12},{6,14},{8,0},{10,2},{12,4},{14,6},{1,9},{3,11}... | collective-permute-start | bytes 196616 | tf_op jit(solution)/shard_map/ppermute | solution.py:257
  154.0 14.5 %collective-permute-start.21 = (bf16[256,1024]{1,0:T(8,128)(2,1)S(1)}, bf16[256,1024]{1,0:T(8,128)(2,1)S(1)}, u32[]{:S(2)}, u32[]{:S(2)}) collective-permute-start(bf16[256,1024]{1,0:T(8,128)(2,1)S(1)} %get-tuple-element.22), channel_id=1, source_target_pairs={{0,1},{1,0},{2,3},{3,2},{4,5},{5,4},{6,7},{7,6},{8,9},{9,8},{10,11... | collective-permute-start | bytes 1572872 | tf_op jit(solution)/shard_map/ppermute | solution.py:267
  168.7 4.7 %copy-start.5 = (f32[16]{0:T(128)S(1)}, f32[16]{0:T(128)}, u32[]{:S(2)}) copy-start(f32[16]{0:T(128)} %param.19) | copy-start | bytes 196
  169.8 20.7 %all-to-all-start.2 = ((bf16[16,32,1024]{2,1,0:T(8,128)(2,1)}), bf16[16,32,1024]{2,1,0:T(8,128)(2,1)S(1)}, u32[]{:S(2)}, u32[]{:S(2)}) async-start(bf16[16,32,1024]{2,1,0:T(8,128)(2,1)} %bitcast.20), calls=%async_computation.2 | async-start | bytes 2097152 | tf_op jit(solution)/shard_map/all_to_all | solution.py:272

commit v2 on v1

--- a/solution.py
+++ b/solution.py
@@ -55,7 +55,8 @@
         ).astype(BF)
 
 
-def slice_kernel(x_ref, comp_a, comp_b, perm_ref, out_ref, cut):
+def slice_kernel(at_ref, x_ref, comp_a, comp_b, perm_ref, *refs):
+    outs, (cut, made) = refs[:Z], refs[Z:]
     y = jnp.concatenate([comp_a[...], comp_b[...]], axis=1) + x_ref[32 * U :, :].astype(F32)
     m = jnp.mean(y, axis=-1, keepdims=True)
     q = jnp.mean(y * y, axis=-1, keepdims=True)
@@ -76,9 +77,11 @@
         for t in range(2):
             at = (2 * big + t) * U
             for e in range(8):
-                out_ref[t * 8 + e, :, big * 128 : big * 128 + 128] = o[
+                made[t * 4 + e // 2, e % 2, :, big * 128 : big * 128 + 128] = o[
                     at : at + U, e * 128 : e * 128 + 128
                 ]
+    for k, ref in enumerate(outs):
+        ref[...] = made[lax.rem(at_ref[0] + k, Z)]
 
 
 def hidden_kernel(at_ref, *refs):
@@ -94,43 +97,64 @@
         out_ref[:, pl.ds(pl.multiple_of(where * 256, 256), 256)] = jnp.maximum(h, 0.0).astype(BF)
 
 
-def out_kernel(at_ref, *refs):
-    chunks = refs[:9]
-    own, other, s_own, s_other, o_own, o_other, t1_ref, t2_ref = refs[9:]
-    z = at_ref[0]
-    users, wide = o_own.shape
+def part_kernel(n, at_ref, *refs):
+    chunks, weights = refs[:n], refs[n : 3 * n]
+    sums, outs = refs[3 * n : -2], refs[-2:]
+    for side, out in enumerate(outs):
+        acc = sum(dot_t(chunks[i][...], weights[2 * i + side][...]) for i in range(n))
+        out[...] = acc + sums[side][...] if sums else acc
+
+
+def part(place, blocks, weights, sums):
+    n = len(blocks)
+
+    def columns(k):
+        return pl.BlockSpec((512, 512), lambda i, at: (0, lax.rem(at[0] + k, Z)))
+
+    whole = pl.BlockSpec((Z * U, 512), lambda i, at: (0, 0))
+    return pl.pallas_call(
+        functools.partial(part_kernel, n),
+        grid_spec=pltpu.PrefetchScalarGridSpec(
+            num_scalar_prefetch=1,
+            grid=(1,),
+            in_specs=[whole] * n
+            + [columns(k) for k, _ in blocks for _ in range(2)]
+            + [whole] * len(sums),
+            out_specs=[whole] * 2,
+        ),
+        out_shape=[jax.ShapeDtypeStruct((Z * U, 512), F32)] * 2,
+        compiler_params=PARAMS,
+        cost_estimate=pl.CostEstimate(
+            flops=n * 2 * 2 * 256 * 512 * 512, bytes_accessed=n * 2**20, transcendentals=0
+        ),
+        name="fm_out_part",
+    )(place, *[v for _, v in blocks], *[w for _ in blocks for w in weights], *sums)
+
+
+def out_kernel(at_ref, low, high, w_own, w_other, a_own, a_other, *refs):
+    slices, (o_own, o_other, tot_ref) = refs[:Z], refs[Z:]
+    z, c = at_ref[0], at_ref[1]
+    half = low.shape[0]
+    for which, w, a, o in ((c, w_own, a_own, o_own), (1 - c, w_other, a_other, o_other)):
+        o[:half] = a[:half] + dot_t(low[...], w[...])
+        o[half:] = a[half:] + dot_t(high[...], w[...])
+        for k, ref in enumerate(slices):
+            rows = pl.ds(pl.multiple_of(lax.rem(z + Z - k, Z) * U, U), U)
+            o[rows, :] += ref[pl.ds(which, 1), :, :512][0].astype(F32)
     mask = (
-        lax.broadcasted_iota(jnp.int32, (8, wide), 1) // 16
-        == lax.broadcasted_iota(jnp.int32, (8, wide), 0)
+        lax.broadcasted_iota(jnp.int32, (32, 512), 1) // 16
+        == lax.broadcasted_iota(jnp.int32, (32, 512), 0)
     ).astype(BF)
-    t1 = jnp.zeros((8, users), F32)
-    t2 = jnp.zeros((8, users), F32)
-    for w, s, o in ((own, s_own, o_own), (other, s_other, o_other)):
-        acc = s[:, 0].reshape(users, wide).astype(F32)
-        for k, ref in zip((0, 7, 6, 5, 1, 2, 3), chunks[:7]):
-            at = pl.multiple_of(lax.rem(z + k, Z) * 512, 512)
-            acc += dot_t(ref[...], w[:, pl.ds(at, 512)])
-        at = pl.multiple_of(lax.rem(z + 4, Z) * 512, 512)
-        acc += jnp.concatenate(
-            [dot_t(chunks[7][...], w[:, pl.ds(at, 512)]), dot_t(chunks[8][...], w[:, pl.ds(at, 512)])],
-            axis=0,
-        )
-        o[...] = acc
-        for v, which in ((acc, 0), (acc * acc, 1)):
-            high = v.astype(BF)
-            low = (v - high.astype(F32)).astype(BF)
-            part = dot_t(mask, high) + dot_t(mask, low)
-            if which:
-                t2 += part
-            else:
-                t1 += part
-    t1_ref[...] = t1
-    t2_ref[...] = t2
-
-
-def scale_kernel(c_ref, s_own, s_other, tot_ref, slices_ref, o_own, o_other):
-    c = c_ref[1]
-    users = s_own.shape[0]
+    x, y = o_own[...], o_other[...]
+    for at, v in ((0, x + y), (32, x * x + y * y)):
+        upper = v.astype(BF)
+        rest = (v - upper.astype(F32)).astype(BF)
+        tot_ref[at : at + 32, :] = dot_t(mask, upper) + dot_t(mask, rest)
+
+
+def scale_kernel(at_ref, s_own, s_other, tot_ref, *refs):
+    slices, (o_own, o_other) = refs[:Z], refs[Z:]
+    z, c = at_ref[0], at_ref[1]
     m = tot_ref[:32, :] / D
     q = tot_ref[32:, :] / D
     r = lax.rsqrt(q - m * m + 1e-05)
@@ -150,7 +174,9 @@
     m, r = widen(m), widen(r)
     for which, s, o in ((c, s_own, o_own), (1 - c, s_other, o_other)):
         o[:, :512] = ((s[...] - m) * r).astype(BF)
-        o[:, 512:] = slices_ref[:, pl.ds(which, 1), :, 512:].reshape(users, 512)
+        for k, ref in enumerate(slices):
+            rows = pl.ds(pl.multiple_of(lax.rem(z + Z - k, Z) * U, U), U)
+            o[rows, 512:] = ref[pl.ds(which, 1), :, 512:][0]
 
 
 def finish_kernel(v_ref, gain_ref, o_ref):
@@ -158,17 +184,12 @@
     o_ref[...] = v.astype(BF)
 
 
-def ring(v):
-    half = v.shape[0] // 2
-    ups, downs = [v], [v]
-    for _ in range(3):
-        ups.append(lax.ppermute(ups[-1], "emb", UP))
-        downs.append(lax.ppermute(downs[-1], "emb", DOWN))
-    last = [
-        lax.ppermute(ups[-1][:half], "emb", UP),
-        lax.ppermute(downs[-1][half:], "emb", DOWN),
-    ]
-    return [*ups, *downs[1:], *last]
+def step(up, down):
+    return lax.ppermute(up, "emb", UP), lax.ppermute(down, "emb", DOWN)
+
+
+def after(value, event):
+    return lax.optimization_barrier((value, event))
 
 
 def shards(
@@ -183,10 +204,10 @@
 
     inside = (lax.broadcasted_iota(jnp.int32, (1, 1, slot_count), 2) < counts[:, :, None]).astype(BF)
     session_sums = jnp.einsum("usj,usjd->usd", inside, events, preferred_element_type=F32)
-    pooled = (session_sums / counts[:, :, None].astype(F32)).astype(BF)
+    share_of = live.astype(F32) / counts.astype(F32)
+    pooled = (session_sums * share_of[:, :, None]).astype(BF)
     encoded = jnp.dot(pooled.reshape(-1, full_width), enc_weight, preferred_element_type=F32)
-    encoded = encoded.reshape(users_enc, sess_dev, full_width)
-    session = (encoded * live[:, :, None].astype(F32)).astype(BF)
+    session = encoded.reshape(users_enc, sess_dev, full_width).astype(BF)
     chunks = jnp.transpose(session.reshape(16, U, sess_dev, D), (0, 2, 1, 3))
     x = lax.all_to_all(chunks, "dp", 0, 0, tiled=True).reshape(N * U, D)
 
@@ -208,17 +229,37 @@
     perm = (e * 128 + i * 16 + f == lax.broadcasted_iota(jnp.int32, (1, 1024), 1)).astype(BF)
     slices = pl.pallas_call(
         slice_kernel,
-        out_shape=jax.ShapeDtypeStruct((16, U, 1024), BF),
-        in_specs=[VMEM] * 4,
-        out_specs=VMEM,
-        scratch_shapes=[pltpu.VMEM((512, 1024), BF)],
-        compiler_params=PARAMS,
+        out_shape=[jax.ShapeDtypeStruct((2, U, 1024), BF)] * Z,
+        in_specs=[SMEM] + [VMEM] * 4,
+        out_specs=[VMEM] * Z,
+        scratch_shapes=[pltpu.VMEM((512, 1024), BF), pltpu.VMEM((Z, 2, U, 1024), BF)],
+        compiler_params=PARAMS,
+        cost_estimate=pl.CostEstimate(flops=2**30, bytes_accessed=2**22, transcendentals=0),
         name="slices",
-    )(x, comp_a, comp_b, perm)
-    slices = lax.all_to_all(slices.reshape(Z, 2 * U, 1024), "emb", 0, 0, tiled=True)
-    slices = slices.reshape(Z, 2, U, 1024)
-
-    gathered = ring(normed)
+    )(place, x, comp_a, comp_b, perm)
+    came = [slices[0]] + [None] * 7
+
+    def exchange(event, distances):
+        held, event = after([slices[k] for k in distances], event)
+        for k, v in zip(distances, held):
+            came[k] = lax.ppermute(v, "emb", [(i, (i + k) % Z) for i in range(Z)])
+        return event
+
+    def arrived(event, distances):
+        held, event = after([came[k] for k in distances], event)
+        for k, v in zip(distances, held):
+            came[k] = v
+        return event
+
+    up1, down1 = step(normed, normed)
+    up1, down1 = exchange((up1, down1), (1, 7))
+    up2, down2 = step(up1, down1)
+    up2, down2 = exchange((up2, down2), (2, 6))
+    up3, down3 = step(up2, down2)
+    up3, down3 = arrived((up3, down3), (1, 7))
+    up3, down3 = exchange((up3, down3), (3, 5))
+    low, high = step(up3[: U // 2], down3[U // 2 :])
+    low, high = arrived((low, high), (2, 6))
     hidden = pl.pallas_call(
         hidden_kernel,
         out_shape=jax.ShapeDtypeStruct((Z * U, 512), BF),
@@ -227,43 +268,59 @@
         scratch_shapes=[pltpu.VMEM((Z * U, N * K), BF)],
         compiler_params=PARAMS,
         name="hidden",
-    )(place, *gathered, w_hidden, w_hidden_other)
-
-    gathered = ring(hidden)
+    )(place, normed, up1, up2, up3, down1, down2, down3, low, high, w_hidden, w_hidden_other)
+
     users = Z * U
-    whole = [pl.BlockSpec(v.shape, lambda i, s: (0, 0)) for v in gathered]
-    s_own, s_other, t1, t2 = pl.pallas_call(
+    weights = w_own, w_other
+    up1, down1 = step(hidden, hidden)
+    sums = part(place, [(0, hidden)], weights, [])
+    (up1, down1), sums = after((up1, down1), sums)
+    up1, down1 = arrived((up1, down1), (3, 5))
+    up1, down1 = exchange((up1, down1), (4,))
+    up2, down2 = step(up1, down1)
+    sums = part(place, [(7, up1), (1, down1)], weights, sums)
+    (up2, down2), sums = after((up2, down2), sums)
+    up3, down3 = step(up2, down2)
+    sums = part(place, [(6, up2), (2, down2)], weights, sums)
+    (up3, down3), sums = after((up3, down3), sums)
+    up3, down3 = arrived((up3, down3), (4,))
+    low, high = step(up3[: users // 2], down3[users // 2 :])
+    sums = part(place, [(5, up3), (3, down3)], weights, sums)
+    slices = came
+
+    def all_of(*shape):
+        return pl.BlockSpec(shape, lambda i, at: (0,) * len(shape))
+
+    column = pl.BlockSpec((512, 512), lambda i, at: (0, lax.rem(at[0] + 4, Z)))
+    s_own, s_other, totals = pl.pallas_call(
         out_kernel,
         grid_spec=pltpu.PrefetchScalarGridSpec(
             num_scalar_prefetch=1,
-            grid=(4,),
-            in_specs=whole
-            + [pl.BlockSpec((128, 4096), lambda i, s: (i, 0))] * 2
-            + [
-                pl.BlockSpec((Z, 1, U, 128), lambda i, s: (0, s[1], 0, i)),
-                pl.BlockSpec((Z, 1, U, 128), lambda i, s: (0, 1 - s[1], 0, i)),
-            ],
-            out_specs=[pl.BlockSpec((users, 128), lambda i, s: (0, i))] * 2
-            + [pl.BlockSpec((8, users), lambda i, s: (i, 0))] * 2,
+            grid=(1,),
+            in_specs=[all_of(users // 2, 512)] * 2
+            + [column] * 2
+            + [all_of(users, 512)] * 2
+            + [all_of(2, U, 1024)] * Z,
+            out_specs=[all_of(users, 512)] * 2 + [all_of(64, users)],
         ),
         out_shape=[jax.ShapeDtypeStruct((users, 512), F32)] * 2
-        + [jax.ShapeDtypeStruct((32, users), F32)] * 2,
+        + [jax.ShapeDtypeStruct((64, users), F32)],
         compiler_params=PARAMS,
         name="fm_out",
-    )(place, *gathered, w_own, w_other, slices, slices)
-
-    totals = jnp.concatenate([t1, t2], axis=0)
+    )(place, low, high, *weights, *sums, *slices)
+
     for bit in (1, 2, 4):
-        totals = totals + lax.ppermute(totals, "emb", [(i, i ^ bit) for i in range(Z)])
+        theirs = lax.ppermute(totals.astype(BF), "emb", [(i, i ^ bit) for i in range(Z)])
+        totals = totals + theirs.astype(F32)
 
     o_own, o_other = pl.pallas_call(
         scale_kernel,
         out_shape=[jax.ShapeDtypeStruct((users, 1024), BF)] * 2,
-        in_specs=[SMEM] + [VMEM] * 4,
+        in_specs=[SMEM] + [VMEM] * (3 + Z),
         out_specs=[VMEM] * 2,
         compiler_params=PARAMS,
         name="scale",
-    )(place, s_own, s_other, totals, slices)
+    )(place, s_own, s_other, totals, *slices)
     came = lax.ppermute(o_other, "section", SWAP)
     o_own, came = o_own.reshape(Z, 1, U, 1024), came.reshape(Z, 1, U, 1024)
     send = jnp.where(

time: 192 us -> 173 us (0.901)
  waiting for transfers between devices: 91.7 us -> 66.3 us
  starting transfers between devices: 63.6 us -> 69.9 us
    ppermute x19 -> x26, waiting for transfers between devices: 57.3 us -> 32.6 us  [the longest x16 13.2 us: step(): return (lax.ppermute(up, 'emb', UP), lax.ppermute(down, 'emb', DOWN))]
    ppermute x19 -> x26, starting transfers between devices: 30 us -> 41.9 us  [the longest x16 25.8 us: step(): return (lax.ppermute(up, 'emb', UP), lax.ppermute(down, 'emb', DOWN))]
    pallas_call x1 -> x5, Pallas kernels: 1.39 us -> 12.6 us  [the longest x4 10.6 us: part(): pl.pallas_call(functools.partial(part_kernel, n), grid_spec=pltpu.Prefetc...]
    pallas_call x1, Pallas kernels: 13 us -> 3.08 us  [shards(): pl.pallas_call(out_kernel, grid_spec=pltpu.PrefetchScalarGridSpec(num_sca...]
    all_to_all x1 -> x0, starting transfers between devices: 8.19 us -> none  [shards(): lax.all_to_all(slices.reshape(Z, 2 * U, 1024), 'emb', 0, 0, tiled=True)]
    ppermute x1, starting transfers between devices: 13 us -> 15.1 us  [shards(): came = lax.ppermute(o_other, 'section', SWAP)]
  transfers between devices with their start and end apart: 25 -> 31, of which waited for: 14 -> 21; matrix products, arithmetic and copies ran while one was open for 6% -> 6% of each run, Pallas kernels for 4% -> 11%
where the time goes in v2:
time: 173 us; the launch traced here: 172 us
  starting transfers between devices  69.9 us (40%)
  waiting for transfers between devices  66.3 us (38%)
  Pallas kernels  24.2 us (14%)
  matrix products  5.23 us (3%)
  local copies, waits for them, and re-layouts  3.61 us (2%)
  other arithmetic  2.87 us (2%)
    ppermute x16, starting transfers between devices, step(): return (lax.ppermute(up, 'emb', UP), lax.ppermute(down, 'emb', DOWN))  25.8 us
    all_to_all x1, waiting for transfers between devices, shards(): x = lax.all_to_all(chunks, 'dp', 0, 0, tiled=True).reshape(N * U, D)  16.1 us
    all_to_all x1, waiting for transfers between devices, shards(): out = lax.all_to_all(send.reshape(16, U, 1024), 'dp', 0, 0, tiled=True)  16 us
    ppermute x1, starting transfers between devices, shards(): came = lax.ppermute(o_other, 'section', SWAP)  15.1 us
    ppermute x16, waiting for transfers between devices, step(): return (lax.ppermute(up, 'emb', UP), lax.ppermute(down, 'emb', DOWN))  13.2 us
    ppermute x7, starting transfers between devices, exchange(): came[k] = lax.ppermute(v, 'emb', [(i, (i + k) % Z) for i in range(Z)])  11.7 us
    pallas_call x4, Pallas kernels, part(): pl.pallas_call(functools.partial(part_kernel, n), grid_spec=pltpu.Prefetc...  10.6 us
    ppermute x3, waiting for transfers between devices, shards(): lax.ppermute(totals.astype(BF), 'emb', [(i, i ^ bit) for i in range(Z)])  9.78 us
  transfers between devices with their start and end apart: 31, of which 21 were waited for; matrix products, arithmetic and copies ran while one was open for 6% of the time, Pallas kernels for 11%

profile of v2, /device:TPU:1, one launch (start us, length us, event | category | flops | bytes accessed | tf_op | source)
XLA Modules:
  0.0 172.4 jit_solution(9994767729963241632)
XLA Ops:
  0.0 3.2 %collective-permute-start.17 = (bf16[512,4096]{1,0:T(8,128)(2,1)}, bf16[512,4096]{1,0:T(8,128)(2,1)}, u32[]{:S(2)}, u32[]{:S(2)}) collective-permute-start(bf16[512,4096]{1,0:T(8,128)(2,1)} %bitcast.34), channel_id=1, source_target_pairs={{0,1},{1,0},{2,3},{3,2},{4,5},{5,4},{6,7},{7,6},{8,9},{9,8},{10,11... | collective-permute-start | bytes 12582920 | tf_op jit(solution)/shard_map/ppermute | solution.py:203
  4.8 1.3 fusion.6
  6.2 4.7 %fusion.1 = f32[512,4,1,256]{3,2,1,0:T(1,128)S(1)} fusion(bf16[512,4,4,256]{3,2,1,0:T(4,128)(2,1)} %param.10, pred[512,4,4,1]{2,1,0,3:T(4,128)(4,1)S(1)} %fusion.6), kind=kOutput, calls=%fused_computation.2 | convolution fusion | flops 4194304 | bytes 6299648 | tf_op jit(solution)/shard_map/usj,usjd->usd/dot_general | solution.py:206
  12.5 5.2 %all-to-all-start = ((bf16[16,4,32,256]{3,2,1,0:T(8,128)(2,1)}), bf16[16,4,32,256]{3,2,1,0:T(8,128)(2,1)S(1)}, u32[]{:S(2)}, u32[]{:S(2)}) async-start(bf16[16,4,32,256]{3,2,1,0:T(8,128)(2,1)} %bitcast.33), calls=%async_computation | async-start | bytes 2097152 | tf_op jit(solution)/shard_map/all_to_all | solution.py:212
  18.9 16.1 %all-to-all-done = bf16[16,4,32,256]{3,2,1,0:T(8,128)(2,1)S(1)} async-done(((bf16[16,4,32,256]{3,2,1,0:T(8,128)(2,1)}), bf16[16,4,32,256]{3,2,1,0:T(8,128)(2,1)S(1)}, u32[]{:S(2)}, u32[]{:S(2)}) %all-to-all-start) | async-done | bytes 1048608 | tf_op jit(solution)/shard_map/all_to_all | solution.py:212
  35.0 3.6 %fm_rows.1 = (bf16[32,2048]{1,0:T(8,128)(2,1)S(1)}, f32[1024,128]{1,0:T(8,128)S(1)}, f32[1024,128]{1,0:T(8,128)S(1)}) custom-call(bf16[2048,256]{1,0:T(8,128)(2,1)S(1)} %bitcast.43, bf16[64,64]{1,0:T(8,128)(2,1)S(1)} %copy.20.mix_ref, f32[16,128]{1,0:T(8,128)S(1)} %bitcast.47), custom_call_target="tpu_custom_call" | custom-call | tf_op jit(solution)/shard_map/fm_rows/pallas_call | solution.py:216
  38.6 1.7 collective-permute-start
  40.3 4.0 %collective-permute-start.1 = (bf16[32,2048]{1,0:T(8,128)(2,1)S(1)}, bf16[32,2048]{1,0:T(8,128)(2,1)S(1)}, u32[]{:S(2)}, u32[]{:S(2)}) collective-permute-start(bf16[32,2048]{1,0:T(8,128)(2,1)S(1)} %get-tuple-element.78.refs_0_), channel_id=1, source_target_pairs={{0,14},{2,0},{4,2},{6,4},{8,6},{10,8},{12,10},{14,12},{1,15},{3,1}... | collective-permute-start | bytes 393224 | tf_op jit(solution)/shard_map/ppermute | solution.py:188
  44.4 2.0 %slices.1 = (bf16[2,32,1024]{2,1,0:T(8,128)(2,1)S(1)}, bf16[2,32,1024]{2,1,0:T(8,128)(2,1)S(1)}, bf16[2,32,1024]{2,1,0:T(8,128)(2,1)S(1)}, bf16[2,32,1024]{2,1,0...) custom-call(s32[2]{0:T(128)S(1)} %pad_add_fusion.at_ref, ...), custom_call_target="tpu_custom_call" | custom-call | flops 1073741824 | bytes 4194304 | tf_op jit(solution)/shard_map/slices/pallas_call | solution.py:230
  46.7 2.7 %collective-permute-start.5 = (bf16[32,2048]{1,0:T(8,128)(2,1)S(1)}, bf16[32,2048]{1,0:T(8,128)(2,1)S(1)}, u32[]{:S(2)}, u32[]{:S(2)}) collective-permute-start(bf16[32,2048]{1,0:T(8,128)(2,1)S(1)} %collective-permute-done.1.refs_4_), channel_id=1, source_target_pairs={{0,14},{2,0},{4,2},{6,4},{8,6},{10,8},{12,10},{14,12},{1,15},{3,1}... | collective-permute-start | bytes 393224 | tf_op jit(solution)/shard_map/ppermute | solution.py:188
  49.4 2.3 %collective-permute-done.4.refs_2_ = bf16[32,2048]{1,0:T(8,128)(2,1)S(1)} collective-permute-done((bf16[32,2048]{1,0:T(8,128)(2,1)S(1)}, bf16[32,2048]{1,0:T(8,128)(2,1)S(1)}, u32[]{:S(2)}, u32[]{:S(2)}) %collective-permute-start.4) | collective-permute-done | bytes 131104 | tf_op jit(solution)/shard_map/ppermute | solution.py:188
  51.7 1.4 collective-permute-start.3
  54.1 1.8 %collective-permute-done.2.refs_1_ = bf16[2,32,1024]{2,1,0:T(8,128)(2,1)S(1)} collective-permute-done((bf16[2,32,1024]{2,1,0:T(8,128)(2,1)S(1)}, bf16[2,32,1024]{2,1,0:T(8,128)(2,1)S(1)}, u32[]{:S(2)}, u32[]{:S(2)}) %collective-permute-start.2) | collective-permute-done | bytes 131104 | tf_op jit(solution)/shard_map/ppermute | solution.py:245
  56.0 1.7 collective-permute-start.10
  57.7 1.5 collective-permute-done.6.refs_3_
  61.2 1.1 collective-permute-done.10.refs_2_
  62.3 3.8 %collective-permute-start.13 = (bf16[16,2048]{1,0:T(8,128)(2,1)S(1)}, bf16[16,2048]{1,0:T(8,128)(2,1)S(1)}, u32[]{:S(2)}, u32[]{:S(2)}) collective-permute-start(bf16[16,2048]{1,0:T(8,128)(2,1)S(1)} %slice.13), channel_id=1, source_target_pairs={{0,14},{2,0},{4,2},{6,4},{8,6},{10,8},{12,10},{14,12},{1,15},{3,1}... | collective-permute-start | bytes 196616 | tf_op jit(solution)/shard_map/ppermute | solution.py:188
  66.1 2.9 %collective-permute-done.13.refs_8_ = bf16[16,2048]{1,0:T(8,128)(2,1)S(1)} collective-permute-done((bf16[16,2048]{1,0:T(8,128)(2,1)S(1)}, bf16[16,2048]{1,0:T(8,128)(2,1)S(1)}, u32[]{:S(2)}, u32[]{:S(2)}) %collective-permute-start.13) | collective-permute-done | bytes 65568 | tf_op jit(solution)/shard_map/ppermute | solution.py:188
  69.0 2.3 %hidden.1.refs_0_ = bf16[256,512]{1,0:T(8,128)(2,1)S(1)} custom-call(s32[2]{0:T(128)S(1)} %pad_add_fusion.at_ref, bf16[32,2048]{1,0:T(8,128)(2,1)S(1)} %get-tuple-element.78.refs_0_, bf16[32,2048]{1,0:T(8,128)(2,1)S(1)} %collective-permute-done.refs_1_, bf16[32,2048]{1,0:T(8,128)(2,1)S(1)} %collective-permute-done.4.refs_2_, ...), custom_call_target="tpu_custom_call" | custom-call | tf_op jit(solution)/shard_map/hidden/pallas_call | solution.py:263
  71.4 3.3 %collective-permute-start.16 = (bf16[256,512]{1,0:T(8,128)(2,1)S(1)}, bf16[256,512]{1,0:T(8,128)(2,1)S(1)}, u32[]{:S(2)}, u32[]{:S(2)}) collective-permute-start(bf16[256,512]{1,0:T(8,128)(2,1)S(1)} %hidden.1.refs_0_), channel_id=1, source_target_pairs={{0,14},{2,0},{4,2},{6,4},{8,6},{10,8},{12,10},{14,12},{1,15},{3,1}... | collective-permute-start | bytes 786440 | tf_op jit(solution)/shard_map/ppermute | solution.py:188
  74.7 4.5 %collective-permute-start.9 = (bf16[2,32,1024]{2,1,0:T(8,128)(2,1)S(1)}, bf16[2,32,1024]{2,1,0:T(8,128)(2,1)S(1)}, u32[]{:S(2)}, u32[]{:S(2)}) collective-permute-start(bf16[2,32,1024]{2,1,0:T(8,128)(2,1)S(1)} %get-tuple-element.90), channel_id=1, source_target_pairs={{0,10},{2,12},{4,14},{6,0},{8,2},{10,4},{12,6},{14,8},{1,11},{3,13... | collective-permute-start | bytes 393224 | tf_op jit(solution)/shard_map/ppermute | solution.py:245
  79.2 2.1 %fm_out_part.4 = (f32[256,512]{1,0:T(8,128)S(1)}, f32[256,512]{1,0:T(8,128)S(1)}) custom-call(s32[2]{0:T(128)S(1)} %pad_add_fusion.at_ref, bf16[256,512]{1,0:T(8,128)(2,1)S(1)} %hidden.1.refs_0_, bf16[512,4096]{1,0:T(8,128)(2,1)S(1)} %bitcast.42, bf16[512,4096]{1,0:T(8,128)(2,1)} %collective-permute-done.17.refs_2_.refs_3_.refs_5_.w_other), custom_call_target="tpu_custom_call" | custom-call | flops 268435456 | bytes 1048576 | tf_op jit(solution)/shard_map/fm_out_part/pallas_call | solution.py:115
  81.3 4.3 %collective-permute-done.8.refs_3_ = bf16[2,32,1024]{2,1,0:T(8,128)(2,1)S(1)} collective-permute-done((bf16[2,32,1024]{2,1,0:T(8,128)(2,1)S(1)}, bf16[2,32,1024]{2,1,0:T(8,128)(2,1)S(1)}, u32[]{:S(2)}, u32[]{:S(2)}) %collective-permute-start.8) | collective-permute-done | bytes 131104 | tf_op jit(solution)/shard_map/ppermute | solution.py:245
  85.6 2.7 %collective-permute-start.20 = (bf16[256,512]{1,0:T(8,128)(2,1)S(1)}, bf16[256,512]{1,0:T(8,128)(2,1)S(1)}, u32[]{:S(2)}, u32[]{:S(2)}) collective-permute-start(bf16[256,512]{1,0:T(8,128)(2,1)S(1)} %collective-permute-done.16.refs_1_), channel_id=1, source_target_pairs={{0,14},{2,0},{4,2},{6,4},{8,6},{10,8},{12,10},{14,12},{1,15},{3,1}... | collective-permute-start | bytes 786440 | tf_op jit(solution)/shard_map/ppermute | solution.py:188
  88.3 2.9 %fm_out_part.5 = (f32[256,512]{1,0:T(8,128)S(1)}, f32[256,512]{1,0:T(8,128)S(1)}) custom-call(s32[2]{0:T(128)S(1)} %pad_add_fusion.at_ref, bf16[256,512]{1,0:T(8,128)(2,1)S(1)} %collective-permute-done.15.refs_0_, bf16[256,512]{1,0:T(8,128)(2,1)S(1)} %collective-permute-done.16.refs_1_, bf16[512,4096]{1,0:T(8,128)(2,1)} %bitcast.35, ...), custom_call_target="tpu_custom_call" | custom-call | flops 536870912 | bytes 2097152 | tf_op jit(solution)/shard_map/fm_out_part/pallas_call | solution.py:115
  91.2 2.0 %collective-permute-done.19.refs_0_ = bf16[256,512]{1,0:T(8,128)(2,1)S(1)} collective-permute-done((bf16[256,512]{1,0:T(8,128)(2,1)S(1)}, bf16[256,512]{1,0:T(8,128)(2,1)S(1)}, u32[]{:S(2)}, u32[]{:S(2)}) %collective-permute-start.19) | collective-permute-done | bytes 262176 | tf_op jit(solution)/shard_map/ppermute | solution.py:188
  93.9 2.2 %collective-permute-start.22 = (bf16[256,512]{1,0:T(8,128)(2,1)S(1)}, bf16[256,512]{1,0:T(8,128)(2,1)S(1)}, u32[]{:S(2)}, u32[]{:S(2)}) collective-permute-start(bf16[256,512]{1,0:T(8,128)(2,1)S(1)} %collective-permute-done.20.refs_1_), channel_id=1, source_target_pairs={{0,14},{2,0},{4,2},{6,4},{8,6},{10,8},{12,10},{14,12},{1,15},{3,1}... | collective-permute-start | bytes 786440 | tf_op jit(solution)/shard_map/ppermute | solution.py:188
  96.1 3.2 %collective-permute-start.18 = (bf16[2,32,1024]{2,1,0:T(8,128)(2,1)S(1)}, bf16[2,32,1024]{2,1,0:T(8,128)(2,1)S(1)}, u32[]{:S(2)}, u32[]{:S(2)}) collective-permute-start(bf16[2,32,1024]{2,1,0:T(8,128)(2,1)S(1)} %get-tuple-element.103), channel_id=1, source_target_pairs={{0,8},{2,10},{4,12},{6,14},{8,0},{10,2},{12,4},{14,6},{1,9},{3,11}... | collective-permute-start | bytes 393224 | tf_op jit(solution)/shard_map/ppermute | solution.py:245
  99.2 2.8 %fm_out_part.6 = (f32[256,512]{1,0:T(8,128)S(1)}, f32[256,512]{1,0:T(8,128)S(1)}) custom-call(s32[2]{0:T(128)S(1)} %pad_add_fusion.at_ref, bf16[256,512]{1,0:T(8,128)(2,1)S(1)} %collective-permute-done.19.refs_0_, bf16[256,512]{1,0:T(8,128)(2,1)S(1)} %collective-permute-done.20.refs_1_, bf16[512,4096]{1,0:T(8,128)(2,1)} %bitcast.37, ...), custom_call_target="tpu_custom_call" | custom-call | flops 536870912 | bytes 2097152 | tf_op jit(solution)/shard_map/fm_out_part/pallas_call | solution.py:115
  102.1 1.2 collective-permute-done.21.refs_0_
  103.3 1.2 collective-permute-done.22.refs_1_
  104.6 2.3 %collective-permute-done.18.refs_4_ = bf16[2,32,1024]{2,1,0:T(8,128)(2,1)S(1)} collective-permute-done((bf16[2,32,1024]{2,1,0:T(8,128)(2,1)S(1)}, bf16[2,32,1024]{2,1,0:T(8,128)(2,1)S(1)}, u32[]{:S(2)}, u32[]{:S(2)}) %collective-permute-start.18) | collective-permute-done | bytes 131104 | tf_op jit(solution)/shard_map/ppermute | solution.py:245
  106.9 1.5 collective-permute-start.23
  108.5 1.3 collective-permute-start.24
  109.8 2.8 %fm_out_part.7 = (f32[256,512]{1,0:T(8,128)S(1)}, f32[256,512]{1,0:T(8,128)S(1)}) custom-call(s32[2]{0:T(128)S(1)} %pad_add_fusion.at_ref, bf16[256,512]{1,0:T(8,128)(2,1)S(1)} %collective-permute-done.21.refs_0_, bf16[256,512]{1,0:T(8,128)(2,1)S(1)} %collective-permute-done.22.refs_1_, bf16[512,4096]{1,0:T(8,128)(2,1)} %bitcast.39, ...), custom_call_target="tpu_custom_call" | custom-call | flops 536870912 | bytes 2097152 | tf_op jit(solution)/shard_map/fm_out_part/pallas_call | solution.py:115
  112.6 1.1 collective-permute-done.23.low
  114.1 3.1 %fm_out.1 = (f32[256,512]{1,0:T(8,128)S(1)}, f32[256,512]{1,0:T(8,128)S(1)}, f32[64,256]{1,0:T(8,128)S(1)}) custom-call(s32[2]{0:T(128)S(1)} %pad_add_fusion.at_ref, bf16[128,512]{1,0:T(8,128)(2,1)S(1)} %collective-permute-done.23.low, bf16[128,512]{1,0:T(8,128)(2,1)S(1)} %collective-permute-done.24.high, bf16[512,4096]{1,0:T(8,128)(2,1)} %bitcast.41, ...), custom_call_target="tpu_custom_call" | custom-call | tf_op jit(solution)/shard_map/fm_out/pallas_call | solution.py:295
  117.3 2.8 %collective-permute-done.25 = bf16[64,256]{1,0:T(8,128)(2,1)S(1)} collective-permute-done((bf16[64,256]{1,0:T(8,128)(2,1)S(1)}, bf16[64,256]{1,0:T(8,128)(2,1)S(1)}, u32[]{:S(2)}, u32[]{:S(2)}) %collective-permute-start.25) | collective-permute-done | bytes 32800 | tf_op jit(solution)/shard_map/ppermute | solution.py:313
  120.6 4.1 %collective-permute-done.26 = bf16[64,256]{1,0:T(8,128)(2,1)S(1)} collective-permute-done((bf16[64,256]{1,0:T(8,128)(2,1)S(1)}, bf16[64,256]{1,0:T(8,128)(2,1)S(1)}, u32[]{:S(2)}, u32[]{:S(2)}) %collective-permute-start.26) | collective-permute-done | bytes 32800 | tf_op jit(solution)/shard_map/ppermute | solution.py:313
  124.7 3.8 %collective-permute-start.27 = (bf16[64,256]{1,0:T(8,128)(2,1)S(1)}, bf16[64,256]{1,0:T(8,128)(2,1)S(1)}, u32[]{:S(2)}, u32[]{:S(2)}) collective-permute-start(bf16[64,256]{1,0:T(8,128)(2,1)S(1)} %fusion.9), channel_id=1, source_target_pairs={{0,8},{2,10},{4,12},{6,14},{8,0},{10,2},{12,4},{14,6},{1,9},{3,11}... | collective-permute-start | bytes 98312 | tf_op jit(solution)/shard_map/ppermute | solution.py:313
  128.5 2.9 %collective-permute-done.27 = bf16[64,256]{1,0:T(8,128)(2,1)S(1)} collective-permute-done((bf16[64,256]{1,0:T(8,128)(2,1)S(1)}, bf16[64,256]{1,0:T(8,128)(2,1)S(1)}, u32[]{:S(2)}, u32[]{:S(2)}) %collective-permute-start.27) | collective-permute-done | bytes 32800 | tf_op jit(solution)/shard_map/ppermute | solution.py:313
  131.5 1.1 scale.1
  132.6 15.1 %collective-permute-start.28 = (bf16[256,1024]{1,0:T(8,128)(2,1)S(1)}, bf16[256,1024]{1,0:T(8,128)(2,1)S(1)}, u32[]{:S(2)}, u32[]{:S(2)}) collective-permute-start(bf16[256,1024]{1,0:T(8,128)(2,1)S(1)} %get-tuple-element.136), channel_id=1, source_target_pairs={{0,1},{1,0},{2,3},{3,2},{4,5},{5,4},{6,7},{7,6},{8,9},{9,8},{10,11... | collective-permute-start | bytes 1572872 | tf_op jit(solution)/shard_map/ppermute | solution.py:324
  147.7 1.5 collective-permute-done.28
  149.4 1.1 copy.21
  150.5 4.1 %all-to-all-start.1 = ((bf16[16,32,1024]{2,1,0:T(8,128)(2,1)}), bf16[16,32,1024]{2,1,0:T(8,128)(2,1)S(1)}, u32[]{:S(2)}, u32[]{:S(2)}) async-start(bf16[16,32,1024]{2,1,0:T(8,128)(2,1)} %bitcast.18), calls=%async_computation.1 | async-start | bytes 2097152 | tf_op jit(solution)/shard_map/all_to_all | solution.py:329
  154.9 16.0 %all-to-all-done.1 = bf16[16,32,1024]{2,1,0:T(8,128)(2,1)S(1)} async-done(((bf16[16,32,1024]{2,1,0:T(8,128)(2,1)}), bf16[16,32,1024]{2,1,0:T(8,128)(2,1)S(1)}, u32[]{:S(2)}, u32[]{:S(2)}) %all-to-all-start.1) | async-done | bytes 1048608 | tf_op jit(solution)/shard_map/all_to_all | solution.py:329
  170.9 1.5 finish.1
  (62 shorter events, 10.2 us)
Async XLA Ops:
  0.0 10.9 %copy-start = (bf16[256,256]{1,0:T(8,128)(2,1)S(1)}, bf16[256,256]{1,0:T(8,128)(2,1)}, u32[]{:S(2)}) copy-start(bf16[256,256]{1,0:T(8,128)(2,1)} %param.13) | copy-start | bytes 393220
  0.0 79.2 %collective-permute-start.17 = (bf16[512,4096]{1,0:T(8,128)(2,1)}, bf16[512,4096]{1,0:T(8,128)(2,1)}, u32[]{:S(2)}, u32[]{:S(2)}) collective-permute-start(bf16[512,4096]{1,0:T(8,128)(2,1)} %bitcast.34), channel_id=1, source_target_pairs={{0,1},{1,0},{2,3},{3,2},{4,5},{5,4},{6,7},{7,6},{8,9},{9,8},{10,11... | collective-permute-start | bytes 12582920 | tf_op jit(solution)/shard_map/ppermute | solution.py:203
  11.4 6.7 %copy-start.3 = (bf16[64,32]{0,1:T(8,128)(2,1)S(1)}, bf16[64,32]{0,1:T(8,128)(2,1)}, u32[]{:S(2)}) copy-start(bf16[64,32]{0,1:T(8,128)(2,1)} %param.14) | copy-start | bytes 12292
  11.4 6.7 %copy-start.4 = (bf16[32,64]{1,0:T(8,128)(2,1)S(1)}, bf16[32,64]{1,0:T(8,128)(2,1)}, u32[]{:S(2)}) copy-start(bf16[32,64]{1,0:T(8,128)(2,1)} %param.18) | copy-start | bytes 12292
  12.5 22.5 %copy-start.2 = (f32[2048]{0:T(1024)S(1)}, f32[2048]{0:T(1024)}, u32[]{:S(2)}) copy-start(f32[2048]{0:T(1024)} %param.15) | copy-start | bytes 24580
  12.5 22.5 %all-to-all-start = ((bf16[16,4,32,256]{3,2,1,0:T(8,128)(2,1)}), bf16[16,4,32,256]{3,2,1,0:T(8,128)(2,1)S(1)}, u32[]{:S(2)}, u32[]{:S(2)}) async-start(bf16[16,4,32,256]{3,2,1,0:T(8,128)(2,1)} %bitcast.33), calls=%async_computation | async-start | bytes 2097152 | tf_op jit(solution)/shard_map/all_to_all | solution.py:212
  17.7 51.3 %collective-permute-start.14 = (bf16[2048,256]{1,0:T(8,128)(2,1)}, bf16[2048,256]{1,0:T(8,128)(2,1)}, u32[]{:S(2)}, u32[]{:S(2)}) collective-permute-start(bf16[2048,256]{1,0:T(8,128)(2,1)} %refs_9_.1), channel_id=1, source_target_pairs={{0,1},{1,0},{2,3},{3,2},{4,5},{5,4},{6,7},{7,6},{8,9},{9,8},{10,11... | collective-permute-start | bytes 3145736 | tf_op jit(solution)/shard_map/ppermute | solution.py:201
  38.6 8.0 %collective-permute-start = (bf16[32,2048]{1,0:T(8,128)(2,1)S(1)}, bf16[32,2048]{1,0:T(8,128)(2,1)S(1)}, u32[]{:S(2)}, u32[]{:S(2)}) collective-permute-start(bf16[32,2048]{1,0:T(8,128)(2,1)S(1)} %get-tuple-element.78.refs_0_), channel_id=1, source_target_pairs={{0,2},{2,4},{4,6},{6,8},{8,10},{10,12},{12,14},{14,0},{1,3},{3,5},... | collective-permute-start | bytes 393224 | tf_op jit(solution)/shard_map/ppermute | solution.py:188
  40.3 6.3 %collective-permute-start.1 = (bf16[32,2048]{1,0:T(8,128)(2,1)S(1)}, bf16[32,2048]{1,0:T(8,128)(2,1)S(1)}, u32[]{:S(2)}, u32[]{:S(2)}) collective-permute-start(bf16[32,2048]{1,0:T(8,128)(2,1)S(1)} %get-tuple-element.78.refs_0_), channel_id=1, source_target_pairs={{0,14},{2,0},{4,2},{6,4},{8,6},{10,8},{12,10},{14,12},{1,15},{3,1}... | collective-permute-start | bytes 393224 | tf_op jit(solution)/shard_map/ppermute | solution.py:188
  44.4 34.8 %copy-start.1 = (bf16[4096,32,16]{0,2,1:T(8,128)(2,1)S(1)}, bf16[4096,32,16]{0,2,1:T(8,128)(2,1)}, u32[]{:S(2)}) copy-start(bf16[4096,32,16]{0,2,1:T(8,128)(2,1)} %param.17) | copy-start | bytes 12582916
  46.6 5.1 %collective-permute-start.4 = (bf16[32,2048]{1,0:T(8,128)(2,1)S(1)}, bf16[32,2048]{1,0:T(8,128)(2,1)S(1)}, u32[]{:S(2)}, u32[]{:S(2)}) collective-permute-start(bf16[32,2048]{1,0:T(8,128)(2,1)S(1)} %collective-permute-done.refs_1_), channel_id=1, source_target_pairs={{0,2},{2,4},{4,6},{6,8},{8,10},{10,12},{12,14},{14,0},{1,3},{3,5},... | collective-permute-start | bytes 393224 | tf_op jit(solution)/shard_map/ppermute | solution.py:188
  46.7 6.5 %collective-permute-start.5 = (bf16[32,2048]{1,0:T(8,128)(2,1)S(1)}, bf16[32,2048]{1,0:T(8,128)(2,1)S(1)}, u32[]{:S(2)}, u32[]{:S(2)}) collective-permute-start(bf16[32,2048]{1,0:T(8,128)(2,1)S(1)} %collective-permute-done.1.refs_4_), channel_id=1, source_target_pairs={{0,14},{2,0},{4,2},{6,4},{8,6},{10,8},{12,10},{14,12},{1,15},{3,1}... | collective-permute-start | bytes 393224 | tf_op jit(solution)/shard_map/ppermute | solution.py:188
  49.4 6.6 %collective-permute-start.2 = (bf16[2,32,1024]{2,1,0:T(8,128)(2,1)S(1)}, bf16[2,32,1024]{2,1,0:T(8,128)(2,1)S(1)}, u32[]{:S(2)}, u32[]{:S(2)}) collective-permute-start(bf16[2,32,1024]{2,1,0:T(8,128)(2,1)S(1)} %get-tuple-element.79), channel_id=1, source_target_pairs={{0,2},{2,4},{4,6},{6,8},{8,10},{10,12},{12,14},{14,0},{1,3},{3,5},... | collective-permute-start | bytes 393224 | tf_op jit(solution)/shard_map/ppermute | solution.py:245
  51.7 4.3 %collective-permute-start.3 = (bf16[2,32,1024]{2,1,0:T(8,128)(2,1)S(1)}, bf16[2,32,1024]{2,1,0:T(8,128)(2,1)S(1)}, u32[]{:S(2)}, u32[]{:S(2)}) collective-permute-start(bf16[2,32,1024]{2,1,0:T(8,128)(2,1)S(1)} %get-tuple-element.80), channel_id=1, source_target_pairs={{0,14},{2,0},{4,2},{6,4},{8,6},{10,8},{12,10},{14,12},{1,15},{3,1}... | collective-permute-start | bytes 393224 | tf_op jit(solution)/shard_map/ppermute | solution.py:245
  53.2 6.0 %collective-permute-start.6 = (bf16[32,2048]{1,0:T(8,128)(2,1)S(1)}, bf16[32,2048]{1,0:T(8,128)(2,1)S(1)}, u32[]{:S(2)}, u32[]{:S(2)}) collective-permute-start(bf16[32,2048]{1,0:T(8,128)(2,1)S(1)} %collective-permute-done.4.refs_2_), channel_id=1, source_target_pairs={{0,2},{2,4},{4,6},{6,8},{8,10},{10,12},{12,14},{14,0},{1,3},{3,5},... | collective-permute-start | bytes 393224 | tf_op jit(solution)/shard_map/ppermute | solution.py:188
  55.9 4.5 %collective-permute-start.7 = (bf16[32,2048]{1,0:T(8,128)(2,1)S(1)}, bf16[32,2048]{1,0:T(8,128)(2,1)S(1)}, u32[]{:S(2)}, u32[]{:S(2)}) collective-permute-start(bf16[32,2048]{1,0:T(8,128)(2,1)S(1)} %collective-permute-done.5.refs_5_), channel_id=1, source_target_pairs={{0,14},{2,0},{4,2},{6,4},{8,6},{10,8},{12,10},{14,12},{1,15},{3,1}... | collective-permute-start | bytes 393224 | tf_op jit(solution)/shard_map/ppermute | solution.py:188
  56.0 6.3 %collective-permute-start.10 = (bf16[2,32,1024]{2,1,0:T(8,128)(2,1)S(1)}, bf16[2,32,1024]{2,1,0:T(8,128)(2,1)S(1)}, u32[]{:S(2)}, u32[]{:S(2)}) collective-permute-start(bf16[2,32,1024]{2,1,0:T(8,128)(2,1)S(1)} %get-tuple-element.93), channel_id=1, source_target_pairs={{0,4},{2,6},{4,8},{6,10},{8,12},{10,14},{12,0},{14,2},{1,5},{3,7},... | collective-permute-start | bytes 393224 | tf_op jit(solution)/shard_map/ppermute | solution.py:245
  59.2 6.9 %collective-permute-start.11 = (bf16[2,32,1024]{2,1,0:T(8,128)(2,1)S(1)}, bf16[2,32,1024]{2,1,0:T(8,128)(2,1)S(1)}, u32[]{:S(2)}, u32[]{:S(2)}) collective-permute-start(bf16[2,32,1024]{2,1,0:T(8,128)(2,1)S(1)} %get-tuple-element.94), channel_id=1, source_target_pairs={{0,12},{2,14},{4,0},{6,2},{8,4},{10,6},{12,8},{14,10},{1,13},{3,15... | collective-permute-start | bytes 393224 | tf_op jit(solution)/shard_map/ppermute | solution.py:245
  60.4 5.7 %collective-permute-start.12 = (bf16[16,2048]{1,0:T(8,128)(2,1)S(1)}, bf16[16,2048]{1,0:T(8,128)(2,1)S(1)}, u32[]{:S(2)}, u32[]{:S(2)}) collective-permute-start(bf16[16,2048]{1,0:T(8,128)(2,1)S(1)} %slice.12), channel_id=1, source_target_pairs={{0,2},{2,4},{4,6},{6,8},{8,10},{10,12},{12,14},{14,0},{1,3},{3,5},... | collective-permute-start | bytes 196616 | tf_op jit(solution)/shard_map/ppermute | solution.py:188
  62.3 6.7 %collective-permute-start.13 = (bf16[16,2048]{1,0:T(8,128)(2,1)S(1)}, bf16[16,2048]{1,0:T(8,128)(2,1)S(1)}, u32[]{:S(2)}, u32[]{:S(2)}) collective-permute-start(bf16[16,2048]{1,0:T(8,128)(2,1)S(1)} %slice.13), channel_id=1, source_target_pairs={{0,14},{2,0},{4,2},{6,4},{8,6},{10,8},{12,10},{14,12},{1,15},{3,1}... | collective-permute-start | bytes 196616 | tf_op jit(solution)/shard_map/ppermute | solution.py:188
  71.3 10.0 %collective-permute-start.15 = (bf16[256,512]{1,0:T(8,128)(2,1)S(1)}, bf16[256,512]{1,0:T(8,128)(2,1)S(1)}, u32[]{:S(2)}, u32[]{:S(2)}) collective-permute-start(bf16[256,512]{1,0:T(8,128)(2,1)S(1)} %hidden.1.refs_0_), channel_id=1, source_target_pairs={{0,2},{2,4},{4,6},{6,8},{8,10},{10,12},{12,14},{14,0},{1,3},{3,5},... | collective-permute-start | bytes 786440 | tf_op jit(solution)/shard_map/ppermute | solution.py:188
  71.4 9.9 %collective-permute-start.16 = (bf16[256,512]{1,0:T(8,128)(2,1)S(1)}, bf16[256,512]{1,0:T(8,128)(2,1)S(1)}, u32[]{:S(2)}, u32[]{:S(2)}) collective-permute-start(bf16[256,512]{1,0:T(8,128)(2,1)S(1)} %hidden.1.refs_0_), channel_id=1, source_target_pairs={{0,14},{2,0},{4,2},{6,4},{8,6},{10,8},{12,10},{14,12},{1,15},{3,1}... | collective-permute-start | bytes 786440 | tf_op jit(solution)/shard_map/ppermute | solution.py:188
  74.7 10.9 %collective-permute-start.8 = (bf16[2,32,1024]{2,1,0:T(8,128)(2,1)S(1)}, bf16[2,32,1024]{2,1,0:T(8,128)(2,1)S(1)}, u32[]{:S(2)}, u32[]{:S(2)}) collective-permute-start(bf16[2,32,1024]{2,1,0:T(8,128)(2,1)S(1)} %get-tuple-element.89), channel_id=1, source_target_pairs={{0,6},{2,8},{4,10},{6,12},{8,14},{10,0},{12,2},{14,4},{1,7},{3,9},... | collective-permute-start | bytes 393224 | tf_op jit(solution)/shard_map/ppermute | solution.py:245
  74.7 10.9 %collective-permute-start.9 = (bf16[2,32,1024]{2,1,0:T(8,128)(2,1)S(1)}, bf16[2,32,1024]{2,1,0:T(8,128)(2,1)S(1)}, u32[]{:S(2)}, u32[]{:S(2)}) collective-permute-start(bf16[2,32,1024]{2,1,0:T(8,128)(2,1)S(1)} %get-tuple-element.90), channel_id=1, source_target_pairs={{0,10},{2,12},{4,14},{6,0},{8,2},{10,4},{12,6},{14,8},{1,11},{3,13... | collective-permute-start | bytes 393224 | tf_op jit(solution)/shard_map/ppermute | solution.py:245
  85.6 7.5 %collective-permute-start.19 = (bf16[256,512]{1,0:T(8,128)(2,1)S(1)}, bf16[256,512]{1,0:T(8,128)(2,1)S(1)}, u32[]{:S(2)}, u32[]{:S(2)}) collective-permute-start(bf16[256,512]{1,0:T(8,128)(2,1)S(1)} %collective-permute-done.15.refs_0_), channel_id=1, source_target_pairs={{0,2},{2,4},{4,6},{6,8},{8,10},{10,12},{12,14},{14,0},{1,3},{3,5},... | collective-permute-start | bytes 786440 | tf_op jit(solution)/shard_map/ppermute | solution.py:188
  85.6 7.5 %collective-permute-start.20 = (bf16[256,512]{1,0:T(8,128)(2,1)S(1)}, bf16[256,512]{1,0:T(8,128)(2,1)S(1)}, u32[]{:S(2)}, u32[]{:S(2)}) collective-permute-start(bf16[256,512]{1,0:T(8,128)(2,1)S(1)} %collective-permute-done.16.refs_1_), channel_id=1, source_target_pairs={{0,14},{2,0},{4,2},{6,4},{8,6},{10,8},{12,10},{14,12},{1,15},{3,1}... | collective-permute-start | bytes 786440 | tf_op jit(solution)/shard_map/ppermute | solution.py:188
  93.1 10.2 %collective-permute-start.21 = (bf16[256,512]{1,0:T(8,128)(2,1)S(1)}, bf16[256,512]{1,0:T(8,128)(2,1)S(1)}, u32[]{:S(2)}, u32[]{:S(2)}) collective-permute-start(bf16[256,512]{1,0:T(8,128)(2,1)S(1)} %collective-permute-done.19.refs_0_), channel_id=1, source_target_pairs={{0,2},{2,4},{4,6},{6,8},{8,10},{10,12},{12,14},{14,0},{1,3},{3,5},... | collective-permute-start | bytes 786440 | tf_op jit(solution)/shard_map/ppermute | solution.py:188
  93.9 10.7 %collective-permute-start.22 = (bf16[256,512]{1,0:T(8,128)(2,1)S(1)}, bf16[256,512]{1,0:T(8,128)(2,1)S(1)}, u32[]{:S(2)}, u32[]{:S(2)}) collective-permute-start(bf16[256,512]{1,0:T(8,128)(2,1)S(1)} %collective-permute-done.20.refs_1_), channel_id=1, source_target_pairs={{0,14},{2,0},{4,2},{6,4},{8,6},{10,8},{12,10},{14,12},{1,15},{3,1}... | collective-permute-start | bytes 786440 | tf_op jit(solution)/shard_map/ppermute | solution.py:188
  96.1 10.8 %collective-permute-start.18 = (bf16[2,32,1024]{2,1,0:T(8,128)(2,1)S(1)}, bf16[2,32,1024]{2,1,0:T(8,128)(2,1)S(1)}, u32[]{:S(2)}, u32[]{:S(2)}) collective-permute-start(bf16[2,32,1024]{2,1,0:T(8,128)(2,1)S(1)} %get-tuple-element.103), channel_id=1, source_target_pairs={{0,8},{2,10},{4,12},{6,14},{8,0},{10,2},{12,4},{14,6},{1,9},{3,11}... | collective-permute-start | bytes 393224 | tf_op jit(solution)/shard_map/ppermute | solution.py:245
  106.9 6.8 %collective-permute-start.23 = (bf16[128,512]{1,0:T(8,128)(2,1)S(1)}, bf16[128,512]{1,0:T(8,128)(2,1)S(1)}, u32[]{:S(2)}, u32[]{:S(2)}) collective-permute-start(bf16[128,512]{1,0:T(8,128)(2,1)S(1)} %slice.14), channel_id=1, source_target_pairs={{0,2},{2,4},{4,6},{6,8},{8,10},{10,12},{12,14},{14,0},{1,3},{3,5},... | collective-permute-start | bytes 393224 | tf_op jit(solution)/shard_map/ppermute | solution.py:188
  108.5 5.7 %collective-permute-start.24 = (bf16[128,512]{1,0:T(8,128)(2,1)S(1)}, bf16[128,512]{1,0:T(8,128)(2,1)S(1)}, u32[]{:S(2)}, u32[]{:S(2)}) collective-permute-start(bf16[128,512]{1,0:T(8,128)(2,1)S(1)} %slice.15), channel_id=1, source_target_pairs={{0,14},{2,0},{4,2},{6,4},{8,6},{10,8},{12,10},{14,12},{1,15},{3,1}... | collective-permute-start | bytes 393224 | tf_op jit(solution)/shard_map/ppermute | solution.py:188
  117.2 2.9 %collective-permute-start.25 = (bf16[64,256]{1,0:T(8,128)(2,1)S(1)}, bf16[64,256]{1,0:T(8,128)(2,1)S(1)}, u32[]{:S(2)}, u32[]{:S(2)}) collective-permute-start(bf16[64,256]{1,0:T(8,128)(2,1)S(1)} %convert_element_type.39), channel_id=1, source_target_pairs={{0,2},{2,0},{4,6},{6,4},{8,10},{10,8},{12,14},{14,12},{1,3},{3,1},... | collective-permute-start | bytes 98312 | tf_op jit(solution)/shard_map/ppermute | solution.py:313
  120.1 4.6 %collective-permute-start.26 = (bf16[64,256]{1,0:T(8,128)(2,1)S(1)}, bf16[64,256]{1,0:T(8,128)(2,1)S(1)}, u32[]{:S(2)}, u32[]{:S(2)}) collective-permute-start(bf16[64,256]{1,0:T(8,128)(2,1)S(1)} %fusion.8), channel_id=1, source_target_pairs={{0,4},{2,6},{4,0},{6,2},{8,12},{10,14},{12,8},{14,10},{1,5},{3,7},... | collective-permute-start | bytes 98312 | tf_op jit(solution)/shard_map/ppermute | solution.py:313
  124.7 6.8 %collective-permute-start.27 = (bf16[64,256]{1,0:T(8,128)(2,1)S(1)}, bf16[64,256]{1,0:T(8,128)(2,1)S(1)}, u32[]{:S(2)}, u32[]{:S(2)}) collective-permute-start(bf16[64,256]{1,0:T(8,128)(2,1)S(1)} %fusion.9), channel_id=1, source_target_pairs={{0,8},{2,10},{4,12},{6,14},{8,0},{10,2},{12,4},{14,6},{1,9},{3,11}... | collective-permute-start | bytes 98312 | tf_op jit(solution)/shard_map/ppermute | solution.py:313
  132.6 16.6 %collective-permute-start.28 = (bf16[256,1024]{1,0:T(8,128)(2,1)S(1)}, bf16[256,1024]{1,0:T(8,128)(2,1)S(1)}, u32[]{:S(2)}, u32[]{:S(2)}) collective-permute-start(bf16[256,1024]{1,0:T(8,128)(2,1)S(1)} %get-tuple-element.136), channel_id=1, source_target_pairs={{0,1},{1,0},{2,3},{3,2},{4,5},{5,4},{6,7},{7,6},{8,9},{9,8},{10,11... | collective-permute-start | bytes 1572872 | tf_op jit(solution)/shard_map/ppermute | solution.py:324
  149.4 5.2 %copy-start.5 = (f32[16]{0:T(128)S(1)}, f32[16]{0:T(128)}, u32[]{:S(2)}) copy-start(f32[16]{0:T(128)} %param.19) | copy-start | bytes 196
  150.5 20.5 %all-to-all-start.1 = ((bf16[16,32,1024]{2,1,0:T(8,128)(2,1)}), bf16[16,32,1024]{2,1,0:T(8,128)(2,1)S(1)}, u32[]{:S(2)}, u32[]{:S(2)}) async-start(bf16[16,32,1024]{2,1,0:T(8,128)(2,1)} %bitcast.18), calls=%async_computation.1 | async-start | bytes 2097152 | tf_op jit(solution)/shard_map/all_to_all | solution.py:329

commit v3 on v2

v3 whole, which is shorter than its diff:
```python
import functools

import jax
import jax.numpy as jnp
from jax import lax
from jax.experimental import pallas as pl
from jax.experimental.pallas import tpu as pltpu
from jax.sharding import PartitionSpec as P

D = 256
N = 64
K = 32
U = 32
Z = 8
F32 = jnp.float32
BF = jnp.bfloat16
VMEM = pl.BlockSpec(memory_space=pltpu.VMEM)
SMEM = pl.BlockSpec(memory_space=pltpu.SMEM)
PARAMS = pltpu.CompilerParams(vmem_limit_bytes=24 * 1024 * 1024)
UP = [(i, (i + 1) % Z) for i in range(Z)]
DOWN = [(i, (i - 1) % Z) for i in range(Z)]
SWAP = [(0, 1), (1, 0)]
LANES = ((1,), (1,)), ((), ())


def dot_t(a, b):
    return lax.dot_general(a, b, LANES, preferred_element_type=F32)


def fm_kernel(x_ref, proj_ref, gain_ref, normed_ref, xa, xb, ts):
    xa[...] = x_ref[:, :128].astype(F32)
    xb[...] = x_ref[:, 128:].astype(F32)
    for u in range(U):
        sides = [
            jnp.concatenate(
                [xs[pl.ds(first * U + u, 16, stride=4 * U), :] for first in range(4)], axis=0
            )
            for xs in (xa, xb)
        ]
        xu = jnp.concatenate(sides, axis=1).astype(BF)
        reduced = jnp.dot(proj_ref[...], xu, preferred_element_type=F32).astype(BF)
        fm = dot_t(xu, reduced)
        ts[pl.ds(u, 16, stride=U), :] = jnp.concatenate(
            [fm[16 * i : 16 * i + 16] for i in range(4)], axis=1
        )
    t = ts[...].reshape(16, U, 128)
    m = jnp.sum(jnp.sum(t, axis=0), axis=-1, keepdims=True) / (N * K)
    q = jnp.sum(jnp.sum(t * t, axis=0), axis=-1, keepdims=True) / (N * K)
    scale = lax.rsqrt(q - m * m + 1e-05)
    for g in range(16):
        normed_ref[:, g * 128 : g * 128 + 128] = (
            (t[g] - m) * scale * gain_ref[g : g + 1, :]
        ).astype(BF)


def cut_kernel(at_ref, s_ref, perm_ref, own_ref, other_ref, cut, made):
    z, c = at_ref[0], at_ref[1]
    for t in range(2):
        for s in range(4):
            cut[t * 512 : t * 512 + 512, s * 128 : s * 128 + 128] = s_ref[
                s, :, t * 128 : t * 128 + 128
            ]
    made[...] = jnp.dot(cut[...], perm_ref[...], preferred_element_type=F32).astype(BF)
    for t in range(2):
        for side, ref in ((c, own_ref), (1 - c, other_ref)):
            rows = pl.ds(pl.multiple_of(t * 512 + side * 256, 256), 256)
            for q in range(4):
                ref[lax.rem(t * 4 + q + Z - z, Z)] = made[rows, q * 128 : q * 128 + 128]


def pair_kernel(own_ref, other_ref, *refs):
    for k, ref in enumerate(refs):
        ref[0] = own_ref[k]
        ref[1] = other_ref[k]


def pack_kernel(at_ref, *refs):
    came, out_ref = refs[:Z], refs[Z]
    z, c = at_ref[0], at_ref[1]
    for k, ref in enumerate(came):
        source = lax.rem(z + Z - k, Z)
        out_ref[2 * source + c] = ref[0]
        out_ref[2 * source + 1 - c] = ref[1]


def spread_kernel(lcb_ref, out_ref):
    rows = lax.broadcasted_iota(jnp.int32, (1024, 64), 0) // 16
    wide = (rows == lax.broadcasted_iota(jnp.int32, (1024, 64), 1)).astype(BF)
    cols = lax.broadcasted_iota(jnp.int32, (32, 512), 1) // 16
    long = (cols == lax.broadcasted_iota(jnp.int32, (32, 512), 0)).astype(BF)
    v = dot_t(wide, lcb_ref[...]).astype(BF)
    v = jnp.dot(v, long, preferred_element_type=F32)
    same = (
        lax.broadcasted_iota(jnp.int32, (1024, 512), 0) % 16
        == lax.broadcasted_iota(jnp.int32, (1024, 512), 1) % 16
    )
    out_ref[...] = jnp.where(same, v, 0.0).astype(BF)


def sums_of(x, y):
    mask = (
        lax.broadcasted_iota(jnp.int32, (32, 512), 1) // 16
        == lax.broadcasted_iota(jnp.int32, (32, 512), 0)
    ).astype(BF)
    parts = []
    for v in (x + y, x * x + y * y):
        upper = v.astype(BF)
        rest = (v - upper.astype(F32)).astype(BF)
        parts.append(dot_t(mask, upper) + dot_t(mask, rest))
    return jnp.concatenate(parts, axis=0)


def base_kernel(at_ref, s_ref, perm_ref, lcb_ref, f_own, f_other, c_own, c_other, tot_ref, made):
    c = at_ref[1]
    for p in range(8):
        pair = jnp.concatenate([s_ref[2 * p], s_ref[2 * p + 1]], axis=1)
        v = jnp.dot(pair, perm_ref[...], preferred_element_type=F32).astype(BF)
        made[0, :, p * 128 : p * 128 + 128] = v[:, :128]
        made[1, :, p * 128 : p * 128 + 128] = v[:, 128:]
    for side, f, o in ((c, f_own, c_own), (1 - c, f_other, c_other)):
        v = made[side]
        f[...] = v[:, :512]
        o[...] = v[:, 512:].astype(F32) + jnp.dot(v, lcb_ref[...], preferred_element_type=F32)
    tot_ref[...] = sums_of(c_own[...], c_other[...])


def hidden_kernel(at_ref, *refs):
    chunks, (own, other, out_ref, held) = refs[:9], refs[9:]
    z, c = at_ref[0], at_ref[1]
    for k, ref in zip((0, 7, 6, 5, 1, 2, 3), chunks[:7]):
        held[pl.ds(pl.multiple_of(lax.rem(z + k, Z) * U, U), U), :] = ref[...]
    half = pl.multiple_of(lax.rem(z + 4, Z) * U, U)
    held[pl.ds(half, U // 2), :] = chunks[7][...]
    held[pl.ds(half + U // 2, U // 2), :] = chunks[8][...]
    for where, w in ((c, own), (1 - c, other)):
        h = jnp.dot(held[...], w[...], preferred_element_type=F32)
        out_ref[:, pl.ds(pl.multiple_of(where * 256, 256), 256)] = jnp.maximum(h, 0.0).astype(BF)


def part_kernel(n, at_ref, *refs):
    chunks, weights = refs[:n], refs[n : 3 * n]
    sums, outs = refs[3 * n : -2], refs[-2:]
    for side, out in enumerate(outs):
        acc = sum(dot_t(chunks[i][...], weights[2 * i + side][...]) for i in range(n))
        out[...] = acc + sums[side][...] if sums else acc


def part(place, blocks, weights, sums):
    n = len(blocks)

    def columns(k):
        return pl.BlockSpec((512, 512), lambda i, at: (0, lax.rem(at[0] + k, Z)))

    whole = pl.BlockSpec((Z * U, 512), lambda i, at: (0, 0))
    return pl.pallas_call(
        functools.partial(part_kernel, n),
        grid_spec=pltpu.PrefetchScalarGridSpec(
            num_scalar_prefetch=1,
            grid=(1,),
            in_specs=[whole] * n
            + [columns(k) for k, _ in blocks for _ in range(2)]
            + [whole] * len(sums),
            out_specs=[whole] * 2,
        ),
        out_shape=[jax.ShapeDtypeStruct((Z * U, 512), F32)] * 2,
        compiler_params=PARAMS,
        cost_estimate=pl.CostEstimate(
            flops=n * 2 * 2 * 256 * 512 * 512, bytes_accessed=n * 2**20, transcendentals=0
        ),
        name="fm_out_part",
    )(place, *[v for _, v in blocks], *[w for _ in blocks for w in weights], *sums)


def out_kernel(
    at_ref, low, high, w_own, w_other, a_own, a_other, s_own, s_other, tc_ref, o_own, o_other, tot_ref
):
    half = low.shape[0]
    for w, a, s, o in ((w_own, a_own, s_own, o_own), (w_other, a_other, s_other, o_other)):
        o[:half] = a[:half] + s[:half].astype(F32) + dot_t(low[...], w[...])
        o[half:] = a[half:] + s[half:].astype(F32) + dot_t(high[...], w[...])
    tot_ref[:64] = sums_of(o_own[...], o_other[...])
    tot_ref[64:] = tc_ref[...]


def scale_kernel(f_own, f_other, c_own, c_other, tot_ref, o_own, o_other):
    spread = (
        lax.broadcasted_iota(jnp.int32, (32, 512), 1) // 16
        == lax.broadcasted_iota(jnp.int32, (32, 512), 0)
    ).astype(BF)

    def widen(v):
        high = v.astype(BF)
        low = (v - high.astype(F32)).astype(BF)
        dims = ((0,), (0,)), ((), ())
        return lax.dot_general(high, spread, dims, preferred_element_type=F32) + lax.dot_general(
            low, spread, dims, preferred_element_type=F32
        )

    for at, own, other in ((0, f_own, f_other), (64, c_own, c_other)):
        m = tot_ref[at : at + 32, :] / D
        q = tot_ref[at + 32 : at + 64, :] / D
        r = widen(lax.rsqrt(q - m * m + 1e-05))
        m = widen(m)
        for s, o in ((own, o_own), (other, o_other)):
            o[:, at * 8 : at * 8 + 512] = ((s[...] - m) * r).astype(BF)


def finish_kernel(at_ref, own_ref, came_ref, gain_ref, o_ref):
    c = at_ref[1]
    for side, ref in ((c, own_ref), (1 - c, came_ref)):
        v = ref[...].astype(F32).T * gain_ref[...]
        o_ref[:, pl.ds(pl.multiple_of(side * 256, 256), 256)] = v.astype(BF)


def step(up, down):
    return lax.ppermute(up, "emb", UP), lax.ppermute(down, "emb", DOWN)


def after(value, event):
    return lax.optimization_barrier((value, event))


def shards(
    events, counts, live, enc_weight, fm_proj, ln_gain, w_hidden, w_out, lcb_weight, out_gain
):
    users_enc, sess_dev, slot_count, full_width = events.shape
    z, c = lax.axis_index("emb"), lax.axis_index("section")
    place = jnp.stack([z, c]).astype(jnp.int32)
    w_hidden_other = lax.ppermute(w_hidden, "section", SWAP)
    w_own = jnp.transpose(w_out, (1, 2, 0)).reshape(512, -1)
    w_other = lax.ppermute(w_own, "section", SWAP)

    inside = (lax.broadcasted_iota(jnp.int32, (1, 1, slot_count), 2) < counts[:, :, None]).astype(BF)
    session_sums = jnp.einsum("usj,usjd->usd", inside, events, preferred_element_type=F32)
    share_of = live.astype(F32) / counts.astype(F32)
    pooled = (session_sums * share_of[:, :, None]).astype(BF)
    encoded = jnp.dot(pooled.reshape(-1, full_width), enc_weight, preferred_element_type=F32)
    session = encoded.reshape(users_enc, sess_dev, full_width).astype(BF)
    chunks = jnp.transpose(session.reshape(2, Z, U, sess_dev, D), (1, 0, 3, 2, 4))
    x = lax.all_to_all(chunks.reshape(16, sess_dev, U, D), "dp", 0, 0, tiled=True)
    x = x.reshape(N * U, D)

    def call(kernel, name, shapes, args, scratch=(), scalars=(place,), flops=2**28):
        return pl.pallas_call(
            kernel,
            out_shape=[jax.ShapeDtypeStruct(*v) for v in shapes],
            in_specs=[SMEM] * len(scalars) + [VMEM] * len(args),
            out_specs=[VMEM] * len(shapes),
            scratch_shapes=scratch,
            compiler_params=PARAMS,
            cost_estimate=pl.CostEstimate(flops=flops, bytes_accessed=2**22, transcendentals=0),
            name=name,
        )(*scalars, *args)

    row = lax.broadcasted_iota(jnp.int32, (512, 1), 0)
    goal = (row // 32) % 4 * 128 + (row // 16) % 2 * 64 + row // 128 * 16 + row % 16
    perm = (goal == lax.broadcasted_iota(jnp.int32, (1, 512), 1)).astype(BF)
    own, other = call(
        cut_kernel,
        "cut",
        [((Z, 256, 128), BF)] * 2,
        (jnp.transpose(session, (1, 0, 2)), perm),
        [pltpu.VMEM((1024, 512), BF)] * 2,
    )
    other = lax.ppermute(other, "section", SWAP)
    slices = call(pair_kernel, "pair", [((2, 256, 128), BF)] * Z, (own, other), scalars=())
    came = [slices[0]] + [None] * 7
    for k in (1, 7, 2, 6, 3, 5, 4):
        came[k] = lax.ppermute(slices[k], "emb", [(i, (i + k) % Z) for i in range(Z)])

    def arrived(event, distances):
        held, event = after([came[k] for k in distances], event)
        for k, v in zip(distances, held):
            came[k] = v
        return event

    x = arrived(x, (1, 7))
    row = lax.broadcasted_iota(jnp.int32, (256, 1), 0)
    goal = (row // 64) % 2 * 128 + row // 128 * 64 + row % 64
    perm = (goal == lax.broadcasted_iota(jnp.int32, (1, 256), 1)).astype(BF)
    (spread,) = call(spread_kernel, "spread", [((1024, 512), BF)], (lcb_weight,), scalars=())

    proj = jnp.transpose(fm_proj.T.reshape(K, 16, 4), (0, 2, 1)).reshape(K, N)
    (normed,) = call(
        fm_kernel,
        "fm_rows",
        [((U, N * K), BF)],
        (x, proj, ln_gain.reshape(16, 128)),
        [pltpu.VMEM((N * U, 128), F32)] * 2 + [pltpu.VMEM((16 * U, 128), F32)],
        scalars=(),
    )
    normed = arrived(normed, (2, 6, 3, 5))
    normed = lax.ppermute(
        normed,
        ("dp", "emb", "section"),
        [(a * 16 + b, b * 16 + a) for a in range(16) for b in range(16)],
    )
    normed = arrived(normed, (4,))
    up1, down1 = step(normed, normed)
    came[0], _ = after(came[0], (up1, down1))
    (packed,) = call(pack_kernel, "pack", [((16, 256, 128), BF)], tuple(came))
    slices = lax.all_to_all(packed, "dp", 0, 0, tiled=True)
    up2, down2 = step(up1, down1)
    up3, down3 = step(up2, down2)
    low, high = step(up3[: U // 2], down3[U // 2 :])
    hidden = pl.pallas_call(
        hidden_kernel,
        out_shape=jax.ShapeDtypeStruct((Z * U, 512), BF),
        in_specs=[SMEM] + [VMEM] * 11,
        out_specs=VMEM,
        scratch_shapes=[pltpu.VMEM((Z * U, N * K), BF)],
        compiler_params=PARAMS,
        name="hidden",
    )(place, normed, up1, up2, up3, down1, down2, down3, low, high, w_hidden, w_hidden_other)

    users = Z * U
    weights = w_own, w_other
    up1, down1 = step(hidden, hidden)
    sums = part(place, [(0, hidden)], weights, [])
    f_own, f_other, c_own, c_other, c_sums = call(
        base_kernel,
        "base",
        [((users, 512), BF)] * 2 + [((users, 512), F32)] * 2 + [((64, users), F32)],
        (slices, perm, spread),
        [pltpu.VMEM((2, users, 1024), BF)],
    )
    (up1, down1), sums = after((up1, down1), sums)
    (up1, down1), (f_own, f_other) = after((up1, down1), (f_own, f_other))
    up2, down2 = step(up1, down1)
    sums = part(place, [(7, up1), (1, down1)], weights, sums)
    (up2, down2), sums = after((up2, down2), sums)
    up3, down3 = step(up2, down2)
    sums = part(place, [(6, up2), (2, down2)], weights, sums)
    (up3, down3), sums = after((up3, down3), sums)
    low, high = step(up3[: users // 2], down3[users // 2 :])
    sums = part(place, [(5, up3), (3, down3)], weights, sums)

    def all_of(*shape):
        return pl.BlockSpec(shape, lambda i, at: (0,) * len(shape))

    column = pl.BlockSpec((512, 512), lambda i, at: (0, lax.rem(at[0] + 4, Z)))
    f_own, f_other, totals = pl.pallas_call(
        out_kernel,
        grid_spec=pltpu.PrefetchScalarGridSpec(
            num_scalar_prefetch=1,
            grid=(1,),
            in_specs=[all_of(users // 2, 512)] * 2
            + [column] * 2
            + [all_of(users, 512)] * 4
            + [all_of(64, users)],
            out_specs=[all_of(users, 512)] * 2 + [all_of(128, users)],
        ),
        out_shape=[jax.ShapeDtypeStruct((users, 512), F32)] * 2
        + [jax.ShapeDtypeStruct((128, users), F32)],
        compiler_params=PARAMS,
        name="fm_out",
    )(place, low, high, *weights, *sums, f_own, f_other, c_sums)

    for bit in (1, 2, 4):
        theirs = lax.ppermute(totals.astype(BF), "emb", [(i, i ^ bit) for i in range(Z)])
        totals = totals + theirs.astype(F32)

    own, other = call(
        scale_kernel,
        "scale",
        [((users, 1024), BF)] * 2,
        (f_own, f_other, c_own, c_other, totals),
        scalars=(),
    )
    other = lax.ppermute(other, "section", SWAP)
    gain = jnp.tile(out_gain, 64).reshape(1024, 1)
    (out,) = call(finish_kernel, "finish", [((1024, 512), BF)], (own, other, gain))
    return jnp.transpose(out.reshape(64, 16, 512), (2, 0, 1))


def solution(mesh):
    in_specs = (
        P(("emb", "section"), "dp", None, None),
        P(("emb", "section"), "dp"),
        P(("emb", "section"), "dp"),
        P(),
        P(),
        P(),
        P(None, ("emb", "section")),
        P(None, None, ("emb", "section")),
        P(),
        P(("emb", "section")),
    )
    out_specs = P("dp", None, ("emb", "section"))
    return jax.shard_map(shards, mesh=mesh, in_specs=in_specs, out_specs=out_specs, check_vma=False)
```

time: 173 us -> 171 us (0.988)
  waiting for transfers between devices: 66.3 us -> 36.9 us
  starting transfers between devices: 69.9 us -> 90.7 us
  local copies, waits for them, and re-layouts: 3.61 us -> 8 us
  Pallas kernels: 24.2 us -> 26.6 us
    all_to_all x2, waiting for transfers between devices: 32.1 us -> 0.01 us  [the longest x1 0.01 us: shards(): lax.all_to_all(chunks.reshape(16, sess_dev, U, D), 'dp', 0, 0, tiled=True)]
    ppermute x16, starting transfers between devices: 25.8 us -> 36 us  [step(): return (lax.ppermute(up, 'emb', UP), lax.ppermute(down, 'emb', DOWN))]
    ppermute x8 -> x10, starting transfers between devices: 26.8 us -> 36.6 us  [the longest x7 22.1 us: shards(): lax.ppermute(slices[k], 'emb', [(i, (i + k) % Z) for i in range(Z)])]
    unnamed x15 -> x30, local copies, waits for them, and re-layouts: 1.06 us -> 6.52 us
    ppermute x8 -> x10, waiting for transfers between devices: 11.1 us -> 6.58 us  [the longest x7 3.75 us: shards(): lax.ppermute(slices[k], 'emb', [(i, (i + k) % Z) for i in range(Z)])]
    ppermute x3, waiting for transfers between devices: 9.78 us -> 14.2 us  [shards(): lax.ppermute(totals.astype(BF), 'emb', [(i, i ^ bit) for i in range(Z)])]
    pallas_call x4 -> x8, Pallas kernels: 8.19 us -> 11.8 us  [call(): pl.pallas_call(kernel, out_shape=[jax.ShapeDtypeStruct(*v) for v in shape...]
    ppermute x16, waiting for transfers between devices: 13.2 us -> 16.2 us  [step(): return (lax.ppermute(up, 'emb', UP), lax.ppermute(down, 'emb', DOWN))]
  transfers between devices with their start and end apart: 31 -> 33, of which waited for: 21 -> 15; matrix products, arithmetic and copies ran while one was open for 6% -> 6% of each run, Pallas kernels for 11% -> 12%
where the time goes in v3:
time: 171 us; the launch traced here: 170 us
  starting transfers between devices  90.7 us (53%)
  waiting for transfers between devices  36.9 us (22%)
  Pallas kernels  26.6 us (16%)
  local copies, waits for them, and re-layouts  8 us (5%)
  matrix products  5.23 us (3%)
  other arithmetic  2.5 us (1%)
    ppermute x16, starting transfers between devices, step(): return (lax.ppermute(up, 'emb', UP), lax.ppermute(down, 'emb', DOWN))  36 us
    ppermute x7, starting transfers between devices, shards(): lax.ppermute(slices[k], 'emb', [(i, (i + k) % Z) for i in range(Z)])  22.1 us
    ppermute x16, waiting for transfers between devices, step(): return (lax.ppermute(up, 'emb', UP), lax.ppermute(down, 'emb', DOWN))  16.2 us
    ppermute x3, waiting for transfers between devices, shards(): lax.ppermute(totals.astype(BF), 'emb', [(i, i ^ bit) for i in range(Z)])  14.2 us
    pallas_call x8, Pallas kernels, call(): pl.pallas_call(kernel, out_shape=[jax.ShapeDtypeStruct(*v) for v in shape...  11.8 us
    ppermute x2, starting transfers between devices, shards(): other = lax.ppermute(other, 'section', SWAP)  10.8 us
    pallas_call x4, Pallas kernels, part(): pl.pallas_call(functools.partial(part_kernel, n), grid_spec=pltpu.Prefetc...  9.99 us
    unnamed x30, local copies, waits for them, and re-layouts  6.52 us
  transfers between devices with their start and end apart: 33, of which 15 were waited for; matrix products, arithmetic and copies ran while one was open for 6% of the time, Pallas kernels for 12%

profile of v3, /device:TPU:1, one launch (start us, length us, event | category | flops | bytes accessed | tf_op | source)
XLA Modules:
  0.0 170.4 jit_solution(13815876713038990423)
XLA Ops:
  0.0 3.2 %collective-permute-start.20 = (bf16[512,4096]{1,0:T(8,128)(2,1)}, bf16[512,4096]{1,0:T(8,128)(2,1)}, u32[]{:S(2)}, u32[]{:S(2)}) collective-permute-start(bf16[512,4096]{1,0:T(8,128)(2,1)} %bitcast.32), channel_id=1, source_target_pairs={{0,1},{1,0},{2,3},{3,2},{4,5},{5,4},{6,7},{7,6},{8,9},{9,8},{10,11... | collective-permute-start | bytes 12582920 | tf_op jit(solution)/shard_map/ppermute | solution.py:231
  4.8 1.3 fusion.5
  6.2 4.7 %fusion = f32[512,4,1,256]{3,2,1,0:T(1,128)S(1)} fusion(bf16[512,4,4,256]{3,2,1,0:T(4,128)(2,1)} %param.10, pred[512,4,4,1]{2,1,0,3:T(4,128)(4,1)S(1)} %fusion.5), kind=kOutput, calls=%fused_computation | convolution fusion | flops 4194304 | bytes 6299648 | tf_op jit(solution)/shard_map/usj,usjd->usd/dot_general | solution.py:234
  11.4 1.1 copy.15
  12.5 5.0 %all-to-all-start = ((bf16[16,4,32,256]{3,2,1,0:T(8,128)(2,1)}), bf16[16,4,32,256]{3,2,1,0:T(8,128)(2,1)S(1)}, u32[]{:S(2)}, u32[]{:S(2)}) async-start(bf16[16,4,32,256]{3,2,1,0:T(8,128)(2,1)} %bitcast.8), calls=%async_computation | async-start | bytes 2097152 | tf_op jit(solution)/shard_map/all_to_all | solution.py:240
  17.8 1.4 cut.1
  19.7 1.6 collective-permute-done.other_ref
  21.3 1.7 %collective-permute-start.6 = (bf16[2,256,128]{2,1,0:T(8,128)(2,1)S(1)}, bf16[2,256,128]{2,1,0:T(8,128)(2,1)S(1)}, u32[]{:S(2)}, u32[]{:S(2)}) collective-permute-start(bf16[2,256,128]{2,1,0:T(8,128)(2,1)S(1)} %get-tuple-element.67), channel_id=1, source_target_pairs={{0,2},{2,4},{4,6},{6,8},{8,10},{10,12},{12,14},{14,0},{1,3},{3,5},... | collective-permute-start | bytes 393224 | tf_op jit(solution)/shard_map/ppermute | solution.py:269
  23.0 4.0 %collective-permute-start.7 = (bf16[2,256,128]{2,1,0:T(8,128)(2,1)S(1)}, bf16[2,256,128]{2,1,0:T(8,128)(2,1)S(1)}, u32[]{:S(2)}, u32[]{:S(2)}) collective-permute-start(bf16[2,256,128]{2,1,0:T(8,128)(2,1)S(1)} %get-tuple-element.68), channel_id=1, source_target_pairs={{0,14},{2,0},{4,2},{6,4},{8,6},{10,8},{12,10},{14,12},{1,15},{3,1}... | collective-permute-start | bytes 393224 | tf_op jit(solution)/shard_map/ppermute | solution.py:269
  27.1 3.6 %collective-permute-start.3 = (bf16[2,256,128]{2,1,0:T(8,128)(2,1)S(1)}, bf16[2,256,128]{2,1,0:T(8,128)(2,1)S(1)}, u32[]{:S(2)}, u32[]{:S(2)}) collective-permute-start(bf16[2,256,128]{2,1,0:T(8,128)(2,1)S(1)} %get-tuple-element.64), channel_id=1, source_target_pairs={{0,12},{2,14},{4,0},{6,2},{8,4},{10,6},{12,8},{14,10},{1,13},{3,15... | collective-permute-start | bytes 393224 | tf_op jit(solution)/shard_map/ppermute | solution.py:269
  31.2 4.0 %collective-permute-start.5 = (bf16[2,256,128]{2,1,0:T(8,128)(2,1)S(1)}, bf16[2,256,128]{2,1,0:T(8,128)(2,1)S(1)}, u32[]{:S(2)}, u32[]{:S(2)}) collective-permute-start(bf16[2,256,128]{2,1,0:T(8,128)(2,1)S(1)} %get-tuple-element.66), channel_id=1, source_target_pairs={{0,10},{2,12},{4,14},{6,0},{8,2},{10,4},{12,6},{14,8},{1,11},{3,13... | collective-permute-start | bytes 393224 | tf_op jit(solution)/shard_map/ppermute | solution.py:269
  36.1 3.0 %collective-permute-start.17 = (bf16[2048,256]{1,0:T(8,128)(2,1)}, bf16[2048,256]{1,0:T(8,128)(2,1)}, u32[]{:S(2)}, u32[]{:S(2)}) collective-permute-start(bf16[2048,256]{1,0:T(8,128)(2,1)} %refs_9_.1), channel_id=1, source_target_pairs={{0,1},{1,0},{2,3},{3,2},{4,5},{5,4},{6,7},{7,6},{8,9},{9,8},{10,11... | collective-permute-start | bytes 3145736 | tf_op jit(solution)/shard_map/ppermute | solution.py:229
  39.1 3.1 %fm_rows.1 = bf16[32,2048]{1,0:T(8,128)(2,1)S(1)} custom-call(bf16[2048,256]{1,0:T(8,128)(2,1)S(1)} %bitcast.43, bf16[32,64]{1,0:T(8,128)(2,1)S(1)} %copy.18.proj_ref, f32[16,128]{1,0:T(8,128)S(1)} %bitcast.44), custom_call_target="tpu_custom_call" | custom-call | flops 268435456 | bytes 4194304 | tf_op jit(solution)/shard_map/fm_rows/pallas_call | solution.py:244
  42.2 8.3 %collective-permute-start.1 = (bf16[2,256,128]{2,1,0:T(8,128)(2,1)S(1)}, bf16[2,256,128]{2,1,0:T(8,128)(2,1)S(1)}, u32[]{:S(2)}, u32[]{:S(2)}) collective-permute-start(bf16[2,256,128]{2,1,0:T(8,128)(2,1)S(1)} %get-tuple-element.62), channel_id=1, source_target_pairs={{0,8},{2,10},{4,12},{6,14},{8,0},{10,2},{12,4},{14,6},{1,9},{3,11}... | collective-permute-start | bytes 393224 | tf_op jit(solution)/shard_map/ppermute | solution.py:269
  50.5 3.8 %collective-permute-start.8 = (bf16[32,2048]{1,0:T(8,128)(2,1)S(1)}, bf16[32,2048]{1,0:T(8,128)(2,1)S(1)}, u32[]{:S(2)}, u32[]{:S(2)}) collective-permute-start(bf16[32,2048]{1,0:T(8,128)(2,1)S(1)} %fm_rows.1), channel_id=1, source_target_pairs={{0,0},{1,16},{2,32},{3,48},{4,64},{5,80},{6,96},{7,112},{8,128},{9... | collective-permute-start | bytes 393224 | tf_op jit(solution)/shard_map/ppermute | solution.py:293
  54.3 2.9 %collective-permute-done.1.refs_4_ = bf16[2,256,128]{2,1,0:T(8,128)(2,1)S(1)} collective-permute-done((bf16[2,256,128]{2,1,0:T(8,128)(2,1)S(1)}, bf16[2,256,128]{2,1,0:T(8,128)(2,1)S(1)}, u32[]{:S(2)}, u32[]{:S(2)}) %collective-permute-start.1) | collective-permute-done | bytes 131104 | tf_op jit(solution)/shard_map/ppermute | solution.py:269
  57.2 16.1 %collective-permute-start.12 = (bf16[32,2048]{1,0:T(8,128)(2,1)S(1)}, bf16[32,2048]{1,0:T(8,128)(2,1)S(1)}, u32[]{:S(2)}, u32[]{:S(2)}) collective-permute-start(bf16[32,2048]{1,0:T(8,128)(2,1)S(1)} %collective-permute-done.8.refs_0_), channel_id=1, source_target_pairs={{0,14},{2,0},{4,2},{6,4},{8,6},{10,8},{12,10},{14,12},{1,15},{3,1}... | collective-permute-start | bytes 393224 | tf_op jit(solution)/shard_map/ppermute | solution.py:216
  74.0 1.3 collective-permute-done.12.refs_4_
  75.3 3.1 %collective-permute-done.9.refs_1_ = bf16[32,2048]{1,0:T(8,128)(2,1)S(1)} collective-permute-done((bf16[32,2048]{1,0:T(8,128)(2,1)S(1)}, bf16[32,2048]{1,0:T(8,128)(2,1)S(1)}, u32[]{:S(2)}, u32[]{:S(2)}) %collective-permute-start.9) | collective-permute-done | bytes 131104 | tf_op jit(solution)/shard_map/ppermute | solution.py:216
  78.4 1.6 pack.1
  80.0 5.2 %all-to-all-start.1 = ((bf16[16,256,128]{2,1,0:T(8,128)(2,1)}), bf16[16,256,128]{2,1,0:T(8,128)(2,1)S(1)}, u32[]{:S(2)}, u32[]{:S(2)}) async-start(bf16[16,256,128]{2,1,0:T(8,128)(2,1)} %pack.1), calls=%async_computation.1 | async-start | bytes 2097152 | tf_op jit(solution)/shard_map/all_to_all | solution.py:302
  85.3 2.7 %collective-permute-start.13 = (bf16[32,2048]{1,0:T(8,128)(2,1)S(1)}, bf16[32,2048]{1,0:T(8,128)(2,1)S(1)}, u32[]{:S(2)}, u32[]{:S(2)}) collective-permute-start(bf16[32,2048]{1,0:T(8,128)(2,1)S(1)} %collective-permute-done.12.refs_4_), channel_id=1, source_target_pairs={{0,14},{2,0},{4,2},{6,4},{8,6},{10,8},{12,10},{14,12},{1,15},{3,1}... | collective-permute-start | bytes 393224 | tf_op jit(solution)/shard_map/ppermute | solution.py:216
  87.9 2.3 %collective-permute-done.10.refs_2_ = bf16[32,2048]{1,0:T(8,128)(2,1)S(1)} collective-permute-done((bf16[32,2048]{1,0:T(8,128)(2,1)S(1)}, bf16[32,2048]{1,0:T(8,128)(2,1)S(1)}, u32[]{:S(2)}, u32[]{:S(2)}) %collective-permute-start.10) | collective-permute-done | bytes 131104 | tf_op jit(solution)/shard_map/ppermute | solution.py:216
  90.3 2.7 %collective-permute-start.14 = (bf16[32,2048]{1,0:T(8,128)(2,1)S(1)}, bf16[32,2048]{1,0:T(8,128)(2,1)S(1)}, u32[]{:S(2)}, u32[]{:S(2)}) collective-permute-start(bf16[32,2048]{1,0:T(8,128)(2,1)S(1)} %collective-permute-done.13.refs_5_), channel_id=1, source_target_pairs={{0,14},{2,0},{4,2},{6,4},{8,6},{10,8},{12,10},{14,12},{1,15},{3,1}... | collective-permute-start | bytes 393224 | tf_op jit(solution)/shard_map/ppermute | solution.py:216
  92.9 2.6 %collective-permute-done.11.refs_3_ = bf16[32,2048]{1,0:T(8,128)(2,1)S(1)} collective-permute-done((bf16[32,2048]{1,0:T(8,128)(2,1)S(1)}, bf16[32,2048]{1,0:T(8,128)(2,1)S(1)}, u32[]{:S(2)}, u32[]{:S(2)}) %collective-permute-start.11) | collective-permute-done | bytes 131104 | tf_op jit(solution)/shard_map/ppermute | solution.py:216
  95.6 2.7 %collective-permute-start.16 = (bf16[16,2048]{1,0:T(8,128)(2,1)S(1)}, bf16[16,2048]{1,0:T(8,128)(2,1)S(1)}, u32[]{:S(2)}, u32[]{:S(2)}) collective-permute-start(bf16[16,2048]{1,0:T(8,128)(2,1)S(1)} %slice.17), channel_id=1, source_target_pairs={{0,14},{2,0},{4,2},{6,4},{8,6},{10,8},{12,10},{14,12},{1,15},{3,1}... | collective-permute-start | bytes 196616 | tf_op jit(solution)/shard_map/ppermute | solution.py:216
  98.9 1.2 collective-permute-done.15.refs_7_
  102.9 2.0 %hidden.1.refs_0_ = bf16[256,512]{1,0:T(8,128)(2,1)S(1)} custom-call(s32[2]{0:T(128)S(1)} %pad_add_fusion.at_ref, bf16[32,2048]{1,0:T(8,128)(2,1)S(1)} %copy-done.5, bf16[32,2048]{1,0:T(8,128)(2,1)S(1)} %copy-done.9, bf16[32,2048]{1,0:T(8,128)(2,1)S(1)} %collective-permute-done.10.refs_2_, bf16[32,2048]{1,0:T(8,128)(2,1)S(1)} %collective-permute-done.11.refs_3_, ...), custom_call_target="tpu_custom_call" | custom-call | tf_op jit(solution)/shard_map/hidden/pallas_call | solution.py:306
  105.0 3.1 %collective-permute-start.19 = (bf16[256,512]{1,0:T(8,128)(2,1)S(1)}, bf16[256,512]{1,0:T(8,128)(2,1)S(1)}, u32[]{:S(2)}, u32[]{:S(2)}) collective-permute-start(bf16[256,512]{1,0:T(8,128)(2,1)S(1)} %hidden.1.refs_0_), channel_id=1, source_target_pairs={{0,14},{2,0},{4,2},{6,4},{8,6},{10,8},{12,10},{14,12},{1,15},{3,1}... | collective-permute-start | bytes 786440 | tf_op jit(solution)/shard_map/ppermute | solution.py:216
  108.2 2.1 %base.1 = (bf16[256,512]{1,0:T(8,128)(2,1)S(1)}, bf16[256,512]{1,0:T(8,128)(2,1)S(1)}, f32[256,512]{1,0:T(8,128)S(1)}, f32[256,512]{1,0:T(8,128)S(1)}, f32[64,256]{1,0:T(8,128)S(1)}) custom-call(s32[2]{0:T(128)S(1)} %pad_add_fusion.at_ref, bf16[16,256,128]{2,1,0:T(8,128)(2,1)S(1)} %all-to-all-done.1.s_ref, bf16[256,256]{1,0:T(8,128)(2,1)S(1)} %fusion.7.perm_ref, ...), custom_call_target="tpu_custom_call" | custom-call | flops 268435456 | bytes 4194304 | tf_op jit(solution)/shard_map/base/pallas_call | solution.py:244
  110.3 2.2 %copy-done.1 = bf16[4096,32,16]{0,2,1:T(8,128)(2,1)S(1)} copy-done((bf16[4096,32,16]{0,2,1:T(8,128)(2,1)S(1)}, bf16[4096,32,16]{0,2,1:T(8,128)(2,1)}, u32[]{:S(2)}) %copy-start.1) | copy-done | bytes 4194328
  112.5 2.4 %fm_out_part.4 = (f32[256,512]{1,0:T(8,128)S(1)}, f32[256,512]{1,0:T(8,128)S(1)}) custom-call(s32[2]{0:T(128)S(1)} %pad_add_fusion.at_ref, bf16[256,512]{1,0:T(8,128)(2,1)S(1)} %hidden.1.refs_0_, bf16[512,4096]{1,0:T(8,128)(2,1)S(1)} %bitcast.33, bf16[512,4096]{1,0:T(8,128)(2,1)} %collective-permute-done.20.refs_2_.refs_3_.refs_5_.w_other), custom_call_target="tpu_custom_call" | custom-call | flops 268435456 | bytes 1048576 | tf_op jit(solution)/shard_map/fm_out_part/pallas_call | solution.py:155
  115.0 2.7 %collective-permute-start.22 = (bf16[256,512]{1,0:T(8,128)(2,1)S(1)}, bf16[256,512]{1,0:T(8,128)(2,1)S(1)}, u32[]{:S(2)}, u32[]{:S(2)}) collective-permute-start(bf16[256,512]{1,0:T(8,128)(2,1)S(1)} %collective-permute-done.19.refs_1_), channel_id=1, source_target_pairs={{0,14},{2,0},{4,2},{6,4},{8,6},{10,8},{12,10},{14,12},{1,15},{3,1}... | collective-permute-start | bytes 786440 | tf_op jit(solution)/shard_map/ppermute | solution.py:216
  117.7 2.5 %fm_out_part.5 = (f32[256,512]{1,0:T(8,128)S(1)}, f32[256,512]{1,0:T(8,128)S(1)}) custom-call(s32[2]{0:T(128)S(1)} %pad_add_fusion.at_ref, bf16[256,512]{1,0:T(8,128)(2,1)S(1)} %collective-permute-done.18.refs_0_, bf16[256,512]{1,0:T(8,128)(2,1)S(1)} %collective-permute-done.19.refs_1_, bf16[512,4096]{1,0:T(8,128)(2,1)S(1)} %bitcast.34, ...), custom_call_target="tpu_custom_call" | custom-call | flops 536870912 | bytes 2097152 | tf_op jit(solution)/shard_map/fm_out_part/pallas_call | solution.py:155
  120.2 1.2 collective-permute-done.21.refs_0_
  121.4 2.7 %collective-permute-start.24 = (bf16[256,512]{1,0:T(8,128)(2,1)S(1)}, bf16[256,512]{1,0:T(8,128)(2,1)S(1)}, u32[]{:S(2)}, u32[]{:S(2)}) collective-permute-start(bf16[256,512]{1,0:T(8,128)(2,1)S(1)} %collective-permute-done.22.refs_1_), channel_id=1, source_target_pairs={{0,14},{2,0},{4,2},{6,4},{8,6},{10,8},{12,10},{14,12},{1,15},{3,1}... | collective-permute-start | bytes 786440 | tf_op jit(solution)/shard_map/ppermute | solution.py:216
  124.1 2.5 %fm_out_part.6 = (f32[256,512]{1,0:T(8,128)S(1)}, f32[256,512]{1,0:T(8,128)S(1)}) custom-call(s32[2]{0:T(128)S(1)} %pad_add_fusion.at_ref, bf16[256,512]{1,0:T(8,128)(2,1)S(1)} %collective-permute-done.21.refs_0_, bf16[256,512]{1,0:T(8,128)(2,1)S(1)} %collective-permute-done.22.refs_1_, bf16[512,4096]{1,0:T(8,128)(2,1)S(1)} %bitcast.36, ...), custom_call_target="tpu_custom_call" | custom-call | flops 536870912 | bytes 2097152 | tf_op jit(solution)/shard_map/fm_out_part/pallas_call | solution.py:155
  126.7 3.0 %collective-permute-done.23.refs_0_ = bf16[256,512]{1,0:T(8,128)(2,1)S(1)} collective-permute-done((bf16[256,512]{1,0:T(8,128)(2,1)S(1)}, bf16[256,512]{1,0:T(8,128)(2,1)S(1)}, u32[]{:S(2)}, u32[]{:S(2)}) %collective-permute-start.23) | collective-permute-done | bytes 262176 | tf_op jit(solution)/shard_map/ppermute | solution.py:216
  129.8 3.0 %collective-permute-start.26 = (bf16[128,512]{1,0:T(8,128)(2,1)S(1)}, bf16[128,512]{1,0:T(8,128)(2,1)S(1)}, u32[]{:S(2)}, u32[]{:S(2)}) collective-permute-start(bf16[128,512]{1,0:T(8,128)(2,1)S(1)} %slice.15), channel_id=1, source_target_pairs={{0,14},{2,0},{4,2},{6,4},{8,6},{10,8},{12,10},{14,12},{1,15},{3,1}... | collective-permute-start | bytes 393224 | tf_op jit(solution)/shard_map/ppermute | solution.py:216
  132.9 2.5 %fm_out_part.7 = (f32[256,512]{1,0:T(8,128)S(1)}, f32[256,512]{1,0:T(8,128)S(1)}) custom-call(s32[2]{0:T(128)S(1)} %pad_add_fusion.at_ref, bf16[256,512]{1,0:T(8,128)(2,1)S(1)} %collective-permute-done.23.refs_0_, bf16[256,512]{1,0:T(8,128)(2,1)S(1)} %collective-permute-done.24.refs_1_, bf16[512,4096]{1,0:T(8,128)(2,1)S(1)} %bitcast.38, ...), custom_call_target="tpu_custom_call" | custom-call | flops 536870912 | bytes 2097152 | tf_op jit(solution)/shard_map/fm_out_part/pallas_call | solution.py:155
  135.4 1.3 collective-permute-done.25.low
  136.7 2.8 %fm_out.1 = (f32[256,512]{1,0:T(8,128)S(1)}, f32[256,512]{1,0:T(8,128)S(1)}, f32[128,256]{1,0:T(8,128)S(1)}) custom-call(s32[2]{0:T(128)S(1)} %pad_add_fusion.at_ref, bf16[128,512]{1,0:T(8,128)(2,1)S(1)} %collective-permute-done.25.low, bf16[128,512]{1,0:T(8,128)(2,1)S(1)} %collective-permute-done.26.high, bf16[512,4096]{1,0:T(8,128)(2,1)S(1)} %bitcast.40, ...), custom_call_target="tpu_custom_call" | custom-call | tf_op jit(solution)/shard_map/fm_out/pallas_call | solution.py:342
  139.6 3.8 %collective-permute-done.27 = bf16[128,256]{1,0:T(8,128)(2,1)S(1)} collective-permute-done((bf16[128,256]{1,0:T(8,128)(2,1)S(1)}, bf16[128,256]{1,0:T(8,128)(2,1)S(1)}, u32[]{:S(2)}, u32[]{:S(2)}) %collective-permute-start.27) | collective-permute-done | bytes 65568 | tf_op jit(solution)/shard_map/ppermute | solution.py:360
  144.0 4.2 %collective-permute-done.28 = bf16[128,256]{1,0:T(8,128)(2,1)S(1)} collective-permute-done((bf16[128,256]{1,0:T(8,128)(2,1)S(1)}, bf16[128,256]{1,0:T(8,128)(2,1)S(1)}, u32[]{:S(2)}, u32[]{:S(2)}) %collective-permute-start.28) | collective-permute-done | bytes 65568 | tf_op jit(solution)/shard_map/ppermute | solution.py:360
  149.3 6.1 %collective-permute-done.29 = bf16[128,256]{1,0:T(8,128)(2,1)S(1)} collective-permute-done((bf16[128,256]{1,0:T(8,128)(2,1)S(1)}, bf16[128,256]{1,0:T(8,128)(2,1)S(1)}, u32[]{:S(2)}, u32[]{:S(2)}) %collective-permute-start.29) | collective-permute-done | bytes 65568 | tf_op jit(solution)/shard_map/ppermute | solution.py:360
  156.3 10.4 %collective-permute-start.30 = (bf16[256,1024]{1,0:T(8,128)(2,1)S(1)}, bf16[256,1024]{1,0:T(8,128)(2,1)S(1)}, u32[]{:S(2)}, u32[]{:S(2)}) collective-permute-start(bf16[256,1024]{1,0:T(8,128)(2,1)S(1)} %get-tuple-element.114), channel_id=1, source_target_pairs={{0,1},{1,0},{2,3},{3,2},{4,5},{5,4},{6,7},{7,6},{8,9},{9,8},{10,11... | collective-permute-start | bytes 1572872 | tf_op jit(solution)/shard_map/ppermute | solution.py:370
  167.0 1.2 collective-permute-done.30.came_ref
  168.2 2.1 %finish.1 = bf16[1024,512]{1,0:T(8,128)(2,1)} custom-call(s32[2]{0:T(128)S(1)} %pad_add_fusion.at_ref, bf16[256,1024]{1,0:T(8,128)(2,1)S(1)} %get-tuple-element.113.own_ref, bf16[256,1024]{1,0:T(8,128)(2,1)S(1)} %collective-permute-done.30.came_ref, f32[1024,1]{1,0:T(8,128)S(1)} %reshape_tile.4.gain_ref), custom_call_target="tpu_custom_call" | custom-call | flops 268435456 | bytes 4194304 | tf_op jit(solution)/shard_map/finish/pallas_call | solution.py:244
  (84 shorter events, 11.7 us)
Async XLA Ops:
  0.0 10.9 %copy-start = (bf16[256,256]{1,0:T(8,128)(2,1)S(1)}, bf16[256,256]{1,0:T(8,128)(2,1)}, u32[]{:S(2)}) copy-start(bf16[256,256]{1,0:T(8,128)(2,1)} %param.13) | copy-start | bytes 393220
  0.0 110.3 %collective-permute-start.20 = (bf16[512,4096]{1,0:T(8,128)(2,1)}, bf16[512,4096]{1,0:T(8,128)(2,1)}, u32[]{:S(2)}, u32[]{:S(2)}) collective-permute-start(bf16[512,4096]{1,0:T(8,128)(2,1)} %bitcast.32), channel_id=1, source_target_pairs={{0,1},{1,0},{2,3},{3,2},{4,5},{5,4},{6,7},{7,6},{8,9},{9,8},{10,11... | collective-permute-start | bytes 12582920 | tf_op jit(solution)/shard_map/ppermute | solution.py:231
  12.5 22.8 %all-to-all-start = ((bf16[16,4,32,256]{3,2,1,0:T(8,128)(2,1)}), bf16[16,4,32,256]{3,2,1,0:T(8,128)(2,1)S(1)}, u32[]{:S(2)}, u32[]{:S(2)}) async-start(bf16[16,4,32,256]{3,2,1,0:T(8,128)(2,1)} %bitcast.8), calls=%async_computation | async-start | bytes 2097152 | tf_op jit(solution)/shard_map/all_to_all | solution.py:240
  17.5 17.6 %copy-start.12 = (bf16[64,32]{0,1:T(8,128)(2,1)S(1)}, bf16[64,32]{0,1:T(8,128)(2,1)}, u32[]{:S(2)}) copy-start(bf16[64,32]{0,1:T(8,128)(2,1)} %param.14) | copy-start | bytes 12292
  17.5 21.6 %copy-start.10 = (f32[2048]{0:T(1024)S(1)}, f32[2048]{0:T(1024)}, u32[]{:S(2)}) copy-start(f32[2048]{0:T(1024)} %param.15) | copy-start | bytes 24580
  19.3 2.0 %collective-permute-start = (bf16[8,256,128]{2,1,0:T(8,128)(2,1)S(1)}, bf16[8,256,128]{2,1,0:T(8,128)(2,1)S(1)}, u32[]{:S(2)}, u32[]{:S(2)}) collective-permute-start(bf16[8,256,128]{2,1,0:T(8,128)(2,1)S(1)} %get-tuple-element.61), channel_id=1, source_target_pairs={{0,1},{1,0},{2,3},{3,2},{4,5},{5,4},{6,7},{7,6},{8,9},{9,8},{10,11... | collective-permute-start | bytes 1572872 | tf_op jit(solution)/shard_map/ppermute | solution.py:265
  21.3 9.3 %collective-permute-start.6 = (bf16[2,256,128]{2,1,0:T(8,128)(2,1)S(1)}, bf16[2,256,128]{2,1,0:T(8,128)(2,1)S(1)}, u32[]{:S(2)}, u32[]{:S(2)}) collective-permute-start(bf16[2,256,128]{2,1,0:T(8,128)(2,1)S(1)} %get-tuple-element.67), channel_id=1, source_target_pairs={{0,2},{2,4},{4,6},{6,8},{8,10},{10,12},{12,14},{14,0},{1,3},{3,5},... | collective-permute-start | bytes 393224 | tf_op jit(solution)/shard_map/ppermute | solution.py:269
  23.0 8.1 %collective-permute-start.7 = (bf16[2,256,128]{2,1,0:T(8,128)(2,1)S(1)}, bf16[2,256,128]{2,1,0:T(8,128)(2,1)S(1)}, u32[]{:S(2)}, u32[]{:S(2)}) collective-permute-start(bf16[2,256,128]{2,1,0:T(8,128)(2,1)S(1)} %get-tuple-element.68), channel_id=1, source_target_pairs={{0,14},{2,0},{4,2},{6,4},{8,6},{10,8},{12,10},{14,12},{1,15},{3,1}... | collective-permute-start | bytes 393224 | tf_op jit(solution)/shard_map/ppermute | solution.py:269
  27.1 9.1 %collective-permute-start.2 = (bf16[2,256,128]{2,1,0:T(8,128)(2,1)S(1)}, bf16[2,256,128]{2,1,0:T(8,128)(2,1)S(1)}, u32[]{:S(2)}, u32[]{:S(2)}) collective-permute-start(bf16[2,256,128]{2,1,0:T(8,128)(2,1)S(1)} %get-tuple-element.63), channel_id=1, source_target_pairs={{0,4},{2,6},{4,8},{6,10},{8,12},{10,14},{12,0},{14,2},{1,5},{3,7},... | collective-permute-start | bytes 393224 | tf_op jit(solution)/shard_map/ppermute | solution.py:269
  27.1 15.2 %collective-permute-start.3 = (bf16[2,256,128]{2,1,0:T(8,128)(2,1)S(1)}, bf16[2,256,128]{2,1,0:T(8,128)(2,1)S(1)}, u32[]{:S(2)}, u32[]{:S(2)}) collective-permute-start(bf16[2,256,128]{2,1,0:T(8,128)(2,1)S(1)} %get-tuple-element.64), channel_id=1, source_target_pairs={{0,12},{2,14},{4,0},{6,2},{8,4},{10,6},{12,8},{14,10},{1,13},{3,15... | collective-permute-start | bytes 393224 | tf_op jit(solution)/shard_map/ppermute | solution.py:269
  30.6 19.9 %collective-permute-start.4 = (bf16[2,256,128]{2,1,0:T(8,128)(2,1)S(1)}, bf16[2,256,128]{2,1,0:T(8,128)(2,1)S(1)}, u32[]{:S(2)}, u32[]{:S(2)}) collective-permute-start(bf16[2,256,128]{2,1,0:T(8,128)(2,1)S(1)} %get-tuple-element.65), channel_id=1, source_target_pairs={{0,6},{2,8},{4,10},{6,12},{8,14},{10,0},{12,2},{14,4},{1,7},{3,9},... | collective-permute-start | bytes 393224 | tf_op jit(solution)/shard_map/ppermute | solution.py:269
  31.2 19.4 %collective-permute-start.5 = (bf16[2,256,128]{2,1,0:T(8,128)(2,1)S(1)}, bf16[2,256,128]{2,1,0:T(8,128)(2,1)S(1)}, u32[]{:S(2)}, u32[]{:S(2)}) collective-permute-start(bf16[2,256,128]{2,1,0:T(8,128)(2,1)S(1)} %get-tuple-element.66), channel_id=1, source_target_pairs={{0,10},{2,12},{4,14},{6,0},{8,2},{10,4},{12,6},{14,8},{1,11},{3,13... | collective-permute-start | bytes 393224 | tf_op jit(solution)/shard_map/ppermute | solution.py:269
  36.1 62.8 %collective-permute-start.17 = (bf16[2048,256]{1,0:T(8,128)(2,1)}, bf16[2048,256]{1,0:T(8,128)(2,1)}, u32[]{:S(2)}, u32[]{:S(2)}) collective-permute-start(bf16[2048,256]{1,0:T(8,128)(2,1)} %refs_9_.1), channel_id=1, source_target_pairs={{0,1},{1,0},{2,3},{3,2},{4,5},{5,4},{6,7},{7,6},{8,9},{9,8},{10,11... | collective-permute-start | bytes 3145736 | tf_op jit(solution)/shard_map/ppermute | solution.py:229
  42.2 15.0 %collective-permute-start.1 = (bf16[2,256,128]{2,1,0:T(8,128)(2,1)S(1)}, bf16[2,256,128]{2,1,0:T(8,128)(2,1)S(1)}, u32[]{:S(2)}, u32[]{:S(2)}) collective-permute-start(bf16[2,256,128]{2,1,0:T(8,128)(2,1)S(1)} %get-tuple-element.62), channel_id=1, source_target_pairs={{0,8},{2,10},{4,12},{6,14},{8,0},{10,2},{12,4},{14,6},{1,9},{3,11}... | collective-permute-start | bytes 393224 | tf_op jit(solution)/shard_map/ppermute | solution.py:269
  50.5 6.7 %collective-permute-start.8 = (bf16[32,2048]{1,0:T(8,128)(2,1)S(1)}, bf16[32,2048]{1,0:T(8,128)(2,1)S(1)}, u32[]{:S(2)}, u32[]{:S(2)}) collective-permute-start(bf16[32,2048]{1,0:T(8,128)(2,1)S(1)} %fm_rows.1), channel_id=1, source_target_pairs={{0,0},{1,16},{2,32},{3,48},{4,64},{5,80},{6,96},{7,112},{8,128},{9... | collective-permute-start | bytes 393224 | tf_op jit(solution)/shard_map/ppermute | solution.py:293
  57.2 18.0 %collective-permute-start.12 = (bf16[32,2048]{1,0:T(8,128)(2,1)S(1)}, bf16[32,2048]{1,0:T(8,128)(2,1)S(1)}, u32[]{:S(2)}, u32[]{:S(2)}) collective-permute-start(bf16[32,2048]{1,0:T(8,128)(2,1)S(1)} %collective-permute-done.8.refs_0_), channel_id=1, source_target_pairs={{0,14},{2,0},{4,2},{6,4},{8,6},{10,8},{12,10},{14,12},{1,15},{3,1}... | collective-permute-start | bytes 393224 | tf_op jit(solution)/shard_map/ppermute | solution.py:216
  73.3 5.0 %collective-permute-start.9 = (bf16[32,2048]{1,0:T(8,128)(2,1)S(1)}, bf16[32,2048]{1,0:T(8,128)(2,1)S(1)}, u32[]{:S(2)}, u32[]{:S(2)}) collective-permute-start(bf16[32,2048]{1,0:T(8,128)(2,1)S(1)} %collective-permute-done.8.refs_0_), channel_id=1, source_target_pairs={{0,2},{2,4},{4,6},{6,8},{8,10},{10,12},{12,14},{14,0},{1,3},{3,5},... | collective-permute-start | bytes 393224 | tf_op jit(solution)/shard_map/ppermute | solution.py:216
  73.3 0.6 copy-start.4
  75.3 10.0 %copy-start.6 = (bf16[32,2048]{1,0:T(8,128)(2,1)}, bf16[32,2048]{1,0:T(8,128)(2,1)S(1)}, u32[]{:S(2)}) copy-start(bf16[32,2048]{1,0:T(8,128)(2,1)S(1)} %collective-permute-done.12.refs_4_) | copy-start | bytes 393220
  78.4 6.8 %copy-start.8 = (bf16[32,2048]{1,0:T(8,128)(2,1)}, bf16[32,2048]{1,0:T(8,128)(2,1)S(1)}, u32[]{:S(2)}) copy-start(bf16[32,2048]{1,0:T(8,128)(2,1)S(1)} %collective-permute-done.9.refs_1_) | copy-start | bytes 393220
  78.4 20.0 %copy-start.11 = (bf16[32,64]{1,0:T(8,128)(2,1)S(1)}, bf16[32,64]{1,0:T(8,128)(2,1)}, u32[]{:S(2)}) copy-start(bf16[32,64]{1,0:T(8,128)(2,1)} %lcb_ref.1) | copy-start | bytes 12292
  80.0 20.2 %copy-start.3 = (bf16[2048,256]{1,0:T(8,128)(2,1)S(1)}, bf16[2048,256]{1,0:T(8,128)(2,1)}, u32[]{:S(2)}) copy-start(bf16[2048,256]{1,0:T(8,128)(2,1)} %refs_9_.1) | copy-start | bytes 3145732
  80.0 28.3 %all-to-all-start.1 = ((bf16[16,256,128]{2,1,0:T(8,128)(2,1)}), bf16[16,256,128]{2,1,0:T(8,128)(2,1)S(1)}, u32[]{:S(2)}, u32[]{:S(2)}) async-start(bf16[16,256,128]{2,1,0:T(8,128)(2,1)} %pack.1), calls=%async_computation.1 | async-start | bytes 2097152 | tf_op jit(solution)/shard_map/all_to_all | solution.py:302
  85.2 5.1 %collective-permute-start.10 = (bf16[32,2048]{1,0:T(8,128)(2,1)S(1)}, bf16[32,2048]{1,0:T(8,128)(2,1)S(1)}, u32[]{:S(2)}, u32[]{:S(2)}) collective-permute-start(bf16[32,2048]{1,0:T(8,128)(2,1)S(1)} %collective-permute-done.9.refs_1_), channel_id=1, source_target_pairs={{0,2},{2,4},{4,6},{6,8},{8,10},{10,12},{12,14},{14,0},{1,3},{3,5},... | collective-permute-start | bytes 393224 | tf_op jit(solution)/shard_map/ppermute | solution.py:216
  85.3 5.0 %collective-permute-start.13 = (bf16[32,2048]{1,0:T(8,128)(2,1)S(1)}, bf16[32,2048]{1,0:T(8,128)(2,1)S(1)}, u32[]{:S(2)}, u32[]{:S(2)}) collective-permute-start(bf16[32,2048]{1,0:T(8,128)(2,1)S(1)} %collective-permute-done.12.refs_4_), channel_id=1, source_target_pairs={{0,14},{2,0},{4,2},{6,4},{8,6},{10,8},{12,10},{14,12},{1,15},{3,1}... | collective-permute-start | bytes 393224 | tf_op jit(solution)/shard_map/ppermute | solution.py:216
  90.3 5.3 %collective-permute-start.11 = (bf16[32,2048]{1,0:T(8,128)(2,1)S(1)}, bf16[32,2048]{1,0:T(8,128)(2,1)S(1)}, u32[]{:S(2)}, u32[]{:S(2)}) collective-permute-start(bf16[32,2048]{1,0:T(8,128)(2,1)S(1)} %collective-permute-done.10.refs_2_), channel_id=1, source_target_pairs={{0,2},{2,4},{4,6},{6,8},{8,10},{10,12},{12,14},{14,0},{1,3},{3,5},... | collective-permute-start | bytes 393224 | tf_op jit(solution)/shard_map/ppermute | solution.py:216
  90.3 5.3 %collective-permute-start.14 = (bf16[32,2048]{1,0:T(8,128)(2,1)S(1)}, bf16[32,2048]{1,0:T(8,128)(2,1)S(1)}, u32[]{:S(2)}, u32[]{:S(2)}) collective-permute-start(bf16[32,2048]{1,0:T(8,128)(2,1)S(1)} %collective-permute-done.13.refs_5_), channel_id=1, source_target_pairs={{0,14},{2,0},{4,2},{6,4},{8,6},{10,8},{12,10},{14,12},{1,15},{3,1}... | collective-permute-start | bytes 393224 | tf_op jit(solution)/shard_map/ppermute | solution.py:216
  95.6 4.6 %collective-permute-start.15 = (bf16[16,2048]{1,0:T(8,128)(2,1)S(1)}, bf16[16,2048]{1,0:T(8,128)(2,1)S(1)}, u32[]{:S(2)}, u32[]{:S(2)}) collective-permute-start(bf16[16,2048]{1,0:T(8,128)(2,1)S(1)} %slice.16), channel_id=1, source_target_pairs={{0,2},{2,4},{4,6},{6,8},{8,10},{10,12},{12,14},{14,0},{1,3},{3,5},... | collective-permute-start | bytes 196616 | tf_op jit(solution)/shard_map/ppermute | solution.py:216
  95.6 4.5 %collective-permute-start.16 = (bf16[16,2048]{1,0:T(8,128)(2,1)S(1)}, bf16[16,2048]{1,0:T(8,128)(2,1)S(1)}, u32[]{:S(2)}, u32[]{:S(2)}) collective-permute-start(bf16[16,2048]{1,0:T(8,128)(2,1)S(1)} %slice.17), channel_id=1, source_target_pairs={{0,14},{2,0},{4,2},{6,4},{8,6},{10,8},{12,10},{14,12},{1,15},{3,1}... | collective-permute-start | bytes 196616 | tf_op jit(solution)/shard_map/ppermute | solution.py:216
  100.2 0.9 copy-start.5
  101.1 0.9 copy-start.7
  102.0 0.9 copy-start.9
  104.9 10.0 %collective-permute-start.18 = (bf16[256,512]{1,0:T(8,128)(2,1)S(1)}, bf16[256,512]{1,0:T(8,128)(2,1)S(1)}, u32[]{:S(2)}, u32[]{:S(2)}) collective-permute-start(bf16[256,512]{1,0:T(8,128)(2,1)S(1)} %hidden.1.refs_0_), channel_id=1, source_target_pairs={{0,2},{2,4},{4,6},{6,8},{8,10},{10,12},{12,14},{14,0},{1,3},{3,5},... | collective-permute-start | bytes 786440 | tf_op jit(solution)/shard_map/ppermute | solution.py:216
  105.0 9.9 %collective-permute-start.19 = (bf16[256,512]{1,0:T(8,128)(2,1)S(1)}, bf16[256,512]{1,0:T(8,128)(2,1)S(1)}, u32[]{:S(2)}, u32[]{:S(2)}) collective-permute-start(bf16[256,512]{1,0:T(8,128)(2,1)S(1)} %hidden.1.refs_0_), channel_id=1, source_target_pairs={{0,14},{2,0},{4,2},{6,4},{8,6},{10,8},{12,10},{14,12},{1,15},{3,1}... | collective-permute-start | bytes 786440 | tf_op jit(solution)/shard_map/ppermute | solution.py:216
  110.3 2.2 %copy-start.1 = (bf16[4096,32,16]{0,2,1:T(8,128)(2,1)S(1)}, bf16[4096,32,16]{0,2,1:T(8,128)(2,1)}, u32[]{:S(2)}) copy-start(bf16[4096,32,16]{0,2,1:T(8,128)(2,1)} %param.17) | copy-start | bytes 12582916
  112.5 5.2 %copy-start.2 = (bf16[4096,32,16]{0,2,1:T(8,128)(2,1)S(1)}, bf16[4096,32,16]{0,2,1:T(8,128)(2,1)}, u32[]{:S(2)}) copy-start(bf16[4096,32,16]{0,2,1:T(8,128)(2,1)} %param.17) | copy-start | bytes 12582916
  114.9 6.5 %collective-permute-start.21 = (bf16[256,512]{1,0:T(8,128)(2,1)S(1)}, bf16[256,512]{1,0:T(8,128)(2,1)S(1)}, u32[]{:S(2)}, u32[]{:S(2)}) collective-permute-start(bf16[256,512]{1,0:T(8,128)(2,1)S(1)} %collective-permute-done.18.refs_0_), channel_id=1, source_target_pairs={{0,2},{2,4},{4,6},{6,8},{8,10},{10,12},{12,14},{14,0},{1,3},{3,5},... | collective-permute-start | bytes 786440 | tf_op jit(solution)/shard_map/ppermute | solution.py:216
  115.0 6.4 %collective-permute-start.22 = (bf16[256,512]{1,0:T(8,128)(2,1)S(1)}, bf16[256,512]{1,0:T(8,128)(2,1)S(1)}, u32[]{:S(2)}, u32[]{:S(2)}) collective-permute-start(bf16[256,512]{1,0:T(8,128)(2,1)S(1)} %collective-permute-done.19.refs_1_), channel_id=1, source_target_pairs={{0,14},{2,0},{4,2},{6,4},{8,6},{10,8},{12,10},{14,12},{1,15},{3,1}... | collective-permute-start | bytes 786440 | tf_op jit(solution)/shard_map/ppermute | solution.py:216
  121.4 8.3 %collective-permute-start.23 = (bf16[256,512]{1,0:T(8,128)(2,1)S(1)}, bf16[256,512]{1,0:T(8,128)(2,1)S(1)}, u32[]{:S(2)}, u32[]{:S(2)}) collective-permute-start(bf16[256,512]{1,0:T(8,128)(2,1)S(1)} %collective-permute-done.21.refs_0_), channel_id=1, source_target_pairs={{0,2},{2,4},{4,6},{6,8},{8,10},{10,12},{12,14},{14,0},{1,3},{3,5},... | collective-permute-start | bytes 786440 | tf_op jit(solution)/shard_map/ppermute | solution.py:216
  121.4 8.3 %collective-permute-start.24 = (bf16[256,512]{1,0:T(8,128)(2,1)S(1)}, bf16[256,512]{1,0:T(8,128)(2,1)S(1)}, u32[]{:S(2)}, u32[]{:S(2)}) collective-permute-start(bf16[256,512]{1,0:T(8,128)(2,1)S(1)} %collective-permute-done.22.refs_1_), channel_id=1, source_target_pairs={{0,14},{2,0},{4,2},{6,4},{8,6},{10,8},{12,10},{14,12},{1,15},{3,1}... | collective-permute-start | bytes 786440 | tf_op jit(solution)/shard_map/ppermute | solution.py:216
  129.7 7.0 %collective-permute-start.25 = (bf16[128,512]{1,0:T(8,128)(2,1)S(1)}, bf16[128,512]{1,0:T(8,128)(2,1)S(1)}, u32[]{:S(2)}, u32[]{:S(2)}) collective-permute-start(bf16[128,512]{1,0:T(8,128)(2,1)S(1)} %slice.14), channel_id=1, source_target_pairs={{0,2},{2,4},{4,6},{6,8},{8,10},{10,12},{12,14},{14,0},{1,3},{3,5},... | collective-permute-start | bytes 393224 | tf_op jit(solution)/shard_map/ppermute | solution.py:216
  129.8 6.9 %collective-permute-start.26 = (bf16[128,512]{1,0:T(8,128)(2,1)S(1)}, bf16[128,512]{1,0:T(8,128)(2,1)S(1)}, u32[]{:S(2)}, u32[]{:S(2)}) collective-permute-start(bf16[128,512]{1,0:T(8,128)(2,1)S(1)} %slice.15), channel_id=1, source_target_pairs={{0,14},{2,0},{4,2},{6,4},{8,6},{10,8},{12,10},{14,12},{1,15},{3,1}... | collective-permute-start | bytes 393224 | tf_op jit(solution)/shard_map/ppermute | solution.py:216
  139.5 27.2 %copy-start.13 = (f32[16]{0:T(128)S(1)}, f32[16]{0:T(128)}, u32[]{:S(2)}) copy-start(f32[16]{0:T(128)} %param.19) | copy-start | bytes 196
  139.5 3.9 %collective-permute-start.27 = (bf16[128,256]{1,0:T(8,128)(2,1)S(1)}, bf16[128,256]{1,0:T(8,128)(2,1)S(1)}, u32[]{:S(2)}, u32[]{:S(2)}) collective-permute-start(bf16[128,256]{1,0:T(8,128)(2,1)S(1)} %convert_element_type.48), channel_id=1, source_target_pairs={{0,2},{2,0},{4,6},{6,4},{8,10},{10,8},{12,14},{14,12},{1,3},{3,1},... | collective-permute-start | bytes 196616 | tf_op jit(solution)/shard_map/ppermute | solution.py:360
  143.5 4.8 %collective-permute-start.28 = (bf16[128,256]{1,0:T(8,128)(2,1)S(1)}, bf16[128,256]{1,0:T(8,128)(2,1)S(1)}, u32[]{:S(2)}, u32[]{:S(2)}) collective-permute-start(bf16[128,256]{1,0:T(8,128)(2,1)S(1)} %fusion.9), channel_id=1, source_target_pairs={{0,4},{2,6},{4,0},{6,2},{8,12},{10,14},{12,8},{14,10},{1,5},{3,7},... | collective-permute-start | bytes 196616 | tf_op jit(solution)/shard_map/ppermute | solution.py:360
  148.3 7.1 %collective-permute-start.29 = (bf16[128,256]{1,0:T(8,128)(2,1)S(1)}, bf16[128,256]{1,0:T(8,128)(2,1)S(1)}, u32[]{:S(2)}, u32[]{:S(2)}) collective-permute-start(bf16[128,256]{1,0:T(8,128)(2,1)S(1)} %fusion.10), channel_id=1, source_target_pairs={{0,8},{2,10},{4,12},{6,14},{8,0},{10,2},{12,4},{14,6},{1,9},{3,11}... | collective-permute-start | bytes 196616 | tf_op jit(solution)/shard_map/ppermute | solution.py:360
  156.3 11.9 %collective-permute-start.30 = (bf16[256,1024]{1,0:T(8,128)(2,1)S(1)}, bf16[256,1024]{1,0:T(8,128)(2,1)S(1)}, u32[]{:S(2)}, u32[]{:S(2)}) collective-permute-start(bf16[256,1024]{1,0:T(8,128)(2,1)S(1)} %get-tuple-element.114), channel_id=1, source_target_pairs={{0,1},{1,0},{2,3},{3,2},{4,5},{5,4},{6,7},{7,6},{8,9},{9,8},{10,11... | collective-permute-start | bytes 1572872 | tf_op jit(solution)/shard_map/ppermute | solution.py:370

commit v4 on v3

--- a/solution.py
+++ b/solution.py
@@ -237,7 +237,9 @@
     encoded = jnp.dot(pooled.reshape(-1, full_width), enc_weight, preferred_element_type=F32)
     session = encoded.reshape(users_enc, sess_dev, full_width).astype(BF)
     chunks = jnp.transpose(session.reshape(2, Z, U, sess_dev, D), (1, 0, 3, 2, 4))
-    x = lax.all_to_all(chunks.reshape(16, sess_dev, U, D), "dp", 0, 0, tiled=True)
+    chunks = chunks.reshape(16, sess_dev, U, D)
+    chunks = lax.dynamic_slice_in_dim(jnp.concatenate([chunks, chunks], axis=0), 2 * z + c, 16)
+    x = lax.all_to_all(chunks, "dp", 0, 0, tiled=True)
     x = x.reshape(N * U, D)
 
     def call(kernel, name, shapes, args, scratch=(), scalars=(place,), flops=2**28):
@@ -293,7 +295,7 @@
     normed = lax.ppermute(
         normed,
         ("dp", "emb", "section"),
-        [(a * 16 + b, b * 16 + a) for a in range(16) for b in range(16)],
+        [(a * 16 + b, b * 16 + (a + b) % 16) for a in range(16) for b in range(16)],
     )
     normed = arrived(normed, (4,))
     up1, down1 = step(normed, normed)

time: 171 us -> 171 us (level)
  waiting for transfers between devices: 36.9 us -> 32.1 us
  starting transfers between devices: 90.7 us -> 94.5 us
    ppermute x16, starting transfers between devices: 36 us -> 26.9 us  [step(): return (lax.ppermute(up, 'emb', UP), lax.ppermute(down, 'emb', DOWN))]
    all_to_all x1, starting transfers between devices: 5.18 us -> 10.8 us  [shards(): slices = lax.all_to_all(packed, 'dp', 0, 0, tiled=True)]
    ppermute x3, starting transfers between devices: 1.64 us -> 5.9 us  [shards(): lax.ppermute(totals.astype(BF), 'emb', [(i, i ^ bit) for i in range(Z)])]
    ppermute x3, waiting for transfers between devices: 14.2 us -> 10 us  [shards(): lax.ppermute(totals.astype(BF), 'emb', [(i, i ^ bit) for i in range(Z)])]
    ppermute x2, starting transfers between devices: 10.8 us -> 14.1 us  [shards(): other = lax.ppermute(other, 'section', SWAP)]
  transfers between devices with their start and end apart: 33 -> 33, of which waited for: 15 -> 16; matrix products, arithmetic and copies ran while one was open for 6% -> 7% of each run, Pallas kernels for 12% -> 13%
where the time goes in v4:
time: 171 us; the launch traced here: 170 us
  starting transfers between devices  94.5 us (55%)
  waiting for transfers between devices  32.1 us (19%)
  Pallas kernels  27.3 us (16%)
  local copies, waits for them, and re-layouts  7.06 us (4%)
  matrix products  5.23 us (3%)
  other arithmetic  3.87 us (2%)
    ppermute x16, starting transfers between devices, step(): return (lax.ppermute(up, 'emb', UP), lax.ppermute(down, 'emb', DOWN))  26.9 us
    ppermute x7, starting transfers between devices, shards(): lax.ppermute(slices[k], 'emb', [(i, (i + k) % Z) for i in range(Z)])  21.8 us
    ppermute x16, waiting for transfers between devices, step(): return (lax.ppermute(up, 'emb', UP), lax.ppermute(down, 'emb', DOWN))  16.1 us
    ppermute x2, starting transfers between devices, shards(): other = lax.ppermute(other, 'section', SWAP)  14.1 us
    pallas_call x8, Pallas kernels, call(): pl.pallas_call(kernel, out_shape=[jax.ShapeDtypeStruct(*v) for v in shape...  12.5 us
    all_to_all x1, starting transfers between devices, shards(): slices = lax.all_to_all(packed, 'dp', 0, 0, tiled=True)  10.8 us
    pallas_call x4, Pallas kernels, part(): pl.pallas_call(functools.partial(part_kernel, n), grid_spec=pltpu.Prefetc...  10 us
    ppermute x3, waiting for transfers between devices, shards(): lax.ppermute(totals.astype(BF), 'emb', [(i, i ^ bit) for i in range(Z)])  10 us
  transfers between devices with their start and end apart: 33, of which 16 were waited for; matrix products, arithmetic and copies ran while one was open for 7% of the time, Pallas kernels for 13%

profile of v4, /device:TPU:1, one launch (start us, length us, event | category | flops | bytes accessed | tf_op | source)
XLA Modules:
  0.0 170.4 jit_solution(16564852743505151562)
XLA Ops:
  0.0 3.2 %collective-permute-start.20 = (bf16[512,4096]{1,0:T(8,128)(2,1)}, bf16[512,4096]{1,0:T(8,128)(2,1)}, u32[]{:S(2)}, u32[]{:S(2)}) collective-permute-start(bf16[512,4096]{1,0:T(8,128)(2,1)} %bitcast.32), channel_id=1, source_target_pairs={{0,1},{1,0},{2,3},{3,2},{4,5},{5,4},{6,7},{7,6},{8,9},{9,8},{10,11... | collective-permute-start | bytes 12582920 | tf_op jit(solution)/shard_map/ppermute | solution.py:231
  4.8 1.3 fusion.6
  6.2 4.7 %fusion = f32[512,4,1,256]{3,2,1,0:T(1,128)S(1)} fusion(bf16[512,4,4,256]{3,2,1,0:T(4,128)(2,1)} %param.10, pred[512,4,4,1]{2,1,0,3:T(4,128)(4,1)S(1)} %fusion.6), kind=kOutput, calls=%fused_computation | convolution fusion | flops 4194304 | bytes 6299648 | tf_op jit(solution)/shard_map/usj,usjd->usd/dot_general | solution.py:234
  11.5 1.4 fusion.4
  12.9 5.0 %all-to-all-start = ((bf16[16,4,32,256]{3,2,1,0:T(8,128)(2,1)}), bf16[16,4,32,256]{3,2,1,0:T(8,128)(2,1)S(1)}, u32[]{:S(2)}, u32[]{:S(2)}) async-start(bf16[16,4,32,256]{3,2,1,0:T(8,128)(2,1)} %fusion.4), calls=%async_computation | async-start | bytes 2097152 | tf_op jit(solution)/shard_map/all_to_all | solution.py:242
  18.2 1.5 cut.1
  20.1 1.6 collective-permute-done.other_ref
  22.4 1.6 collective-permute-start.6
  24.1 3.9 %collective-permute-start.7 = (bf16[2,256,128]{2,1,0:T(8,128)(2,1)S(1)}, bf16[2,256,128]{2,1,0:T(8,128)(2,1)S(1)}, u32[]{:S(2)}, u32[]{:S(2)}) collective-permute-start(bf16[2,256,128]{2,1,0:T(8,128)(2,1)S(1)} %get-tuple-element.68), channel_id=1, source_target_pairs={{0,14},{2,0},{4,2},{6,4},{8,6},{10,8},{12,10},{14,12},{1,15},{3,1}... | collective-permute-start | bytes 393224 | tf_op jit(solution)/shard_map/ppermute | solution.py:271
  28.0 3.6 %collective-permute-start.3 = (bf16[2,256,128]{2,1,0:T(8,128)(2,1)S(1)}, bf16[2,256,128]{2,1,0:T(8,128)(2,1)S(1)}, u32[]{:S(2)}, u32[]{:S(2)}) collective-permute-start(bf16[2,256,128]{2,1,0:T(8,128)(2,1)S(1)} %get-tuple-element.64), channel_id=1, source_target_pairs={{0,12},{2,14},{4,0},{6,2},{8,4},{10,6},{12,8},{14,10},{1,13},{3,15... | collective-permute-start | bytes 393224 | tf_op jit(solution)/shard_map/ppermute | solution.py:271
  32.2 3.9 %collective-permute-start.5 = (bf16[2,256,128]{2,1,0:T(8,128)(2,1)}, bf16[2,256,128]{2,1,0:T(8,128)(2,1)S(1)}, u32[]{:S(2)}, u32[]{:S(2)}) collective-permute-start(bf16[2,256,128]{2,1,0:T(8,128)(2,1)} %get-tuple-element.66), channel_id=1, source_target_pairs={{0,10},{2,12},{4,14},{6,0},{8,2},{10,4},{12,6},{14,8},{1,11},{3,13... | collective-permute-start | bytes 393224 | tf_op jit(solution)/shard_map/ppermute | solution.py:271
  37.2 3.1 %collective-permute-start.17 = (bf16[2048,256]{1,0:T(8,128)(2,1)S(1)}, bf16[2048,256]{1,0:T(8,128)(2,1)}, u32[]{:S(2)}, u32[]{:S(2)}) collective-permute-start(bf16[2048,256]{1,0:T(8,128)(2,1)S(1)} %copy-done.3), channel_id=1, source_target_pairs={{0,1},{1,0},{2,3},{3,2},{4,5},{5,4},{6,7},{7,6},{8,9},{9,8},{10,11... | collective-permute-start | bytes 3145736 | tf_op jit(solution)/shard_map/ppermute | solution.py:229
  40.3 3.1 %fm_rows.1 = bf16[32,2048]{1,0:T(8,128)(2,1)S(1)} custom-call(bf16[2048,256]{1,0:T(8,128)(2,1)S(1)} %bitcast.43, bf16[32,64]{1,0:T(8,128)(2,1)S(1)} %copy.18.proj_ref, f32[16,128]{1,0:T(8,128)S(1)} %bitcast.44), custom_call_target="tpu_custom_call" | custom-call | flops 268435456 | bytes 4194304 | tf_op jit(solution)/shard_map/fm_rows/pallas_call | solution.py:246
  43.4 8.2 %collective-permute-start.1 = (bf16[2,256,128]{2,1,0:T(8,128)(2,1)}, bf16[2,256,128]{2,1,0:T(8,128)(2,1)S(1)}, u32[]{:S(2)}, u32[]{:S(2)}) collective-permute-start(bf16[2,256,128]{2,1,0:T(8,128)(2,1)} %copy-done.12), channel_id=1, source_target_pairs={{0,8},{2,10},{4,12},{6,14},{8,0},{10,2},{12,4},{14,6},{1,9},{3,11}... | collective-permute-start | bytes 393224 | tf_op jit(solution)/shard_map/ppermute | solution.py:271
  51.6 3.6 %collective-permute-start.8 = (bf16[32,2048]{1,0:T(8,128)(2,1)S(1)}, bf16[32,2048]{1,0:T(8,128)(2,1)S(1)}, u32[]{:S(2)}, u32[]{:S(2)}) collective-permute-start(bf16[32,2048]{1,0:T(8,128)(2,1)S(1)} %fm_rows.1), channel_id=1, source_target_pairs={{0,0},{1,17},{2,34},{3,51},{4,68},{5,85},{6,102},{7,119},{8,136},{... | collective-permute-start | bytes 393224 | tf_op jit(solution)/shard_map/ppermute | solution.py:295
  55.2 3.0 %collective-permute-done.1.refs_4_ = bf16[2,256,128]{2,1,0:T(8,128)(2,1)S(1)} collective-permute-done((bf16[2,256,128]{2,1,0:T(8,128)(2,1)}, bf16[2,256,128]{2,1,0:T(8,128)(2,1)S(1)}, u32[]{:S(2)}, u32[]{:S(2)}) %collective-permute-start.1) | collective-permute-done | bytes 131104 | tf_op jit(solution)/shard_map/ppermute | solution.py:271
  58.1 6.8 %collective-permute-start.12 = (bf16[32,2048]{1,0:T(8,128)(2,1)S(1)}, bf16[32,2048]{1,0:T(8,128)(2,1)S(1)}, u32[]{:S(2)}, u32[]{:S(2)}) collective-permute-start(bf16[32,2048]{1,0:T(8,128)(2,1)S(1)} %collective-permute-done.8.refs_0_), channel_id=1, source_target_pairs={{0,14},{2,0},{4,2},{6,4},{8,6},{10,8},{12,10},{14,12},{1,15},{3,1}... | collective-permute-start | bytes 393224 | tf_op jit(solution)/shard_map/ppermute | solution.py:216
  64.9 2.9 %collective-permute-done.12.refs_4_ = bf16[32,2048]{1,0:T(8,128)(2,1)S(1)} collective-permute-done((bf16[32,2048]{1,0:T(8,128)(2,1)S(1)}, bf16[32,2048]{1,0:T(8,128)(2,1)S(1)}, u32[]{:S(2)}, u32[]{:S(2)}) %collective-permute-start.12) | collective-permute-done | bytes 131104 | tf_op jit(solution)/shard_map/ppermute | solution.py:216
  67.8 2.1 %collective-permute-done.9.refs_1_ = bf16[32,2048]{1,0:T(8,128)(2,1)S(1)} collective-permute-done((bf16[32,2048]{1,0:T(8,128)(2,1)S(1)}, bf16[32,2048]{1,0:T(8,128)(2,1)S(1)}, u32[]{:S(2)}, u32[]{:S(2)}) %collective-permute-start.9) | collective-permute-done | bytes 131104 | tf_op jit(solution)/shard_map/ppermute | solution.py:216
  70.0 1.6 pack.1
  71.5 10.8 %all-to-all-start.1 = ((bf16[16,256,128]{2,1,0:T(8,128)(2,1)}), bf16[16,256,128]{2,1,0:T(8,128)(2,1)S(1)}, u32[]{:S(2)}, u32[]{:S(2)}) async-start(bf16[16,256,128]{2,1,0:T(8,128)(2,1)} %pack.1), calls=%async_computation.1 | async-start | bytes 2097152 | tf_op jit(solution)/shard_map/all_to_all | solution.py:304
  82.7 2.4 %collective-permute-start.13 = (bf16[32,2048]{1,0:T(8,128)(2,1)S(1)}, bf16[32,2048]{1,0:T(8,128)(2,1)S(1)}, u32[]{:S(2)}, u32[]{:S(2)}) collective-permute-start(bf16[32,2048]{1,0:T(8,128)(2,1)S(1)} %collective-permute-done.12.refs_4_), channel_id=1, source_target_pairs={{0,14},{2,0},{4,2},{6,4},{8,6},{10,8},{12,10},{14,12},{1,15},{3,1}... | collective-permute-start | bytes 393224 | tf_op jit(solution)/shard_map/ppermute | solution.py:216
  85.1 2.3 %collective-permute-done.10.refs_2_ = bf16[32,2048]{1,0:T(8,128)(2,1)S(1)} collective-permute-done((bf16[32,2048]{1,0:T(8,128)(2,1)S(1)}, bf16[32,2048]{1,0:T(8,128)(2,1)S(1)}, u32[]{:S(2)}, u32[]{:S(2)}) %collective-permute-start.10) | collective-permute-done | bytes 131104 | tf_op jit(solution)/shard_map/ppermute | solution.py:216
  87.4 3.0 %collective-permute-start.14 = (bf16[32,2048]{1,0:T(8,128)(2,1)S(1)}, bf16[32,2048]{1,0:T(8,128)(2,1)S(1)}, u32[]{:S(2)}, u32[]{:S(2)}) collective-permute-start(bf16[32,2048]{1,0:T(8,128)(2,1)S(1)} %collective-permute-done.13.refs_5_), channel_id=1, source_target_pairs={{0,14},{2,0},{4,2},{6,4},{8,6},{10,8},{12,10},{14,12},{1,15},{3,1}... | collective-permute-start | bytes 393224 | tf_op jit(solution)/shard_map/ppermute | solution.py:216
  90.4 2.3 %collective-permute-done.11.refs_3_ = bf16[32,2048]{1,0:T(8,128)(2,1)S(1)} collective-permute-done((bf16[32,2048]{1,0:T(8,128)(2,1)S(1)}, bf16[32,2048]{1,0:T(8,128)(2,1)S(1)}, u32[]{:S(2)}, u32[]{:S(2)}) %collective-permute-start.11) | collective-permute-done | bytes 131104 | tf_op jit(solution)/shard_map/ppermute | solution.py:216
  92.8 2.9 %collective-permute-start.16 = (bf16[16,2048]{1,0:T(8,128)(2,1)S(1)}, bf16[16,2048]{1,0:T(8,128)(2,1)S(1)}, u32[]{:S(2)}, u32[]{:S(2)}) collective-permute-start(bf16[16,2048]{1,0:T(8,128)(2,1)S(1)} %slice.17), channel_id=1, source_target_pairs={{0,14},{2,0},{4,2},{6,4},{8,6},{10,8},{12,10},{14,12},{1,15},{3,1}... | collective-permute-start | bytes 196616 | tf_op jit(solution)/shard_map/ppermute | solution.py:216
  100.1 2.0 %hidden.1.refs_0_ = bf16[256,512]{1,0:T(8,128)(2,1)S(1)} custom-call(s32[2]{0:T(128)S(1)} %pad_add_fusion.at_ref, bf16[32,2048]{1,0:T(8,128)(2,1)S(1)} %copy-done.5, bf16[32,2048]{1,0:T(8,128)(2,1)S(1)} %copy-done.9, bf16[32,2048]{1,0:T(8,128)(2,1)S(1)} %collective-permute-done.10.refs_2_, bf16[32,2048]{1,0:T(8,128)(2,1)S(1)} %collective-permute-done.11.refs_3_, ...), custom_call_target="tpu_custom_call" | custom-call | tf_op jit(solution)/shard_map/hidden/pallas_call | solution.py:308
  102.2 3.1 %collective-permute-start.19 = (bf16[256,512]{1,0:T(8,128)(2,1)S(1)}, bf16[256,512]{1,0:T(8,128)(2,1)S(1)}, u32[]{:S(2)}, u32[]{:S(2)}) collective-permute-start(bf16[256,512]{1,0:T(8,128)(2,1)S(1)} %hidden.1.refs_0_), channel_id=1, source_target_pairs={{0,14},{2,0},{4,2},{6,4},{8,6},{10,8},{12,10},{14,12},{1,15},{3,1}... | collective-permute-start | bytes 786440 | tf_op jit(solution)/shard_map/ppermute | solution.py:216
  105.5 2.1 %base.1 = (bf16[256,512]{1,0:T(8,128)(2,1)S(1)}, bf16[256,512]{1,0:T(8,128)(2,1)S(1)}, f32[256,512]{1,0:T(8,128)S(1)}, f32[256,512]{1,0:T(8,128)S(1)}, f32[64,256]{1,0:T(8,128)S(1)}) custom-call(s32[2]{0:T(128)S(1)} %pad_add_fusion.at_ref, bf16[16,256,128]{2,1,0:T(8,128)(2,1)S(1)} %all-to-all-done.1.s_ref, bf16[256,256]{1,0:T(8,128)(2,1)S(1)} %fusion.8.perm_ref, ...), custom_call_target="tpu_custom_call" | custom-call | flops 268435456 | bytes 4194304 | tf_op jit(solution)/shard_map/base/pallas_call | solution.py:246
  107.6 2.2 %copy-done.1 = bf16[4096,32,16]{0,2,1:T(8,128)(2,1)S(1)} copy-done((bf16[4096,32,16]{0,2,1:T(8,128)(2,1)S(1)}, bf16[4096,32,16]{0,2,1:T(8,128)(2,1)}, u32[]{:S(2)}) %copy-start.1) | copy-done | bytes 4194328
  109.8 2.4 %fm_out_part.4 = (f32[256,512]{1,0:T(8,128)S(1)}, f32[256,512]{1,0:T(8,128)S(1)}) custom-call(s32[2]{0:T(128)S(1)} %pad_add_fusion.at_ref, bf16[256,512]{1,0:T(8,128)(2,1)S(1)} %hidden.1.refs_0_, bf16[512,4096]{1,0:T(8,128)(2,1)S(1)} %bitcast.33, bf16[512,4096]{1,0:T(8,128)(2,1)} %collective-permute-done.20.refs_2_.refs_3_.refs_5_.w_other), custom_call_target="tpu_custom_call" | custom-call | flops 268435456 | bytes 1048576 | tf_op jit(solution)/shard_map/fm_out_part/pallas_call | solution.py:155
  112.3 2.7 %collective-permute-start.22 = (bf16[256,512]{1,0:T(8,128)(2,1)S(1)}, bf16[256,512]{1,0:T(8,128)(2,1)S(1)}, u32[]{:S(2)}, u32[]{:S(2)}) collective-permute-start(bf16[256,512]{1,0:T(8,128)(2,1)S(1)} %collective-permute-done.19.refs_1_), channel_id=1, source_target_pairs={{0,14},{2,0},{4,2},{6,4},{8,6},{10,8},{12,10},{14,12},{1,15},{3,1}... | collective-permute-start | bytes 786440 | tf_op jit(solution)/shard_map/ppermute | solution.py:216
  114.9 2.5 %fm_out_part.5 = (f32[256,512]{1,0:T(8,128)S(1)}, f32[256,512]{1,0:T(8,128)S(1)}) custom-call(s32[2]{0:T(128)S(1)} %pad_add_fusion.at_ref, bf16[256,512]{1,0:T(8,128)(2,1)S(1)} %collective-permute-done.18.refs_0_, bf16[256,512]{1,0:T(8,128)(2,1)S(1)} %collective-permute-done.19.refs_1_, bf16[512,4096]{1,0:T(8,128)(2,1)S(1)} %bitcast.34, ...), custom_call_target="tpu_custom_call" | custom-call | flops 536870912 | bytes 2097152 | tf_op jit(solution)/shard_map/fm_out_part/pallas_call | solution.py:155
  119.8 1.5 collective-permute-start.24
  121.4 2.5 %fm_out_part.6 = (f32[256,512]{1,0:T(8,128)S(1)}, f32[256,512]{1,0:T(8,128)S(1)}) custom-call(s32[2]{0:T(128)S(1)} %pad_add_fusion.at_ref, bf16[256,512]{1,0:T(8,128)(2,1)S(1)} %collective-permute-done.21.refs_0_, bf16[256,512]{1,0:T(8,128)(2,1)S(1)} %collective-permute-done.22.refs_1_, bf16[512,4096]{1,0:T(8,128)(2,1)S(1)} %bitcast.36, ...), custom_call_target="tpu_custom_call" | custom-call | flops 536870912 | bytes 2097152 | tf_op jit(solution)/shard_map/fm_out_part/pallas_call | solution.py:155
  123.9 3.5 %collective-permute-done.23.refs_0_ = bf16[256,512]{1,0:T(8,128)(2,1)S(1)} collective-permute-done((bf16[256,512]{1,0:T(8,128)(2,1)S(1)}, bf16[256,512]{1,0:T(8,128)(2,1)S(1)}, u32[]{:S(2)}, u32[]{:S(2)}) %collective-permute-start.23) | collective-permute-done | bytes 262176 | tf_op jit(solution)/shard_map/ppermute | solution.py:216
  129.1 1.6 collective-permute-start.26
  130.7 2.5 %fm_out_part.7 = (f32[256,512]{1,0:T(8,128)S(1)}, f32[256,512]{1,0:T(8,128)S(1)}) custom-call(s32[2]{0:T(128)S(1)} %pad_add_fusion.at_ref, bf16[256,512]{1,0:T(8,128)(2,1)S(1)} %collective-permute-done.23.refs_0_, bf16[256,512]{1,0:T(8,128)(2,1)S(1)} %collective-permute-done.24.refs_1_, bf16[512,4096]{1,0:T(8,128)(2,1)S(1)} %bitcast.38, ...), custom_call_target="tpu_custom_call" | custom-call | flops 536870912 | bytes 2097152 | tf_op jit(solution)/shard_map/fm_out_part/pallas_call | solution.py:155
  133.4 2.8 %fm_out.1 = (f32[256,512]{1,0:T(8,128)S(1)}, f32[256,512]{1,0:T(8,128)S(1)}, f32[128,256]{1,0:T(8,128)S(1)}) custom-call(s32[2]{0:T(128)S(1)} %pad_add_fusion.at_ref, bf16[128,512]{1,0:T(8,128)(2,1)S(1)} %collective-permute-done.25.low, bf16[128,512]{1,0:T(8,128)(2,1)S(1)} %collective-permute-done.26.high, bf16[512,4096]{1,0:T(8,128)(2,1)S(1)} %bitcast.40, ...), custom_call_target="tpu_custom_call" | custom-call | tf_op jit(solution)/shard_map/fm_out/pallas_call | solution.py:344
  136.2 1.9 %collective-permute-start.27 = (bf16[128,256]{1,0:T(8,128)(2,1)S(1)}, bf16[128,256]{1,0:T(8,128)(2,1)S(1)}, u32[]{:S(2)}, u32[]{:S(2)}) collective-permute-start(bf16[128,256]{1,0:T(8,128)(2,1)S(1)} %convert_element_type.48), channel_id=1, source_target_pairs={{0,2},{2,0},{4,6},{6,4},{8,10},{10,8},{12,14},{14,12},{1,3},{3,1},... | collective-permute-start | bytes 196616 | tf_op jit(solution)/shard_map/ppermute | solution.py:362
  138.1 1.7 collective-permute-done.27
  139.8 1.8 %collective-permute-start.28 = (bf16[128,256]{1,0:T(8,128)(2,1)S(1)}, bf16[128,256]{1,0:T(8,128)(2,1)S(1)}, u32[]{:S(2)}, u32[]{:S(2)}) collective-permute-start(bf16[128,256]{1,0:T(8,128)(2,1)S(1)} %fusion.10), channel_id=1, source_target_pairs={{0,4},{2,6},{4,0},{6,2},{8,12},{10,14},{12,8},{14,10},{1,5},{3,7},... | collective-permute-start | bytes 196616 | tf_op jit(solution)/shard_map/ppermute | solution.py:362
  141.7 2.9 %collective-permute-done.28 = bf16[128,256]{1,0:T(8,128)(2,1)S(1)} collective-permute-done((bf16[128,256]{1,0:T(8,128)(2,1)S(1)}, bf16[128,256]{1,0:T(8,128)(2,1)S(1)}, u32[]{:S(2)}, u32[]{:S(2)}) %collective-permute-start.28) | collective-permute-done | bytes 65568 | tf_op jit(solution)/shard_map/ppermute | solution.py:362
  144.6 2.1 %collective-permute-start.29 = (bf16[128,256]{1,0:T(8,128)(2,1)S(1)}, bf16[128,256]{1,0:T(8,128)(2,1)S(1)}, u32[]{:S(2)}, u32[]{:S(2)}) collective-permute-start(bf16[128,256]{1,0:T(8,128)(2,1)S(1)} %fusion.11), channel_id=1, source_target_pairs={{0,8},{2,10},{4,12},{6,14},{8,0},{10,2},{12,4},{14,6},{1,9},{3,11}... | collective-permute-start | bytes 196616 | tf_op jit(solution)/shard_map/ppermute | solution.py:362
  146.7 5.4 %collective-permute-done.29 = bf16[128,256]{1,0:T(8,128)(2,1)S(1)} collective-permute-done((bf16[128,256]{1,0:T(8,128)(2,1)S(1)}, bf16[128,256]{1,0:T(8,128)(2,1)S(1)}, u32[]{:S(2)}, u32[]{:S(2)}) %collective-permute-start.29) | collective-permute-done | bytes 65568 | tf_op jit(solution)/shard_map/ppermute | solution.py:362
  153.1 13.7 %collective-permute-start.30 = (bf16[256,1024]{1,0:T(8,128)(2,1)S(1)}, bf16[256,1024]{1,0:T(8,128)(2,1)S(1)}, u32[]{:S(2)}, u32[]{:S(2)}) collective-permute-start(bf16[256,1024]{1,0:T(8,128)(2,1)S(1)} %get-tuple-element.114), channel_id=1, source_target_pairs={{0,1},{1,0},{2,3},{3,2},{4,5},{5,4},{6,7},{7,6},{8,9},{9,8},{10,11... | collective-permute-start | bytes 1572872 | tf_op jit(solution)/shard_map/ppermute | solution.py:372
  167.1 1.2 collective-permute-done.30.came_ref
  168.3 2.1 %finish.1 = bf16[1024,512]{1,0:T(8,128)(2,1)} custom-call(s32[2]{0:T(128)S(1)} %pad_add_fusion.at_ref, bf16[256,1024]{1,0:T(8,128)(2,1)S(1)} %get-tuple-element.113.own_ref, bf16[256,1024]{1,0:T(8,128)(2,1)S(1)} %collective-permute-done.30.came_ref, f32[1024,1]{1,0:T(8,128)S(1)} %reshape_tile.4.gain_ref), custom_call_target="tpu_custom_call" | custom-call | flops 268435456 | bytes 4194304 | tf_op jit(solution)/shard_map/finish/pallas_call | solution.py:246
  (85 shorter events, 15.7 us)
Async XLA Ops:
  0.0 10.9 %copy-start = (bf16[256,256]{1,0:T(8,128)(2,1)S(1)}, bf16[256,256]{1,0:T(8,128)(2,1)}, u32[]{:S(2)}) copy-start(bf16[256,256]{1,0:T(8,128)(2,1)} %param.13) | copy-start | bytes 393220
  0.0 107.6 %collective-permute-start.20 = (bf16[512,4096]{1,0:T(8,128)(2,1)}, bf16[512,4096]{1,0:T(8,128)(2,1)}, u32[]{:S(2)}, u32[]{:S(2)}) collective-permute-start(bf16[512,4096]{1,0:T(8,128)(2,1)} %bitcast.32), channel_id=1, source_target_pairs={{0,1},{1,0},{2,3},{3,2},{4,5},{5,4},{6,7},{7,6},{8,9},{9,8},{10,11... | collective-permute-start | bytes 12582920 | tf_op jit(solution)/shard_map/ppermute | solution.py:231
  12.9 24.1 %all-to-all-start = ((bf16[16,4,32,256]{3,2,1,0:T(8,128)(2,1)}), bf16[16,4,32,256]{3,2,1,0:T(8,128)(2,1)S(1)}, u32[]{:S(2)}, u32[]{:S(2)}) async-start(bf16[16,4,32,256]{3,2,1,0:T(8,128)(2,1)} %fusion.4), calls=%async_computation | async-start | bytes 2097152 | tf_op jit(solution)/shard_map/all_to_all | solution.py:242
  17.9 19.3 %copy-start.3 = (bf16[2048,256]{1,0:T(8,128)(2,1)S(1)}, bf16[2048,256]{1,0:T(8,128)(2,1)}, u32[]{:S(2)}) copy-start(bf16[2048,256]{1,0:T(8,128)(2,1)} %refs_9_.1) | copy-start | bytes 3145732
  17.9 22.4 %copy-start.10 = (f32[2048]{0:T(1024)S(1)}, f32[2048]{0:T(1024)}, u32[]{:S(2)}) copy-start(f32[2048]{0:T(1024)} %param.15) | copy-start | bytes 24580
  19.6 2.0 %collective-permute-start = (bf16[8,256,128]{2,1,0:T(8,128)(2,1)S(1)}, bf16[8,256,128]{2,1,0:T(8,128)(2,1)S(1)}, u32[]{:S(2)}, u32[]{:S(2)}) collective-permute-start(bf16[8,256,128]{2,1,0:T(8,128)(2,1)S(1)} %get-tuple-element.61), channel_id=1, source_target_pairs={{0,1},{1,0},{2,3},{3,2},{4,5},{5,4},{6,7},{7,6},{8,9},{9,8},{10,11... | collective-permute-start | bytes 1572872 | tf_op jit(solution)/shard_map/ppermute | solution.py:267
  22.4 9.8 %copy-start.12 = (bf16[2,256,128]{2,1,0:T(8,128)(2,1)}, bf16[2,256,128]{2,1,0:T(8,128)(2,1)S(1)}, u32[]{:S(2)}) copy-start(bf16[2,256,128]{2,1,0:T(8,128)(2,1)S(1)} %get-tuple-element.62) | copy-start | bytes 393220
  22.4 9.2 %collective-permute-start.6 = (bf16[2,256,128]{2,1,0:T(8,128)(2,1)S(1)}, bf16[2,256,128]{2,1,0:T(8,128)(2,1)S(1)}, u32[]{:S(2)}, u32[]{:S(2)}) collective-permute-start(bf16[2,256,128]{2,1,0:T(8,128)(2,1)S(1)} %get-tuple-element.67), channel_id=1, source_target_pairs={{0,2},{2,4},{4,6},{6,8},{8,10},{10,12},{12,14},{14,0},{1,3},{3,5},... | collective-permute-start | bytes 393224 | tf_op jit(solution)/shard_map/ppermute | solution.py:271
  24.1 8.1 %collective-permute-start.7 = (bf16[2,256,128]{2,1,0:T(8,128)(2,1)S(1)}, bf16[2,256,128]{2,1,0:T(8,128)(2,1)S(1)}, u32[]{:S(2)}, u32[]{:S(2)}) collective-permute-start(bf16[2,256,128]{2,1,0:T(8,128)(2,1)S(1)} %get-tuple-element.68), channel_id=1, source_target_pairs={{0,14},{2,0},{4,2},{6,4},{8,6},{10,8},{12,10},{14,12},{1,15},{3,1}... | collective-permute-start | bytes 393224 | tf_op jit(solution)/shard_map/ppermute | solution.py:271
  28.0 9.2 %collective-permute-start.2 = (bf16[2,256,128]{2,1,0:T(8,128)(2,1)S(1)}, bf16[2,256,128]{2,1,0:T(8,128)(2,1)S(1)}, u32[]{:S(2)}, u32[]{:S(2)}) collective-permute-start(bf16[2,256,128]{2,1,0:T(8,128)(2,1)S(1)} %get-tuple-element.63), channel_id=1, source_target_pairs={{0,4},{2,6},{4,8},{6,10},{8,12},{10,14},{12,0},{14,2},{1,5},{3,7},... | collective-permute-start | bytes 393224 | tf_op jit(solution)/shard_map/ppermute | solution.py:271
  28.0 15.4 %collective-permute-start.3 = (bf16[2,256,128]{2,1,0:T(8,128)(2,1)S(1)}, bf16[2,256,128]{2,1,0:T(8,128)(2,1)S(1)}, u32[]{:S(2)}, u32[]{:S(2)}) collective-permute-start(bf16[2,256,128]{2,1,0:T(8,128)(2,1)S(1)} %get-tuple-element.64), channel_id=1, source_target_pairs={{0,12},{2,14},{4,0},{6,2},{8,4},{10,6},{12,8},{14,10},{1,13},{3,15... | collective-permute-start | bytes 393224 | tf_op jit(solution)/shard_map/ppermute | solution.py:271
  31.6 20.0 %collective-permute-start.4 = (bf16[2,256,128]{2,1,0:T(8,128)(2,1)}, bf16[2,256,128]{2,1,0:T(8,128)(2,1)S(1)}, u32[]{:S(2)}, u32[]{:S(2)}) collective-permute-start(bf16[2,256,128]{2,1,0:T(8,128)(2,1)} %get-tuple-element.65), channel_id=1, source_target_pairs={{0,6},{2,8},{4,10},{6,12},{8,14},{10,0},{12,2},{14,4},{1,7},{3,9},... | collective-permute-start | bytes 393224 | tf_op jit(solution)/shard_map/ppermute | solution.py:271
  32.2 19.4 %collective-permute-start.5 = (bf16[2,256,128]{2,1,0:T(8,128)(2,1)}, bf16[2,256,128]{2,1,0:T(8,128)(2,1)S(1)}, u32[]{:S(2)}, u32[]{:S(2)}) collective-permute-start(bf16[2,256,128]{2,1,0:T(8,128)(2,1)} %get-tuple-element.66), channel_id=1, source_target_pairs={{0,10},{2,12},{4,14},{6,0},{8,2},{10,4},{12,6},{14,8},{1,11},{3,13... | collective-permute-start | bytes 393224 | tf_op jit(solution)/shard_map/ppermute | solution.py:271
  37.2 59.1 %collective-permute-start.17 = (bf16[2048,256]{1,0:T(8,128)(2,1)S(1)}, bf16[2048,256]{1,0:T(8,128)(2,1)}, u32[]{:S(2)}, u32[]{:S(2)}) collective-permute-start(bf16[2048,256]{1,0:T(8,128)(2,1)S(1)} %copy-done.3), channel_id=1, source_target_pairs={{0,1},{1,0},{2,3},{3,2},{4,5},{5,4},{6,7},{7,6},{8,9},{9,8},{10,11... | collective-permute-start | bytes 3145736 | tf_op jit(solution)/shard_map/ppermute | solution.py:229
  43.4 14.7 %collective-permute-start.1 = (bf16[2,256,128]{2,1,0:T(8,128)(2,1)}, bf16[2,256,128]{2,1,0:T(8,128)(2,1)S(1)}, u32[]{:S(2)}, u32[]{:S(2)}) collective-permute-start(bf16[2,256,128]{2,1,0:T(8,128)(2,1)} %copy-done.12), channel_id=1, source_target_pairs={{0,8},{2,10},{4,12},{6,14},{8,0},{10,2},{12,4},{14,6},{1,9},{3,11}... | collective-permute-start | bytes 393224 | tf_op jit(solution)/shard_map/ppermute | solution.py:271
  51.6 6.5 %collective-permute-start.8 = (bf16[32,2048]{1,0:T(8,128)(2,1)S(1)}, bf16[32,2048]{1,0:T(8,128)(2,1)S(1)}, u32[]{:S(2)}, u32[]{:S(2)}) collective-permute-start(bf16[32,2048]{1,0:T(8,128)(2,1)S(1)} %fm_rows.1), channel_id=1, source_target_pairs={{0,0},{1,17},{2,34},{3,51},{4,68},{5,85},{6,102},{7,119},{8,136},{... | collective-permute-start | bytes 393224 | tf_op jit(solution)/shard_map/ppermute | solution.py:295
  58.1 13.4 %copy-start.4 = (bf16[32,2048]{1,0:T(8,128)(2,1)}, bf16[32,2048]{1,0:T(8,128)(2,1)S(1)}, u32[]{:S(2)}) copy-start(bf16[32,2048]{1,0:T(8,128)(2,1)S(1)} %collective-permute-done.8.refs_0_) | copy-start | bytes 393220
  58.1 9.7 %collective-permute-start.12 = (bf16[32,2048]{1,0:T(8,128)(2,1)S(1)}, bf16[32,2048]{1,0:T(8,128)(2,1)S(1)}, u32[]{:S(2)}, u32[]{:S(2)}) collective-permute-start(bf16[32,2048]{1,0:T(8,128)(2,1)S(1)} %collective-permute-done.8.refs_0_), channel_id=1, source_target_pairs={{0,14},{2,0},{4,2},{6,4},{8,6},{10,8},{12,10},{14,12},{1,15},{3,1}... | collective-permute-start | bytes 393224 | tf_op jit(solution)/shard_map/ppermute | solution.py:216
  64.9 5.0 %collective-permute-start.9 = (bf16[32,2048]{1,0:T(8,128)(2,1)S(1)}, bf16[32,2048]{1,0:T(8,128)(2,1)S(1)}, u32[]{:S(2)}, u32[]{:S(2)}) collective-permute-start(bf16[32,2048]{1,0:T(8,128)(2,1)S(1)} %collective-permute-done.8.refs_0_), channel_id=1, source_target_pairs={{0,2},{2,4},{4,6},{6,8},{8,10},{10,12},{12,14},{14,0},{1,3},{3,5},... | collective-permute-start | bytes 393224 | tf_op jit(solution)/shard_map/ppermute | solution.py:216
  67.8 14.8 %copy-start.6 = (bf16[32,2048]{1,0:T(8,128)(2,1)}, bf16[32,2048]{1,0:T(8,128)(2,1)S(1)}, u32[]{:S(2)}) copy-start(bf16[32,2048]{1,0:T(8,128)(2,1)S(1)} %collective-permute-done.12.refs_4_) | copy-start | bytes 393220
  70.0 12.4 %copy-start.8 = (bf16[32,2048]{1,0:T(8,128)(2,1)}, bf16[32,2048]{1,0:T(8,128)(2,1)S(1)}, u32[]{:S(2)}) copy-start(bf16[32,2048]{1,0:T(8,128)(2,1)S(1)} %collective-permute-done.9.refs_1_) | copy-start | bytes 393220
  70.0 25.8 %copy-start.11 = (bf16[32,64]{1,0:T(8,128)(2,1)S(1)}, bf16[32,64]{1,0:T(8,128)(2,1)}, u32[]{:S(2)}) copy-start(bf16[32,64]{1,0:T(8,128)(2,1)} %lcb_ref.1) | copy-start | bytes 12292
  71.5 33.9 %all-to-all-start.1 = ((bf16[16,256,128]{2,1,0:T(8,128)(2,1)}), bf16[16,256,128]{2,1,0:T(8,128)(2,1)S(1)}, u32[]{:S(2)}, u32[]{:S(2)}) async-start(bf16[16,256,128]{2,1,0:T(8,128)(2,1)} %pack.1), calls=%async_computation.1 | async-start | bytes 2097152 | tf_op jit(solution)/shard_map/all_to_all | solution.py:304
  82.3 5.1 %collective-permute-start.10 = (bf16[32,2048]{1,0:T(8,128)(2,1)S(1)}, bf16[32,2048]{1,0:T(8,128)(2,1)S(1)}, u32[]{:S(2)}, u32[]{:S(2)}) collective-permute-start(bf16[32,2048]{1,0:T(8,128)(2,1)S(1)} %collective-permute-done.9.refs_1_), channel_id=1, source_target_pairs={{0,2},{2,4},{4,6},{6,8},{8,10},{10,12},{12,14},{14,0},{1,3},{3,5},... | collective-permute-start | bytes 393224 | tf_op jit(solution)/shard_map/ppermute | solution.py:216
  82.7 4.8 %collective-permute-start.13 = (bf16[32,2048]{1,0:T(8,128)(2,1)S(1)}, bf16[32,2048]{1,0:T(8,128)(2,1)S(1)}, u32[]{:S(2)}, u32[]{:S(2)}) collective-permute-start(bf16[32,2048]{1,0:T(8,128)(2,1)S(1)} %collective-permute-done.12.refs_4_), channel_id=1, source_target_pairs={{0,14},{2,0},{4,2},{6,4},{8,6},{10,8},{12,10},{14,12},{1,15},{3,1}... | collective-permute-start | bytes 393224 | tf_op jit(solution)/shard_map/ppermute | solution.py:216
  87.4 5.3 %collective-permute-start.11 = (bf16[32,2048]{1,0:T(8,128)(2,1)S(1)}, bf16[32,2048]{1,0:T(8,128)(2,1)S(1)}, u32[]{:S(2)}, u32[]{:S(2)}) collective-permute-start(bf16[32,2048]{1,0:T(8,128)(2,1)S(1)} %collective-permute-done.10.refs_2_), channel_id=1, source_target_pairs={{0,2},{2,4},{4,6},{6,8},{8,10},{10,12},{12,14},{14,0},{1,3},{3,5},... | collective-permute-start | bytes 393224 | tf_op jit(solution)/shard_map/ppermute | solution.py:216
  87.4 5.3 %collective-permute-start.14 = (bf16[32,2048]{1,0:T(8,128)(2,1)S(1)}, bf16[32,2048]{1,0:T(8,128)(2,1)S(1)}, u32[]{:S(2)}, u32[]{:S(2)}) collective-permute-start(bf16[32,2048]{1,0:T(8,128)(2,1)S(1)} %collective-permute-done.13.refs_5_), channel_id=1, source_target_pairs={{0,14},{2,0},{4,2},{6,4},{8,6},{10,8},{12,10},{14,12},{1,15},{3,1}... | collective-permute-start | bytes 393224 | tf_op jit(solution)/shard_map/ppermute | solution.py:216
  92.8 4.6 %collective-permute-start.15 = (bf16[16,2048]{1,0:T(8,128)(2,1)S(1)}, bf16[16,2048]{1,0:T(8,128)(2,1)S(1)}, u32[]{:S(2)}, u32[]{:S(2)}) collective-permute-start(bf16[16,2048]{1,0:T(8,128)(2,1)S(1)} %slice.16), channel_id=1, source_target_pairs={{0,2},{2,4},{4,6},{6,8},{8,10},{10,12},{12,14},{14,0},{1,3},{3,5},... | collective-permute-start | bytes 196616 | tf_op jit(solution)/shard_map/ppermute | solution.py:216
  92.8 4.6 %collective-permute-start.16 = (bf16[16,2048]{1,0:T(8,128)(2,1)S(1)}, bf16[16,2048]{1,0:T(8,128)(2,1)S(1)}, u32[]{:S(2)}, u32[]{:S(2)}) collective-permute-start(bf16[16,2048]{1,0:T(8,128)(2,1)S(1)} %slice.17), channel_id=1, source_target_pairs={{0,14},{2,0},{4,2},{6,4},{8,6},{10,8},{12,10},{14,12},{1,15},{3,1}... | collective-permute-start | bytes 196616 | tf_op jit(solution)/shard_map/ppermute | solution.py:216
  97.4 0.9 copy-start.5
  98.3 0.9 copy-start.7
  99.2 0.9 copy-start.9
  102.1 10.0 %collective-permute-start.18 = (bf16[256,512]{1,0:T(8,128)(2,1)S(1)}, bf16[256,512]{1,0:T(8,128)(2,1)S(1)}, u32[]{:S(2)}, u32[]{:S(2)}) collective-permute-start(bf16[256,512]{1,0:T(8,128)(2,1)S(1)} %hidden.1.refs_0_), channel_id=1, source_target_pairs={{0,2},{2,4},{4,6},{6,8},{8,10},{10,12},{12,14},{14,0},{1,3},{3,5},... | collective-permute-start | bytes 786440 | tf_op jit(solution)/shard_map/ppermute | solution.py:216
  102.2 10.0 %collective-permute-start.19 = (bf16[256,512]{1,0:T(8,128)(2,1)S(1)}, bf16[256,512]{1,0:T(8,128)(2,1)S(1)}, u32[]{:S(2)}, u32[]{:S(2)}) collective-permute-start(bf16[256,512]{1,0:T(8,128)(2,1)S(1)} %hidden.1.refs_0_), channel_id=1, source_target_pairs={{0,14},{2,0},{4,2},{6,4},{8,6},{10,8},{12,10},{14,12},{1,15},{3,1}... | collective-permute-start | bytes 786440 | tf_op jit(solution)/shard_map/ppermute | solution.py:216
  107.6 2.2 %copy-start.1 = (bf16[4096,32,16]{0,2,1:T(8,128)(2,1)S(1)}, bf16[4096,32,16]{0,2,1:T(8,128)(2,1)}, u32[]{:S(2)}) copy-start(bf16[4096,32,16]{0,2,1:T(8,128)(2,1)} %param.17) | copy-start | bytes 12582916
  109.8 5.2 %copy-start.2 = (bf16[4096,32,16]{0,2,1:T(8,128)(2,1)S(1)}, bf16[4096,32,16]{0,2,1:T(8,128)(2,1)}, u32[]{:S(2)}) copy-start(bf16[4096,32,16]{0,2,1:T(8,128)(2,1)} %param.17) | copy-start | bytes 12582916
  112.2 6.5 %collective-permute-start.21 = (bf16[256,512]{1,0:T(8,128)(2,1)S(1)}, bf16[256,512]{1,0:T(8,128)(2,1)S(1)}, u32[]{:S(2)}, u32[]{:S(2)}) collective-permute-start(bf16[256,512]{1,0:T(8,128)(2,1)S(1)} %collective-permute-done.18.refs_0_), channel_id=1, source_target_pairs={{0,2},{2,4},{4,6},{6,8},{8,10},{10,12},{12,14},{14,0},{1,3},{3,5},... | collective-permute-start | bytes 786440 | tf_op jit(solution)/shard_map/ppermute | solution.py:216
  112.3 6.4 %collective-permute-start.22 = (bf16[256,512]{1,0:T(8,128)(2,1)S(1)}, bf16[256,512]{1,0:T(8,128)(2,1)S(1)}, u32[]{:S(2)}, u32[]{:S(2)}) collective-permute-start(bf16[256,512]{1,0:T(8,128)(2,1)S(1)} %collective-permute-done.19.refs_1_), channel_id=1, source_target_pairs={{0,14},{2,0},{4,2},{6,4},{8,6},{10,8},{12,10},{14,12},{1,15},{3,1}... | collective-permute-start | bytes 786440 | tf_op jit(solution)/shard_map/ppermute | solution.py:216
  118.7 8.7 %collective-permute-start.23 = (bf16[256,512]{1,0:T(8,128)(2,1)S(1)}, bf16[256,512]{1,0:T(8,128)(2,1)S(1)}, u32[]{:S(2)}, u32[]{:S(2)}) collective-permute-start(bf16[256,512]{1,0:T(8,128)(2,1)S(1)} %collective-permute-done.21.refs_0_), channel_id=1, source_target_pairs={{0,2},{2,4},{4,6},{6,8},{8,10},{10,12},{12,14},{14,0},{1,3},{3,5},... | collective-permute-start | bytes 786440 | tf_op jit(solution)/shard_map/ppermute | solution.py:216
  119.8 8.0 %collective-permute-start.24 = (bf16[256,512]{1,0:T(8,128)(2,1)S(1)}, bf16[256,512]{1,0:T(8,128)(2,1)S(1)}, u32[]{:S(2)}, u32[]{:S(2)}) collective-permute-start(bf16[256,512]{1,0:T(8,128)(2,1)S(1)} %collective-permute-done.22.refs_1_), channel_id=1, source_target_pairs={{0,14},{2,0},{4,2},{6,4},{8,6},{10,8},{12,10},{14,12},{1,15},{3,1}... | collective-permute-start | bytes 786440 | tf_op jit(solution)/shard_map/ppermute | solution.py:216
  127.9 5.4 %collective-permute-start.25 = (bf16[128,512]{1,0:T(8,128)(2,1)S(1)}, bf16[128,512]{1,0:T(8,128)(2,1)S(1)}, u32[]{:S(2)}, u32[]{:S(2)}) collective-permute-start(bf16[128,512]{1,0:T(8,128)(2,1)S(1)} %slice.14), channel_id=1, source_target_pairs={{0,2},{2,4},{4,6},{6,8},{8,10},{10,12},{12,14},{14,0},{1,3},{3,5},... | collective-permute-start | bytes 393224 | tf_op jit(solution)/shard_map/ppermute | solution.py:216
  129.1 4.2 %collective-permute-start.26 = (bf16[128,512]{1,0:T(8,128)(2,1)S(1)}, bf16[128,512]{1,0:T(8,128)(2,1)S(1)}, u32[]{:S(2)}, u32[]{:S(2)}) collective-permute-start(bf16[128,512]{1,0:T(8,128)(2,1)S(1)} %slice.15), channel_id=1, source_target_pairs={{0,14},{2,0},{4,2},{6,4},{8,6},{10,8},{12,10},{14,12},{1,15},{3,1}... | collective-permute-start | bytes 393224 | tf_op jit(solution)/shard_map/ppermute | solution.py:216
  136.2 30.6 %copy-start.13 = (f32[16]{0:T(128)S(1)}, f32[16]{0:T(128)}, u32[]{:S(2)}) copy-start(f32[16]{0:T(128)} %param.19) | copy-start | bytes 196
  136.2 3.6 %collective-permute-start.27 = (bf16[128,256]{1,0:T(8,128)(2,1)S(1)}, bf16[128,256]{1,0:T(8,128)(2,1)S(1)}, u32[]{:S(2)}, u32[]{:S(2)}) collective-permute-start(bf16[128,256]{1,0:T(8,128)(2,1)S(1)} %convert_element_type.48), channel_id=1, source_target_pairs={{0,2},{2,0},{4,6},{6,4},{8,10},{10,8},{12,14},{14,12},{1,3},{3,1},... | collective-permute-start | bytes 196616 | tf_op jit(solution)/shard_map/ppermute | solution.py:362
  139.8 4.8 %collective-permute-start.28 = (bf16[128,256]{1,0:T(8,128)(2,1)S(1)}, bf16[128,256]{1,0:T(8,128)(2,1)S(1)}, u32[]{:S(2)}, u32[]{:S(2)}) collective-permute-start(bf16[128,256]{1,0:T(8,128)(2,1)S(1)} %fusion.10), channel_id=1, source_target_pairs={{0,4},{2,6},{4,0},{6,2},{8,12},{10,14},{12,8},{14,10},{1,5},{3,7},... | collective-permute-start | bytes 196616 | tf_op jit(solution)/shard_map/ppermute | solution.py:362
  144.6 7.6 %collective-permute-start.29 = (bf16[128,256]{1,0:T(8,128)(2,1)S(1)}, bf16[128,256]{1,0:T(8,128)(2,1)S(1)}, u32[]{:S(2)}, u32[]{:S(2)}) collective-permute-start(bf16[128,256]{1,0:T(8,128)(2,1)S(1)} %fusion.11), channel_id=1, source_target_pairs={{0,8},{2,10},{4,12},{6,14},{8,0},{10,2},{12,4},{14,6},{1,9},{3,11}... | collective-permute-start | bytes 196616 | tf_op jit(solution)/shard_map/ppermute | solution.py:362
  153.1 15.2 %collective-permute-start.30 = (bf16[256,1024]{1,0:T(8,128)(2,1)S(1)}, bf16[256,1024]{1,0:T(8,128)(2,1)S(1)}, u32[]{:S(2)}, u32[]{:S(2)}) collective-permute-start(bf16[256,1024]{1,0:T(8,128)(2,1)S(1)} %get-tuple-element.114), channel_id=1, source_target_pairs={{0,1},{1,0},{2,3},{3,2},{4,5},{5,4},{6,7},{7,6},{8,9},{9,8},{10,11... | collective-permute-start | bytes 1572872 | tf_op jit(solution)/shard_map/ppermute | solution.py:372
